TPU v7x, 32 devices: a whole 2x2x4 slice. The times are simulated.
32 devices in a mesh: path: 8 (over y, x, core), shard: 4 (over z).
Axes of the slice: x: 2, y: 2, z: 4, core: 2. Of those that a mesh axis runs over, the one named last changes fastest.
Arguments:
- path_delta: float32 [8, 2, 512, 1024], P('path', None, 'shard'), may hold values from -500 to 500
- assign: int32 [8, 2], replicated, may hold values from 0 to 15
- params: float32 [32, 4, 128, 1024], P(None, 'shard', 'path'), may hold values from -6 to 6
- momentum: float32 [32, 4, 128, 1024], P(None, 'shard', 'path'), may hold values from -3 to 3
Outputs:
- path_params: float32 [8, 2, 512, 1024], P('path', None, 'shard')
- new_params: float32 [32, 4, 128, 1024], P(None, 'shard', 'path')
- new_momentum: float32 [32, 4, 128, 1024], P(None, 'shard', 'path')
All inputs are finite; a program needn't handle non-finite values.
Results may differ from a plain program's by a relative error of at most 0.00007.
Values sent between devices are 32-bit elements; how exact they have to be, the bound alone decides.
No kernel may reach another device: no remote copies, remote signals or barrier semaphores. Data moves between devices by JAX's collectives and lax.ppermute only.
A program may use at most 128 MiB of HBM per device.

v0:
```python
import jax
import jax.numpy as jnp
from jax import lax
from jax.experimental import pallas as pl
from jax.experimental.pallas import tpu as pltpu
from jax.sharding import PartitionSpec as P

LEVEL_MODULES = 16
LEVELS = 2
MOST_UNROLLED = 16

outer_rate = 0.7
beta_coef = 0.9
moment_coef = outer_rate * beta_coef * beta_coef
grad_coef = outer_rate * (1.0 + beta_coef)

VMEM_LIMIT = 16 * 1024 * 1024

vmem = pl.BlockSpec(memory_space=pltpu.VMEM)
smem = pl.BlockSpec(memory_space=pltpu.SMEM)
anywhere = pl.BlockSpec(memory_space=pl.ANY)


def call(kernel, out_shape, in_specs, out_specs, **more):
    return pl.pallas_call(
        kernel,
        out_shape=out_shape,
        in_specs=in_specs,
        out_specs=out_specs,
        compiler_params=pltpu.CompilerParams(vmem_limit_bytes=VMEM_LIMIT),
        **more,
    )


def mirrored(k, size):
    if size < 8:
        return k
    return (k & ~6) | ((k & 2) << 1) | ((k & 4) >> 1)


def target(here, k, size):
    if isinstance(here, int):
        return here ^ (mirrored(k, size) if here & 1 else k)
    return here ^ jnp.where(here & 1 == 1, mirrored(k, size), k)


def origin(here, k, size):
    if isinstance(here, int):
        return here ^ (mirrored(k, size) if (here ^ k) & 1 else k)
    return here ^ jnp.where((here ^ k) & 1 == 1, mirrored(k, size), k)


def order_of(size):
    return [6, 7, 2, 4, 1, 3, 5, 0] if size == 8 else [*range(1, size), 0]


def exchange(arrays):
    size = len(arrays)
    return [
        lax.ppermute(array, "path", [(i, target(i, k, size)) for i in range(size)]) if k else array
        for k, array in zip(order_of(size), arrays)
    ]


def squares_kernel(delta_ref, out_ref):
    total = jnp.zeros(out_ref.shape, jnp.float32)
    for level in range(delta_ref.shape[0]):
        block = delta_ref[level]
        block = block * block
        folded = block.reshape(block.shape[0] // 8, 8, block.shape[1]).sum(axis=0)
        for lane in range(0, block.shape[1], 128):
            total = total + folded[:, lane : lane + 128]
    out_ref[...] = total


def pack_kernel(here_ref, delta_ref, *outs):
    for k, out in zip(order_of(len(outs)), outs):
        place = target(here_ref[0], k, len(outs))
        for level in range(LEVELS):
            out[level] = delta_ref[level, place]


def scale_kernel(entries, shards, *refs):
    tiles, refs = refs[:shards], refs[shards:]
    tile = tiles[0][...]
    for other in tiles[1:]:
        tile = tile + other[...]
    total = jnp.broadcast_to(jnp.sum(tile, keepdims=True), (8, 128))
    rescale = 1.0 / jnp.sqrt(total / entries + 1e-06)
    count = len(refs) // 2
    for block, out in zip(refs[:count], refs[count:]):
        levels, rows, width = block.shape
        for level in range(levels):
            for row in range(0, rows, 8):
                for lane in range(0, width, 128):
                    here = (level, slice(row, row + 8), slice(lane, lane + 128))
                    out[here] = block[here] * rescale


def weights_kernel(here_ref, ids_ref, chosen_ref, outgoing_ref, state_ref):
    size = ids_ref.shape[0]
    order = order_of(size)
    here = here_ref[0]
    for level in range(LEVELS):
        ids = [ids_ref[origin(here, k, size), level] for k in order]
        for local_module in range(LEVEL_MODULES):
            count = jnp.int32(0)
            for i in range(size):
                count = count + jnp.where(ids[i] == local_module, 1, 0)
            share = 1.0 / jnp.maximum(count, 1).astype(jnp.float32)
            for i in range(size):
                state_ref[level * LEVEL_MODULES + local_module, i] = jnp.where(ids[i] == local_module, share, 0.0)
        for j, k in enumerate(order):
            module = ids_ref[target(here, k, size), level] + level * LEVEL_MODULES
            chosen_ref[level, j] = module
            for i in range(size):
                outgoing_ref[level * size + j, i] = grad_coef * state_ref[module, i]


def base_kernel(chosen_ref, params_ref, momentum_ref, out_ref):
    for level in range(out_ref.shape[0]):
        for j in range(out_ref.shape[1]):
            module = chosen_ref[level, j]
            out_ref[level, j] = params_ref[module] - moment_coef * momentum_ref[module]


def outgoing_kernel(size, weight_ref, base_ref, *refs):
    received, outs = refs[:size], refs[size:]
    for level in range(LEVELS):
        for j, out in enumerate(outs):
            total = base_ref[level, j]
            for i in range(size):
                total = total - weight_ref[level * size + j, i] * received[i][level]
            out[level] = total


def state_kernel(size, weight_ref, *refs):
    received = refs[:size]
    params_ref, momentum_ref, new_params_ref, new_momentum_ref = refs[size:]
    count = new_params_ref.shape[0]
    first = pl.program_id(0) * count
    level = first // LEVEL_MODULES
    for place in range(count):
        module = first + place
        grad = weight_ref[module, 0] * received[0][level]
        for i in range(1, size):
            grad = grad + weight_ref[module, i] * received[i][level]
        new_moment = beta_coef * momentum_ref[module] + grad
        new_momentum_ref[place] = new_moment
        new_params_ref[place] = params_ref[module] - outer_rate * (grad + beta_coef * new_moment)


def assemble_kernel(size, here_ref, *refs):
    returned, out_ref, sems = refs[:size], refs[size], refs[size + 1]
    copies = []
    for j, k in enumerate(order_of(size)):
        place = origin(here_ref[0], k, size)
        copies.append(pltpu.make_async_copy(returned[j], out_ref.at[:, place], sems.at[j]))
    for copy in copies:
        copy.start()
    for copy in copies:
        copy.wait()


def local(path_delta, assign, params, momentum):
    own_slab = path_delta[0]
    path_count = assign.shape[0]
    module_count, _, own_rows, width = params.shape
    shards = lax.axis_size("shard")
    entries = float(own_slab.size * shards)
    state_in = params.reshape(module_count, own_rows, width)
    moment_in = momentum.reshape(module_count, own_rows, width)
    split_slab = own_slab.reshape(LEVELS, path_count, own_rows, width)
    here = lax.axis_index("path").astype(jnp.int32).reshape(1)
    rows_shape = jax.ShapeDtypeStruct((LEVELS, own_rows, width), jnp.float32)

    squares = call(squares_kernel, jax.ShapeDtypeStruct((8, 128), jnp.float32), [vmem], vmem)(own_slab)
    tiles = [squares] + [
        lax.ppermute(squares, "shard", [(i, (i + step) % shards) for i in range(shards)])
        for step in range(1, shards)
    ]
    raw = call(
        pack_kernel, [rows_shape] * path_count, [smem, vmem], [vmem] * path_count
    )(here, split_slab)
    packed = call(
        lambda *refs: scale_kernel(entries, shards, *refs),
        [rows_shape] * path_count,
        [vmem] * (shards + path_count),
        [vmem] * path_count,
    )(*tiles, *raw)
    received = exchange(packed)
    chosen, outgoing_weight, state_weight = call(
        weights_kernel,
        [
            jax.ShapeDtypeStruct((LEVELS, path_count), jnp.int32),
            jax.ShapeDtypeStruct((LEVELS * path_count, path_count), jnp.float32),
            jax.ShapeDtypeStruct((module_count, path_count), jnp.float32),
        ],
        [smem, smem],
        [smem, smem, smem],
    )(here, assign)
    base = call(
        base_kernel,
        jax.ShapeDtypeStruct((LEVELS, path_count, own_rows, width), jnp.float32),
        [smem, vmem, vmem],
        vmem,
    )(chosen, state_in, moment_in)
    outgoing = call(
        lambda *refs: outgoing_kernel(path_count, *refs),
        [rows_shape] * path_count,
        [smem, vmem] + [vmem] * path_count,
        [vmem] * path_count,
    )(outgoing_weight, base, *received)
    returned = exchange(outgoing)
    block = LEVEL_MODULES // 4
    state_block = pl.BlockSpec((block, own_rows, width), lambda i: (i, 0, 0))
    new_state, new_moment = call(
        lambda *refs: state_kernel(path_count, *refs),
        [jax.ShapeDtypeStruct(state_in.shape, jnp.float32)] * 2,
        [smem] + [vmem] * (path_count + 2),
        [state_block, state_block],
        grid=(module_count // block,),
    )(state_weight, *received, state_in, moment_in)
    path_params = call(
        lambda *refs: assemble_kernel(path_count, *refs),
        jax.ShapeDtypeStruct(split_slab.shape, jnp.float32),
        [smem] + [anywhere] * path_count,
        anywhere,
        scratch_shapes=[pltpu.SemaphoreType.DMA((path_count,))],
    )(here, *returned)
    return (path_params.reshape(path_delta.shape), new_state[:, None], new_moment[:, None])


def local_wide(path_delta, assign, params, momentum):
    own_slab = path_delta[0]
    path_count = assign.shape[0]
    module_count, _, own_rows, width = params.shape
    entries = float(own_slab.size * lax.axis_size("shard"))
    total_sq = lax.psum(jnp.sum(own_slab * own_slab), "shard")
    scaled = own_slab * (1.0 / jnp.sqrt(total_sq / entries + 1e-06))
    received = lax.all_to_all(
        scaled.reshape(LEVELS, path_count, own_rows, width), "path", split_axis=1, concat_axis=1, tiled=True
    )
    flat_ids = (assign + LEVEL_MODULES * jnp.arange(LEVELS, dtype=jnp.int32)[None, :]).T.reshape(-1)
    member = (jnp.arange(module_count, dtype=jnp.int32)[:, None] == flat_ids[None, :]).astype(jnp.float32)
    mean = member / jnp.maximum(jnp.sum(member, axis=1), 1.0)[:, None]
    grad = jnp.einsum(
        "mp,prd->mrd", mean, received.reshape(-1, own_rows, width), precision=lax.Precision.HIGHEST
    )
    new_moment = beta_coef * momentum[:, 0] + grad
    new_state = params[:, 0] - outer_rate * (grad + beta_coef * new_moment)
    outgoing = jnp.take(new_state, flat_ids, axis=0).reshape(LEVELS, path_count, own_rows, width)
    returned = lax.all_to_all(outgoing, "path", split_axis=1, concat_axis=1, tiled=True)
    return (returned.reshape(path_delta.shape), new_state[:, None], new_moment[:, None])


def solution(mesh):
    in_specs = (
        P("path", None, "shard", None),
        P(),
        P(None, "shard", "path", None),
        P(None, "shard", "path", None),
    )
    out_specs = (
        P("path", None, "shard", None),
        P(None, "shard", "path", None),
        P(None, "shard", "path", None),
    )
    chosen = local if mesh.shape["path"] <= MOST_UNROLLED else local_wide
    return jax.shard_map(chosen, mesh=mesh, in_specs=in_specs, out_specs=out_specs, check_vma=False)
```

profile of v0, /device:TPU:0, one launch (start us, length us, event | category | flops | bytes accessed | tf_op | source)
XLA Modules:
  0.0 44.8 jit_solution(8456732765154638114)
XLA Ops:
  0.6 0.0 copy-start.3
  0.7 1.4 %copy-done.3 = f32[1,2,128,1024]{3,2,1,0:T(8,128)S(1)} copy-done((f32[1,2,128,1024]{3,2,1,0:T(8,128)S(1)}, f32[1,2,128,1024]{3,2,1,0:T(8,128)}, u32[]{:S(2)}) %copy-start.3) | copy-done | bytes 1048600
  2.0 0.1 shard_map.69.refs_0_
  2.1 5.1 %collective-permute-start.2 = (f32[8,128]{1,0:T(8,128)S(1)}, f32[8,128]{1,0:T(8,128)S(1)}, u32[]{:S(2)}, u32[]{:S(2)}) collective-permute-start(f32[8,128]{1,0:T(8,128)S(1)} %shard_map.69.refs_0_), channel_id=1, source_target_pairs={{0,3},{1,0},{2,1},{3,2},{4,7},{5,4},{6,5},{7,6},{8,11},{9,8},{10,9... | collective-permute-start | bytes 12296 | tf_op jit(solution)/shard_map/ppermute | solution.py:179
  7.2 0.0 collective-permute-start.1
  7.2 1.0 %collective-permute-start = (f32[8,128]{1,0:T(8,128)S(1)}, f32[8,128]{1,0:T(8,128)S(1)}, u32[]{:S(2)}, u32[]{:S(2)}) collective-permute-start(f32[8,128]{1,0:T(8,128)S(1)} %shard_map.69.refs_0_), channel_id=1, source_target_pairs={{0,1},{1,2},{2,3},{3,0},{4,5},{5,6},{6,7},{7,4},{8,9},{9,10},{10,1... | collective-permute-start | bytes 12296 | tf_op jit(solution)/shard_map/ppermute | solution.py:179
  8.2 1.2 %copy-done.4 = f32[1,2,128,1024]{3,2,1,0:T(8,128)S(1)} copy-done((f32[1,2,128,1024]{3,2,1,0:T(8,128)S(1)}, f32[1,2,128,1024]{3,2,1,0:T(8,128)}, u32[]{:S(2)}) %copy-start.4) | copy-done | bytes 1048600
  9.4 0.1 shard_map.70
  9.5 0.0 collective-permute-done.2.refs_3_
  9.5 2.2 %collective-permute-done.1.refs_2_ = f32[8,128]{1,0:T(8,128)S(1)} collective-permute-done((f32[8,128]{1,0:T(8,128)S(1)}, f32[8,128]{1,0:T(8,128)S(1)}, u32[]{:S(2)}, u32[]{:S(2)}) %collective-permute-start.1) | collective-permute-done | bytes 4128 | tf_op jit(solution)/shard_map/ppermute | solution.py:179
  11.7 0.9 %collective-permute-done.refs_1_ = f32[8,128]{1,0:T(8,128)S(1)} collective-permute-done((f32[8,128]{1,0:T(8,128)S(1)}, f32[8,128]{1,0:T(8,128)S(1)}, u32[]{:S(2)}, u32[]{:S(2)}) %collective-permute-start) | collective-permute-done | bytes 4128 | tf_op jit(solution)/shard_map/ppermute | solution.py:179
  12.6 0.9 %shard_map.71 = (f32[2,16,1024]{2,1,0:T(8,128)S(1)}, f32[2,16,1024]{2,1,0:T(8,128)S(1)}, f32[2,16,1024]{2,1,0:T(8,128)}, f32[2,16,1024]{2,1,0:T(8,128)}, f32[2,1...) custom-call(f32[8,128]{1,0:T(8,128)S(1)} %shard_map.69.refs_0_, ...), custom_call_target="tpu_custom_call" | custom-call | tf_op jit(solution)/shard_map/pallas_call | solution.py:185
  13.5 2.4 %collective-permute-start.3 = (f32[2,16,1024]{2,1,0:T(8,128)S(1)}, f32[2,16,1024]{2,1,0:T(8,128)S(1)}, u32[]{:S(2)}, u32[]{:S(2)}) collective-permute-start(f32[2,16,1024]{2,1,0:T(8,128)S(1)} %get-tuple-element.42), channel_id=1, source_target_pairs={{0,24},{4,28},{8,16},{12,20},{16,8},{20,12},{24,0},{28,4},{1,25},{... | collective-permute-start | bytes 393224 | tf_op jit(solution)/shard_map/ppermute | solution.py:60
  15.9 0.0 collective-permute-start.4
  15.9 0.5 %collective-permute-start.5 = (f32[2,16,1024]{2,1,0:T(8,128)}, f32[2,16,1024]{2,1,0:T(8,128)S(1)}, u32[]{:S(2)}, u32[]{:S(2)}) collective-permute-start(f32[2,16,1024]{2,1,0:T(8,128)} %get-tuple-element.44), channel_id=1, source_target_pairs={{0,8},{4,20},{8,0},{12,28},{16,24},{20,4},{24,16},{28,12},{1,9},{5... | collective-permute-start | bytes 393224 | tf_op jit(solution)/shard_map/ppermute | solution.py:60
  16.5 0.7 %collective-permute-start.6 = (f32[2,16,1024]{2,1,0:T(8,128)}, f32[2,16,1024]{2,1,0:T(8,128)S(1)}, u32[]{:S(2)}, u32[]{:S(2)}) collective-permute-start(f32[2,16,1024]{2,1,0:T(8,128)} %get-tuple-element.45), channel_id=1, source_target_pairs={{0,16},{4,12},{8,24},{12,4},{16,0},{20,28},{24,8},{28,20},{1,17},{... | collective-permute-start | bytes 393224 | tf_op jit(solution)/shard_map/ppermute | solution.py:60
  17.1 1.8 %collective-permute-start.7 = (f32[2,16,1024]{2,1,0:T(8,128)S(1)}, f32[2,16,1024]{2,1,0:T(8,128)S(1)}, u32[]{:S(2)}, u32[]{:S(2)}) collective-permute-start(f32[2,16,1024]{2,1,0:T(8,128)S(1)} %get-tuple-element.46), channel_id=1, source_target_pairs={{0,4},{4,0},{8,12},{12,8},{16,20},{20,16},{24,28},{28,24},{1,5},{5... | collective-permute-start | bytes 393224 | tf_op jit(solution)/shard_map/ppermute | solution.py:60
  19.0 0.8 %collective-permute-done.3.refs_2_.refs_1_ = f32[2,16,1024]{2,1,0:T(8,128)S(1)} collective-permute-done((f32[2,16,1024]{2,1,0:T(8,128)S(1)}, f32[2,16,1024]{2,1,0:T(8,128)S(1)}, u32[]{:S(2)}, u32[]{:S(2)}) %collective-permute-start.3) | collective-permute-done | bytes 131104 | tf_op jit(solution)/shard_map/ppermute | solution.py:60
  19.8 0.0 collective-permute-start.8
  19.8 2.9 %collective-permute-done.4.refs_3_.refs_2_ = f32[2,16,1024]{2,1,0:T(8,128)S(1)} collective-permute-done((f32[2,16,1024]{2,1,0:T(8,128)S(1)}, f32[2,16,1024]{2,1,0:T(8,128)S(1)}, u32[]{:S(2)}, u32[]{:S(2)}) %collective-permute-start.4) | collective-permute-done | bytes 131104 | tf_op jit(solution)/shard_map/ppermute | solution.py:60
  22.7 1.0 %collective-permute-start.9 = (f32[2,16,1024]{2,1,0:T(8,128)S(1)}, f32[2,16,1024]{2,1,0:T(8,128)S(1)}, u32[]{:S(2)}, u32[]{:S(2)}) collective-permute-start(f32[2,16,1024]{2,1,0:T(8,128)S(1)} %get-tuple-element.48), channel_id=1, source_target_pairs={{0,20},{4,8},{8,28},{12,0},{16,4},{20,24},{24,12},{28,16},{1,21},{... | collective-permute-start | bytes 393224 | tf_op jit(solution)/shard_map/ppermute | solution.py:60
  23.7 0.1 copy.7.ids_ref
  23.8 2.4 %shard_map.67 = (s32[2,8]{1,0:T(2,128)S(1)}, f32[16,8]{1,0:T(8,128)S(1)}, f32[32,8]{1,0:T(8,128)S(1)}) custom-call(s32[1]{0:T(128)} %bitcast.here_ref.refs_0_, s32[8,2]{1,0:T(8,128)S(1)} %copy.7.ids_ref), custom_call_target="tpu_custom_call" | custom-call | tf_op jit(solution)/shard_map/pallas_call | solution.py:192
  26.2 0.0 copy-start.1
  26.2 1.6 %copy-done.1 = f32[32,1,16,1024]{3,2,1,0:T(8,128)S(1)} copy-done((f32[32,1,16,1024]{3,2,1,0:T(8,128)S(1)}, f32[32,1,16,1024]{3,2,1,0:T(8,128)}, u32[]{:S(2)}) %copy-start.1) | copy-done | bytes 2097176
  27.8 0.7 %shard_map.68.refs_1_ = f32[2,8,16,1024]{3,2,1,0:T(8,128)S(1)} custom-call(s32[2,8]{1,0:T(2,128)S(1)} %get-tuple-element.33.chosen_ref, f32[32,16,1024]{2,1,0:T(8,128)S(1)} %bitcast.12, f32[32,16,1024]{2,1,0:T(8,128)S(1)} %bitcast.14), custom_call_target="tpu_custom_call" | custom-call | tf_op jit(solution)/shard_map/pallas_call | solution.py:202
  28.5 0.0 copy-start.2
  28.6 0.0 collective-permute-done.5.refs_4_.refs_3_
  28.6 0.0 collective-permute-done.6.refs_5_.refs_4_
  28.6 0.0 collective-permute-done.7.refs_6_.refs_5_
  28.6 0.0 collective-permute-done.8.refs_7_.refs_6_
  28.6 0.0 collective-permute-done.9.refs_8_.refs_7_
  28.6 1.3 %shard_map.72 = (f32[2,16,1024]{2,1,0:T(8,128)S(1)}, f32[2,16,1024]{2,1,0:T(8,128)S(1)}, f32[2,16,1024]{2,1,0:T(8,128)S(1)}, f32[2,16,1024]{2,1,0:T(8,128)S(1)},...) custom-call(f32[16,8]{1,0:T(8,128)S(1)} %get-tuple-element.32.refs_0, ...), custom_call_target="tpu_custom_call" | custom-call | tf_op jit(solution)/shard_map/pallas_call | solution.py:208
  29.9 1.4 %collective-permute-start.10 = (f32[2,16,1024]{2,1,0:T(8,128)S(1)}, f32[2,16,1024]{2,1,0:T(8,128)S(1)}, u32[]{:S(2)}, u32[]{:S(2)}) collective-permute-start(f32[2,16,1024]{2,1,0:T(8,128)S(1)} %get-tuple-element.50), channel_id=1, source_target_pairs={{0,24},{4,28},{8,16},{12,20},{16,8},{20,12},{24,0},{28,4},{1,25},{... | collective-permute-start | bytes 393224 | tf_op jit(solution)/shard_map/ppermute | solution.py:60
  31.4 0.5 %collective-permute-start.11 = (f32[2,16,1024]{2,1,0:T(8,128)S(1)}, f32[2,16,1024]{2,1,0:T(8,128)S(1)}, u32[]{:S(2)}, u32[]{:S(2)}) collective-permute-start(f32[2,16,1024]{2,1,0:T(8,128)S(1)} %get-tuple-element.51), channel_id=1, source_target_pairs={{0,28},{4,24},{8,20},{12,16},{16,12},{20,8},{24,4},{28,0},{1,29},{... | collective-permute-start | bytes 393224 | tf_op jit(solution)/shard_map/ppermute | solution.py:60
  31.9 1.5 %collective-permute-start.12 = (f32[2,16,1024]{2,1,0:T(8,128)S(1)}, f32[2,16,1024]{2,1,0:T(8,128)S(1)}, u32[]{:S(2)}, u32[]{:S(2)}) collective-permute-start(f32[2,16,1024]{2,1,0:T(8,128)S(1)} %get-tuple-element.52), channel_id=1, source_target_pairs={{0,8},{4,20},{8,0},{12,28},{16,24},{20,4},{24,16},{28,12},{1,9},{5... | collective-permute-start | bytes 393224 | tf_op jit(solution)/shard_map/ppermute | solution.py:60
  33.4 1.4 %collective-permute-start.13 = (f32[2,16,1024]{2,1,0:T(8,128)S(1)}, f32[2,16,1024]{2,1,0:T(8,128)S(1)}, u32[]{:S(2)}, u32[]{:S(2)}) collective-permute-start(f32[2,16,1024]{2,1,0:T(8,128)S(1)} %get-tuple-element.53), channel_id=1, source_target_pairs={{0,16},{4,12},{8,24},{12,4},{16,0},{20,28},{24,8},{28,20},{1,17},{... | collective-permute-start | bytes 393224 | tf_op jit(solution)/shard_map/ppermute | solution.py:60
  34.8 0.1 collective-permute-start.14
  35.0 1.8 %collective-permute-done.10.refs_1_ = f32[2,16,1024]{2,1,0:T(8,128)S(1)} collective-permute-done((f32[2,16,1024]{2,1,0:T(8,128)S(1)}, f32[2,16,1024]{2,1,0:T(8,128)S(1)}, u32[]{:S(2)}, u32[]{:S(2)}) %collective-permute-start.10) | collective-permute-done | bytes 131104 | tf_op jit(solution)/shard_map/ppermute | solution.py:60
  36.7 0.0 collective-permute-start.15
  36.7 1.4 %collective-permute-done.11.refs_2_ = f32[2,16,1024]{2,1,0:T(8,128)S(1)} collective-permute-done((f32[2,16,1024]{2,1,0:T(8,128)S(1)}, f32[2,16,1024]{2,1,0:T(8,128)S(1)}, u32[]{:S(2)}, u32[]{:S(2)}) %collective-permute-start.11) | collective-permute-done | bytes 131104 | tf_op jit(solution)/shard_map/ppermute | solution.py:60
  38.1 0.4 collective-permute-start.16
  38.5 5.0 %shard_map.74 = (f32[32,16,1024]{2,1,0:T(8,128)}, f32[32,16,1024]{2,1,0:T(8,128)}) custom-call(f32[32,8]{1,0:T(8,128)S(1)} %get-tuple-element.58.refs_0_, f32[2,16,1024]{2,1,0:T(8,128)S(1)} %collective-permute-done.3.refs_2_.refs_1_, f32[2,16,1024]{2,1,0:T(8,128)S(1)} %collective-permute-done.4.refs_3_.refs_2_, ...), custom_call_target="tpu_custom_call" | custom-call | tf_op jit(solution)/shard_map/pallas_call | solution.py:217
  43.5 0.0 collective-permute-done.12.refs_3_
  43.5 0.0 collective-permute-done.13.refs_4_
  43.5 0.0 collective-permute-done.14.refs_5_
  43.5 0.2 collective-permute-done.16.refs_7_
  43.8 1.0 %shard_map.73 = f32[2,8,16,1024]{3,2,1,0:T(8,128)} custom-call(s32[1]{0:T(128)} %bitcast.here_ref.refs_0_, f32[2,16,1024]{2,1,0:T(8,128)S(1)} %collective-permute-done.10.refs_1_, f32[2,16,1024]{2,1,0:T(8,128)S(1)} %collective-permute-done.11.refs_2_, f32[2,16,1024]{2,1,0:T(8,128)S(1)} %collective-permute-done.12.refs_3_, ...), custom_call_target="tpu_custom_call" | custom-call | tf_op jit(solution)/shard_map/pallas_call | solution.py:224
  (7 shorter events, 0.0 us)
Async XLA Ops:
  0.6 25.6 %copy-start = (f32[32,1,16,1024]{3,2,1,0:T(8,128)S(1)}, f32[32,1,16,1024]{3,2,1,0:T(8,128)}, u32[]{:S(2)}) copy-start(f32[32,1,16,1024]{3,2,1,0:T(8,128)} %param.6) | copy-start | bytes 6291460
  0.6 1.4 %copy-start.3 = (f32[1,2,128,1024]{3,2,1,0:T(8,128)S(1)}, f32[1,2,128,1024]{3,2,1,0:T(8,128)}, u32[]{:S(2)}) copy-start(f32[1,2,128,1024]{3,2,1,0:T(8,128)} %param.4) | copy-start | bytes 3145732
  2.1 7.4 %collective-permute-start.2 = (f32[8,128]{1,0:T(8,128)S(1)}, f32[8,128]{1,0:T(8,128)S(1)}, u32[]{:S(2)}, u32[]{:S(2)}) collective-permute-start(f32[8,128]{1,0:T(8,128)S(1)} %shard_map.69.refs_0_), channel_id=1, source_target_pairs={{0,3},{1,0},{2,1},{3,2},{4,7},{5,4},{6,5},{7,6},{8,11},{9,8},{10,9... | collective-permute-start | bytes 12296 | tf_op jit(solution)/shard_map/ppermute | solution.py:179
  7.2 4.5 %collective-permute-start.1 = (f32[8,128]{1,0:T(8,128)S(1)}, f32[8,128]{1,0:T(8,128)S(1)}, u32[]{:S(2)}, u32[]{:S(2)}) collective-permute-start(f32[8,128]{1,0:T(8,128)S(1)} %shard_map.69.refs_0_), channel_id=1, source_target_pairs={{0,2},{1,3},{2,0},{3,1},{4,6},{5,7},{6,4},{7,5},{8,10},{9,11},{10,... | collective-permute-start | bytes 12296 | tf_op jit(solution)/shard_map/ppermute | solution.py:179
  7.2 5.4 %collective-permute-start = (f32[8,128]{1,0:T(8,128)S(1)}, f32[8,128]{1,0:T(8,128)S(1)}, u32[]{:S(2)}, u32[]{:S(2)}) collective-permute-start(f32[8,128]{1,0:T(8,128)S(1)} %shard_map.69.refs_0_), channel_id=1, source_target_pairs={{0,1},{1,2},{2,3},{3,0},{4,5},{5,6},{6,7},{7,4},{8,9},{9,10},{10,1... | collective-permute-start | bytes 12296 | tf_op jit(solution)/shard_map/ppermute | solution.py:179
  8.2 1.2 %copy-start.4 = (f32[1,2,128,1024]{3,2,1,0:T(8,128)S(1)}, f32[1,2,128,1024]{3,2,1,0:T(8,128)}, u32[]{:S(2)}) copy-start(f32[1,2,128,1024]{3,2,1,0:T(8,128)} %param.4) | copy-start | bytes 3145732
  9.4 14.3 %copy-start.5 = (s32[8,2]{0,1:T(2,128)S(1)}, s32[8,2]{0,1:T(2,128)}, u32[]{:S(2)}) copy-start(s32[8,2]{0,1:T(2,128)} %param.5) | copy-start | bytes 196
  13.5 6.3 %collective-permute-start.3 = (f32[2,16,1024]{2,1,0:T(8,128)S(1)}, f32[2,16,1024]{2,1,0:T(8,128)S(1)}, u32[]{:S(2)}, u32[]{:S(2)}) collective-permute-start(f32[2,16,1024]{2,1,0:T(8,128)S(1)} %get-tuple-element.42), channel_id=1, source_target_pairs={{0,24},{4,28},{8,16},{12,20},{16,8},{20,12},{24,0},{28,4},{1,25},{... | collective-permute-start | bytes 393224 | tf_op jit(solution)/shard_map/ppermute | solution.py:60
  15.9 6.8 %collective-permute-start.4 = (f32[2,16,1024]{2,1,0:T(8,128)S(1)}, f32[2,16,1024]{2,1,0:T(8,128)S(1)}, u32[]{:S(2)}, u32[]{:S(2)}) collective-permute-start(f32[2,16,1024]{2,1,0:T(8,128)S(1)} %get-tuple-element.43), channel_id=1, source_target_pairs={{0,28},{4,24},{8,20},{12,16},{16,12},{20,8},{24,4},{28,0},{1,29},{... | collective-permute-start | bytes 393224 | tf_op jit(solution)/shard_map/ppermute | solution.py:60
  15.9 12.6 %collective-permute-start.5 = (f32[2,16,1024]{2,1,0:T(8,128)}, f32[2,16,1024]{2,1,0:T(8,128)S(1)}, u32[]{:S(2)}, u32[]{:S(2)}) collective-permute-start(f32[2,16,1024]{2,1,0:T(8,128)} %get-tuple-element.44), channel_id=1, source_target_pairs={{0,8},{4,20},{8,0},{12,28},{16,24},{20,4},{24,16},{28,12},{1,9},{5... | collective-permute-start | bytes 393224 | tf_op jit(solution)/shard_map/ppermute | solution.py:60
  16.5 12.1 %collective-permute-start.6 = (f32[2,16,1024]{2,1,0:T(8,128)}, f32[2,16,1024]{2,1,0:T(8,128)S(1)}, u32[]{:S(2)}, u32[]{:S(2)}) collective-permute-start(f32[2,16,1024]{2,1,0:T(8,128)} %get-tuple-element.45), channel_id=1, source_target_pairs={{0,16},{4,12},{8,24},{12,4},{16,0},{20,28},{24,8},{28,20},{1,17},{... | collective-permute-start | bytes 393224 | tf_op jit(solution)/shard_map/ppermute | solution.py:60
  17.1 11.4 %collective-permute-start.7 = (f32[2,16,1024]{2,1,0:T(8,128)S(1)}, f32[2,16,1024]{2,1,0:T(8,128)S(1)}, u32[]{:S(2)}, u32[]{:S(2)}) collective-permute-start(f32[2,16,1024]{2,1,0:T(8,128)S(1)} %get-tuple-element.46), channel_id=1, source_target_pairs={{0,4},{4,0},{8,12},{12,8},{16,20},{20,16},{24,28},{28,24},{1,5},{5... | collective-permute-start | bytes 393224 | tf_op jit(solution)/shard_map/ppermute | solution.py:60
  19.8 8.8 %collective-permute-start.8 = (f32[2,16,1024]{2,1,0:T(8,128)S(1)}, f32[2,16,1024]{2,1,0:T(8,128)S(1)}, u32[]{:S(2)}, u32[]{:S(2)}) collective-permute-start(f32[2,16,1024]{2,1,0:T(8,128)S(1)} %get-tuple-element.47), channel_id=1, source_target_pairs={{0,12},{4,16},{8,4},{12,24},{16,28},{20,0},{24,20},{28,8},{1,13},{... | collective-permute-start | bytes 393224 | tf_op jit(solution)/shard_map/ppermute | solution.py:60
  22.7 5.9 %collective-permute-start.9 = (f32[2,16,1024]{2,1,0:T(8,128)S(1)}, f32[2,16,1024]{2,1,0:T(8,128)S(1)}, u32[]{:S(2)}, u32[]{:S(2)}) collective-permute-start(f32[2,16,1024]{2,1,0:T(8,128)S(1)} %get-tuple-element.48), channel_id=1, source_target_pairs={{0,20},{4,8},{8,28},{12,0},{16,4},{20,24},{24,12},{28,16},{1,21},{... | collective-permute-start | bytes 393224 | tf_op jit(solution)/shard_map/ppermute | solution.py:60
  26.2 1.6 %copy-start.1 = (f32[32,1,16,1024]{3,2,1,0:T(8,128)S(1)}, f32[32,1,16,1024]{3,2,1,0:T(8,128)}, u32[]{:S(2)}) copy-start(f32[32,1,16,1024]{3,2,1,0:T(8,128)} %param.7) | copy-start | bytes 6291460
  28.5 10.0 %copy-start.2 = (f32[32,1,16,1024]{3,2,1,0:T(8,128)S(1)}, f32[32,1,16,1024]{3,2,1,0:T(8,128)}, u32[]{:S(2)}) copy-start(f32[32,1,16,1024]{3,2,1,0:T(8,128)} %param.7) | copy-start | bytes 6291460
  29.9 6.8 %collective-permute-start.10 = (f32[2,16,1024]{2,1,0:T(8,128)S(1)}, f32[2,16,1024]{2,1,0:T(8,128)S(1)}, u32[]{:S(2)}, u32[]{:S(2)}) collective-permute-start(f32[2,16,1024]{2,1,0:T(8,128)S(1)} %get-tuple-element.50), channel_id=1, source_target_pairs={{0,24},{4,28},{8,16},{12,20},{16,8},{20,12},{24,0},{28,4},{1,25},{... | collective-permute-start | bytes 393224 | tf_op jit(solution)/shard_map/ppermute | solution.py:60
  31.4 6.8 %collective-permute-start.11 = (f32[2,16,1024]{2,1,0:T(8,128)S(1)}, f32[2,16,1024]{2,1,0:T(8,128)S(1)}, u32[]{:S(2)}, u32[]{:S(2)}) collective-permute-start(f32[2,16,1024]{2,1,0:T(8,128)S(1)} %get-tuple-element.51), channel_id=1, source_target_pairs={{0,28},{4,24},{8,20},{12,16},{16,12},{20,8},{24,4},{28,0},{1,29},{... | collective-permute-start | bytes 393224 | tf_op jit(solution)/shard_map/ppermute | solution.py:60
  31.9 11.6 %collective-permute-start.12 = (f32[2,16,1024]{2,1,0:T(8,128)S(1)}, f32[2,16,1024]{2,1,0:T(8,128)S(1)}, u32[]{:S(2)}, u32[]{:S(2)}) collective-permute-start(f32[2,16,1024]{2,1,0:T(8,128)S(1)} %get-tuple-element.52), channel_id=1, source_target_pairs={{0,8},{4,20},{8,0},{12,28},{16,24},{20,4},{24,16},{28,12},{1,9},{5... | collective-permute-start | bytes 393224 | tf_op jit(solution)/shard_map/ppermute | solution.py:60
  33.4 10.1 %collective-permute-start.13 = (f32[2,16,1024]{2,1,0:T(8,128)S(1)}, f32[2,16,1024]{2,1,0:T(8,128)S(1)}, u32[]{:S(2)}, u32[]{:S(2)}) collective-permute-start(f32[2,16,1024]{2,1,0:T(8,128)S(1)} %get-tuple-element.53), channel_id=1, source_target_pairs={{0,16},{4,12},{8,24},{12,4},{16,0},{20,28},{24,8},{28,20},{1,17},{... | collective-permute-start | bytes 393224 | tf_op jit(solution)/shard_map/ppermute | solution.py:60
  34.8 8.7 %collective-permute-start.14 = (f32[2,16,1024]{2,1,0:T(8,128)S(1)}, f32[2,16,1024]{2,1,0:T(8,128)S(1)}, u32[]{:S(2)}, u32[]{:S(2)}) collective-permute-start(f32[2,16,1024]{2,1,0:T(8,128)S(1)} %get-tuple-element.54), channel_id=1, source_target_pairs={{0,4},{4,0},{8,12},{12,8},{16,20},{20,16},{24,28},{28,24},{1,5},{5... | collective-permute-start | bytes 393224 | tf_op jit(solution)/shard_map/ppermute | solution.py:60
  36.7 6.8 %collective-permute-start.15 = (f32[2,16,1024]{2,1,0:T(8,128)S(1)}, f32[2,16,1024]{2,1,0:T(8,128)S(1)}, u32[]{:S(2)}, u32[]{:S(2)}) collective-permute-start(f32[2,16,1024]{2,1,0:T(8,128)S(1)} %get-tuple-element.55), channel_id=1, source_target_pairs={{0,12},{4,16},{8,4},{12,24},{16,28},{20,0},{24,20},{28,8},{1,13},{... | collective-permute-start | bytes 393224 | tf_op jit(solution)/shard_map/ppermute | solution.py:60
  38.1 5.6 %collective-permute-start.16 = (f32[2,16,1024]{2,1,0:T(8,128)S(1)}, f32[2,16,1024]{2,1,0:T(8,128)S(1)}, u32[]{:S(2)}, u32[]{:S(2)}) collective-permute-start(f32[2,16,1024]{2,1,0:T(8,128)S(1)} %get-tuple-element.56), channel_id=1, source_target_pairs={{0,20},{4,8},{8,28},{12,0},{16,4},{20,24},{24,12},{28,16},{1,21},{... | collective-permute-start | bytes 393224 | tf_op jit(solution)/shard_map/ppermute | solution.py:60
where the time goes:
time: 45.1 us; the launch traced here: 44.8 us
  starting transfers between devices  18 us (40%)
  Pallas kernels  11.5 us (25%)
  waiting for transfers between devices  10.3 us (23%)
  local copies, waits for them, and re-layouts  4.27 us (9%)
  between operations  0.77 us (2%)
    ppermute x14, starting transfers between devices, exchange(): lax.ppermute(array, 'path', [(i, target(i, k, size)) for i in range(size)])  11.9 us
    ppermute x14, waiting for transfers between devices, exchange(): lax.ppermute(array, 'path', [(i, target(i, k, size)) for i in range(size)])  7.22 us
    ppermute x3, starting transfers between devices, local(): lax.ppermute(squares, 'shard', [(i, (i + step) % shards) for i in range(s...  6.11 us
    pallas_call x1, Pallas kernels, local(): call(lambda *refs: state_kernel(path_count, *refs), [jax.ShapeDtypeStruct...  4.98 us
    unnamed x13, local copies, waits for them, and re-layouts  4.27 us
    ppermute x3, waiting for transfers between devices, local(): lax.ppermute(squares, 'shard', [(i, (i + step) % shards) for i in range(s...  3.09 us
    pallas_call x1, Pallas kernels, local(): call(weights_kernel, [jax.ShapeDtypeStruct((LEVELS, path_count), jnp.int3...  2.41 us
    pallas_call x1, Pallas kernels, local(): call(lambda *refs: outgoing_kernel(path_count, *refs), [rows_shape] * pat...  1.31 us
  transfers between devices with their start and end apart: 17, of which 7 were waited for; matrix products, arithmetic and copies ran while one was open for 0% of the time, Pallas kernels for 18%

commit v1 on v0

--- a/solution.py
+++ b/solution.py
@@ -51,7 +51,7 @@
 
 
 def order_of(size):
-    return [6, 7, 2, 4, 1, 3, 5, 0] if size == 8 else [*range(1, size), 0]
+    return [6, 7, 2, 4, 3, 5, 1, 0] if size == 8 else [*range(1, size), 0]
 
 
 def exchange(arrays):
@@ -80,7 +80,7 @@
             out[level] = delta_ref[level, place]
 
 
-def scale_kernel(entries, shards, *refs):
+def scale_kernel(entries, shards, here_ref, ids_ref, *refs):
     tiles, refs = refs[:shards], refs[shards:]
     tile = tiles[0][...]
     for other in tiles[1:]:
@@ -88,33 +88,34 @@
     total = jnp.broadcast_to(jnp.sum(tile, keepdims=True), (8, 128))
     rescale = 1.0 / jnp.sqrt(total / entries + 1e-06)
     count = len(refs) // 2
-    for block, out in zip(refs[:count], refs[count:]):
-        levels, rows, width = block.shape
-        for level in range(levels):
+    for level in range(LEVELS):
+        own = ids_ref[here_ref[0], level]
+        sharers = jnp.int32(0)
+        for path in range(ids_ref.shape[0]):
+            sharers = sharers + jnp.where(ids_ref[path, level] == own, 1, 0)
+        factor = rescale / jnp.full((8, 128), sharers, jnp.int32).astype(jnp.float32)
+        for block, out in zip(refs[:count], refs[count:]):
+            _, rows, width = block.shape
             for row in range(0, rows, 8):
                 for lane in range(0, width, 128):
                     here = (level, slice(row, row + 8), slice(lane, lane + 128))
-                    out[here] = block[here] * rescale
-
-
-def weights_kernel(here_ref, ids_ref, chosen_ref, outgoing_ref, state_ref):
+                    out[here] = block[here] * factor
+
+
+def plan_kernel(here_ref, ids_ref, chosen_ref, sender_ref, target_ref, module_ref):
     size = ids_ref.shape[0]
     order = order_of(size)
     here = here_ref[0]
     for level in range(LEVELS):
-        ids = [ids_ref[origin(here, k, size), level] for k in order]
-        for local_module in range(LEVEL_MODULES):
-            count = jnp.int32(0)
-            for i in range(size):
-                count = count + jnp.where(ids[i] == local_module, 1, 0)
-            share = 1.0 / jnp.maximum(count, 1).astype(jnp.float32)
-            for i in range(size):
-                state_ref[level * LEVEL_MODULES + local_module, i] = jnp.where(ids[i] == local_module, share, 0.0)
+        for module in range(LEVEL_MODULES):
+            module_ref[level * LEVEL_MODULES + module] = -1
+        for j in reversed(range(size)):
+            module_ref[ids_ref[origin(here, order[j], size), level] + level * LEVEL_MODULES] = j
         for j, k in enumerate(order):
+            sender_ref[level, j] = module_ref[ids_ref[origin(here, k, size), level] + level * LEVEL_MODULES]
             module = ids_ref[target(here, k, size), level] + level * LEVEL_MODULES
             chosen_ref[level, j] = module
-            for i in range(size):
-                outgoing_ref[level * size + j, i] = grad_coef * state_ref[module, i]
+            target_ref[level, j] = module_ref[module]
 
 
 def base_kernel(chosen_ref, params_ref, momentum_ref, out_ref):
@@ -124,27 +125,31 @@
             out_ref[level, j] = params_ref[module] - moment_coef * momentum_ref[module]
 
 
-def outgoing_kernel(size, weight_ref, base_ref, *refs):
-    received, outs = refs[:size], refs[size:]
+def outgoing_kernel(size, sender_ref, target_ref, base_ref, *refs):
+    received, outs, grad_ref = refs[:size], refs[size:-1], refs[-1]
     for level in range(LEVELS):
+        for i in range(size):
+            grad_ref[level, i] = received[i][level]
+        for i in range(1, size):
+            leader = sender_ref[level, i]
+
+            @pl.when(leader != i)
+            def _():
+                grad_ref[level, leader] += received[i][level]
+
         for j, out in enumerate(outs):
-            total = base_ref[level, j]
-            for i in range(size):
-                total = total - weight_ref[level * size + j, i] * received[i][level]
-            out[level] = total
-
-
-def state_kernel(size, weight_ref, *refs):
-    received = refs[:size]
-    params_ref, momentum_ref, new_params_ref, new_momentum_ref = refs[size:]
+            out[level] = base_ref[level, j] - grad_coef * grad_ref[level, target_ref[level, j]]
+
+
+def state_kernel(module_ref, grad_ref, params_ref, momentum_ref, new_params_ref, new_momentum_ref):
     count = new_params_ref.shape[0]
     first = pl.program_id(0) * count
     level = first // LEVEL_MODULES
     for place in range(count):
         module = first + place
-        grad = weight_ref[module, 0] * received[0][level]
-        for i in range(1, size):
-            grad = grad + weight_ref[module, i] * received[i][level]
+        leader = module_ref[module]
+        taken = jnp.where(leader < 0, 0.0, 1.0)
+        grad = taken * grad_ref[level, jnp.maximum(leader, 0)]
         new_moment = beta_coef * momentum_ref[module] + grad
         new_momentum_ref[place] = new_moment
         new_params_ref[place] = params_ref[module] - outer_rate * (grad + beta_coef * new_moment)
@@ -185,19 +190,16 @@
     packed = call(
         lambda *refs: scale_kernel(entries, shards, *refs),
         [rows_shape] * path_count,
-        [vmem] * (shards + path_count),
+        [smem, smem] + [vmem] * (shards + path_count),
         [vmem] * path_count,
-    )(*tiles, *raw)
+    )(here, assign, *tiles, *raw)
     received = exchange(packed)
-    chosen, outgoing_weight, state_weight = call(
-        weights_kernel,
-        [
-            jax.ShapeDtypeStruct((LEVELS, path_count), jnp.int32),
-            jax.ShapeDtypeStruct((LEVELS * path_count, path_count), jnp.float32),
-            jax.ShapeDtypeStruct((module_count, path_count), jnp.float32),
-        ],
+    by_round = jax.ShapeDtypeStruct((LEVELS, path_count), jnp.int32)
+    chosen, sender, receiver, leaders = call(
+        plan_kernel,
+        [by_round, by_round, by_round, jax.ShapeDtypeStruct((module_count,), jnp.int32)],
         [smem, smem],
-        [smem, smem, smem],
+        [smem] * 4,
     )(here, assign)
     base = call(
         base_kernel,
@@ -205,22 +207,22 @@
         [smem, vmem, vmem],
         vmem,
     )(chosen, state_in, moment_in)
-    outgoing = call(
+    *outgoing, grad = call(
         lambda *refs: outgoing_kernel(path_count, *refs),
-        [rows_shape] * path_count,
-        [smem, vmem] + [vmem] * path_count,
-        [vmem] * path_count,
-    )(outgoing_weight, base, *received)
+        [rows_shape] * path_count + [jax.ShapeDtypeStruct(base.shape, jnp.float32)],
+        [smem, smem, vmem] + [vmem] * path_count,
+        [vmem] * (path_count + 1),
+    )(sender, receiver, base, *received)
     returned = exchange(outgoing)
     block = LEVEL_MODULES // 4
     state_block = pl.BlockSpec((block, own_rows, width), lambda i: (i, 0, 0))
     new_state, new_moment = call(
-        lambda *refs: state_kernel(path_count, *refs),
+        state_kernel,
         [jax.ShapeDtypeStruct(state_in.shape, jnp.float32)] * 2,
-        [smem] + [vmem] * (path_count + 2),
+        [smem, vmem, vmem, vmem],
         [state_block, state_block],
         grid=(module_count // block,),
-    )(state_weight, *received, state_in, moment_in)
+    )(leaders, grad, state_in, moment_in)
     path_params = call(
         lambda *refs: assemble_kernel(path_count, *refs),
         jax.ShapeDtypeStruct(split_slab.shape, jnp.float32),

time: 45.1 us -> 44.7 us (level)
  Pallas kernels: 11.5 us -> 9.16 us
  waiting for transfers between devices: 10.3 us -> 11.4 us
  local copies, waits for them, and re-layouts: 4.27 us -> 4.94 us
    pallas_call x2, Pallas kernels: 7.39 us -> 5.5 us  [the longest x1 4.17 us: local(): call(state_kernel, [jax.ShapeDtypeStruct(state_in.shape, jnp.float32)] *...]
    ppermute x14, waiting for transfers between devices: 7.22 us -> 9.07 us  [exchange(): lax.ppermute(array, 'path', [(i, target(i, k, size)) for i in range(size)])]
    ppermute x3, waiting for transfers between devices: 3.09 us -> 2.34 us  [local(): lax.ppermute(squares, 'shard', [(i, (i + step) % shards) for i in range(s...]
    unnamed x13 -> x11, local copies, waits for them, and re-layouts: 4.27 us -> 4.94 us
  transfers between devices with their start and end apart: 17 -> 17, of which waited for: 7 -> 8; matrix products, arithmetic and copies ran while one was open for 0% -> 2% of each run, Pallas kernels for 18% -> 14%
where the time goes in v1:
time: 44.7 us; the launch traced here: 44.5 us
  starting transfers between devices  18.2 us (41%)
  waiting for transfers between devices  11.4 us (26%)
  Pallas kernels  9.16 us (20%)
  local copies, waits for them, and re-layouts  4.94 us (11%)
  between operations  0.74 us (2%)
    ppermute x14, starting transfers between devices, exchange(): lax.ppermute(array, 'path', [(i, target(i, k, size)) for i in range(size)])  12.1 us
    ppermute x14, waiting for transfers between devices, exchange(): lax.ppermute(array, 'path', [(i, target(i, k, size)) for i in range(size)])  9.07 us
    ppermute x3, starting transfers between devices, local(): lax.ppermute(squares, 'shard', [(i, (i + step) % shards) for i in range(s...  6.11 us
    unnamed x11, local copies, waits for them, and re-layouts  4.94 us
    pallas_call x1, Pallas kernels, local(): call(state_kernel, [jax.ShapeDtypeStruct(state_in.shape, jnp.float32)] *...  4.17 us
    ppermute x3, waiting for transfers between devices, local(): lax.ppermute(squares, 'shard', [(i, (i + step) % shards) for i in range(s...  2.34 us
    pallas_call x1, Pallas kernels, local(): call(plan_kernel, [by_round, by_round, by_round, jax.ShapeDtypeStruct((mo...  1.33 us
    pallas_call x1, Pallas kernels, local(): call(lambda *refs: assemble_kernel(path_count, *refs), jax.ShapeDtypeStru...  1.03 us
  transfers between devices with their start and end apart: 17, of which 8 were waited for; matrix products, arithmetic and copies ran while one was open for 2% of the time, Pallas kernels for 14%

profile of v1, /device:TPU:0, one launch (start us, length us, event | category | flops | bytes accessed | tf_op | source)
XLA Modules:
  0.0 44.5 jit_solution(8024350789772637067)
XLA Ops:
  0.6 0.0 copy-start.3
  0.7 1.4 %copy-done.3 = f32[1,2,128,1024]{3,2,1,0:T(8,128)S(1)} copy-done((f32[1,2,128,1024]{3,2,1,0:T(8,128)S(1)}, f32[1,2,128,1024]{3,2,1,0:T(8,128)}, u32[]{:S(2)}) %copy-start.3) | copy-done | bytes 1048600
  2.0 0.1 shard_map.69.refs_2_
  2.1 5.1 %collective-permute-start.2 = (f32[8,128]{1,0:T(8,128)S(1)}, f32[8,128]{1,0:T(8,128)S(1)}, u32[]{:S(2)}, u32[]{:S(2)}) collective-permute-start(f32[8,128]{1,0:T(8,128)S(1)} %shard_map.69.refs_2_), channel_id=1, source_target_pairs={{0,3},{1,0},{2,1},{3,2},{4,7},{5,4},{6,5},{7,6},{8,11},{9,8},{10,9... | collective-permute-start | bytes 12296 | tf_op jit(solution)/shard_map/ppermute | solution.py:184
  7.2 0.0 collective-permute-start.1
  7.2 1.0 %collective-permute-start = (f32[8,128]{1,0:T(8,128)S(1)}, f32[8,128]{1,0:T(8,128)S(1)}, u32[]{:S(2)}, u32[]{:S(2)}) collective-permute-start(f32[8,128]{1,0:T(8,128)S(1)} %shard_map.69.refs_2_), channel_id=1, source_target_pairs={{0,1},{1,2},{2,3},{3,0},{4,5},{5,6},{6,7},{7,4},{8,9},{9,10},{10,1... | collective-permute-start | bytes 12296 | tf_op jit(solution)/shard_map/ppermute | solution.py:184
  8.2 0.8 %copy.7.ids_ref.refs_1_ = s32[8,2]{1,0:T(8,128)S(1)} copy(s32[8,2]{0,1:T(2,128)} %param.5) | data formatting | bytes 128 | tf_op args[1]
  9.0 1.2 %copy-done.4 = f32[1,2,128,1024]{3,2,1,0:T(8,128)S(1)} copy-done((f32[1,2,128,1024]{3,2,1,0:T(8,128)S(1)}, f32[1,2,128,1024]{3,2,1,0:T(8,128)}, u32[]{:S(2)}) %copy-start.4) | copy-done | bytes 1048600
  10.2 0.1 shard_map.70
  10.3 0.0 collective-permute-done.2.refs_5_
  10.3 1.4 %collective-permute-done.1.refs_4_ = f32[8,128]{1,0:T(8,128)S(1)} collective-permute-done((f32[8,128]{1,0:T(8,128)S(1)}, f32[8,128]{1,0:T(8,128)S(1)}, u32[]{:S(2)}, u32[]{:S(2)}) %collective-permute-start.1) | collective-permute-done | bytes 4128 | tf_op jit(solution)/shard_map/ppermute | solution.py:184
  11.7 0.9 %collective-permute-done.refs_3_ = f32[8,128]{1,0:T(8,128)S(1)} collective-permute-done((f32[8,128]{1,0:T(8,128)S(1)}, f32[8,128]{1,0:T(8,128)S(1)}, u32[]{:S(2)}, u32[]{:S(2)}) %collective-permute-start) | collective-permute-done | bytes 4128 | tf_op jit(solution)/shard_map/ppermute | solution.py:184
  12.6 0.8 %shard_map.71 = (f32[2,16,1024]{2,1,0:T(8,128)S(1)}, f32[2,16,1024]{2,1,0:T(8,128)S(1)}, f32[2,16,1024]{2,1,0:T(8,128)S(1)}, f32[2,16,1024]{2,1,0:T(8,128)S(1)},...) custom-call(s32[1]{0:T(128)} %bitcast.here_ref.refs_0_, ...), custom_call_target="tpu_custom_call" | custom-call | tf_op jit(solution)/shard_map/pallas_call | solution.py:190
  13.4 2.5 %collective-permute-start.3 = (f32[2,16,1024]{2,1,0:T(8,128)S(1)}, f32[2,16,1024]{2,1,0:T(8,128)S(1)}, u32[]{:S(2)}, u32[]{:S(2)}) collective-permute-start(f32[2,16,1024]{2,1,0:T(8,128)S(1)} %get-tuple-element.45), channel_id=1, source_target_pairs={{0,24},{4,28},{8,16},{12,20},{16,8},{20,12},{24,0},{28,4},{1,25},{... | collective-permute-start | bytes 393224 | tf_op jit(solution)/shard_map/ppermute | solution.py:60
  15.9 0.0 collective-permute-start.4
  15.9 0.5 %collective-permute-start.5 = (f32[2,16,1024]{2,1,0:T(8,128)S(1)}, f32[2,16,1024]{2,1,0:T(8,128)S(1)}, u32[]{:S(2)}, u32[]{:S(2)}) collective-permute-start(f32[2,16,1024]{2,1,0:T(8,128)S(1)} %get-tuple-element.47), channel_id=1, source_target_pairs={{0,8},{4,20},{8,0},{12,28},{16,24},{20,4},{24,16},{28,12},{1,9},{5... | collective-permute-start | bytes 393224 | tf_op jit(solution)/shard_map/ppermute | solution.py:60
  16.5 0.7 %collective-permute-start.6 = (f32[2,16,1024]{2,1,0:T(8,128)S(1)}, f32[2,16,1024]{2,1,0:T(8,128)S(1)}, u32[]{:S(2)}, u32[]{:S(2)}) collective-permute-start(f32[2,16,1024]{2,1,0:T(8,128)S(1)} %get-tuple-element.48), channel_id=1, source_target_pairs={{0,16},{4,12},{8,24},{12,4},{16,0},{20,28},{24,8},{28,20},{1,17},{... | collective-permute-start | bytes 393224 | tf_op jit(solution)/shard_map/ppermute | solution.py:60
  17.2 2.0 %collective-permute-start.7 = (f32[2,16,1024]{2,1,0:T(8,128)S(1)}, f32[2,16,1024]{2,1,0:T(8,128)S(1)}, u32[]{:S(2)}, u32[]{:S(2)}) collective-permute-start(f32[2,16,1024]{2,1,0:T(8,128)S(1)} %get-tuple-element.49), channel_id=1, source_target_pairs={{0,12},{4,16},{8,4},{12,24},{16,28},{20,0},{24,20},{28,8},{1,13},{... | collective-permute-start | bytes 393224 | tf_op jit(solution)/shard_map/ppermute | solution.py:60
  19.1 0.7 %collective-permute-done.3.refs_3_ = f32[2,16,1024]{2,1,0:T(8,128)S(1)} collective-permute-done((f32[2,16,1024]{2,1,0:T(8,128)S(1)}, f32[2,16,1024]{2,1,0:T(8,128)S(1)}, u32[]{:S(2)}, u32[]{:S(2)}) %collective-permute-start.3) | collective-permute-done | bytes 131104 | tf_op jit(solution)/shard_map/ppermute | solution.py:60
  19.8 0.0 collective-permute-start.8
  19.8 2.9 %collective-permute-done.4.refs_4_ = f32[2,16,1024]{2,1,0:T(8,128)S(1)} collective-permute-done((f32[2,16,1024]{2,1,0:T(8,128)S(1)}, f32[2,16,1024]{2,1,0:T(8,128)S(1)}, u32[]{:S(2)}, u32[]{:S(2)}) %collective-permute-start.4) | collective-permute-done | bytes 131104 | tf_op jit(solution)/shard_map/ppermute | solution.py:60
  22.7 0.0 collective-permute-start.9
  22.7 1.3 %shard_map.67 = (s32[2,8]{1,0:T(2,128)S(1)}, s32[2,8]{1,0:T(2,128)S(1)}, s32[2,8]{1,0:T(2,128)S(1)}, s32[32]{0:T(128)S(1)}) custom-call(s32[1]{0:T(128)} %bitcast.here_ref.refs_0_, s32[8,2]{1,0:T(8,128)S(1)} %copy.7.ids_ref.refs_1_), custom_call_target="tpu_custom_call" | custom-call | tf_op jit(solution)/shard_map/pallas_call | solution.py:198
  24.1 0.0 copy-start.1
  24.1 1.6 %copy-done.1 = f32[32,1,16,1024]{3,2,1,0:T(8,128)S(1)} copy-done((f32[32,1,16,1024]{3,2,1,0:T(8,128)S(1)}, f32[32,1,16,1024]{3,2,1,0:T(8,128)}, u32[]{:S(2)}) %copy-start.1) | copy-done | bytes 2097176
  25.7 0.7 %shard_map.68.refs_2_ = f32[2,8,16,1024]{3,2,1,0:T(8,128)S(1)} custom-call(s32[2,8]{1,0:T(2,128)S(1)} %get-tuple-element.36.chosen_ref, f32[32,16,1024]{2,1,0:T(8,128)S(1)} %bitcast.12, f32[32,16,1024]{2,1,0:T(8,128)S(1)} %bitcast.14), custom_call_target="tpu_custom_call" | custom-call | tf_op jit(solution)/shard_map/pallas_call | solution.py:204
  26.4 0.0 copy-start.2
  26.4 0.0 collective-permute-done.5.refs_5_
  26.5 0.0 collective-permute-done.6.refs_6_
  26.5 1.2 %collective-permute-done.7.refs_7_ = f32[2,16,1024]{2,1,0:T(8,128)S(1)} collective-permute-done((f32[2,16,1024]{2,1,0:T(8,128)S(1)}, f32[2,16,1024]{2,1,0:T(8,128)S(1)}, u32[]{:S(2)}, u32[]{:S(2)}) %collective-permute-start.7) | collective-permute-done | bytes 131104 | tf_op jit(solution)/shard_map/ppermute | solution.py:60
  27.7 0.0 collective-permute-done.8.refs_8_
  27.7 0.0 collective-permute-done.9.refs_9_
  27.7 0.9 %shard_map.72 = (f32[2,16,1024]{2,1,0:T(8,128)S(1)}, f32[2,16,1024]{2,1,0:T(8,128)S(1)}, f32[2,16,1024]{2,1,0:T(8,128)S(1)}, f32[2,16,1024]{2,1,0:T(8,128)S(1)},...) custom-call(s32[2,8]{1,0:T(2,128)S(1)} %get-tuple-element.34.refs_0_, ...), custom_call_target="tpu_custom_call" | custom-call | tf_op jit(solution)/shard_map/pallas_call | solution.py:210
  28.6 2.5 %collective-permute-start.10 = (f32[2,16,1024]{2,1,0:T(8,128)S(1)}, f32[2,16,1024]{2,1,0:T(8,128)S(1)}, u32[]{:S(2)}, u32[]{:S(2)}) collective-permute-start(f32[2,16,1024]{2,1,0:T(8,128)S(1)} %get-tuple-element.53), channel_id=1, source_target_pairs={{0,24},{4,28},{8,16},{12,20},{16,8},{20,12},{24,0},{28,4},{1,25},{... | collective-permute-start | bytes 393224 | tf_op jit(solution)/shard_map/ppermute | solution.py:60
  31.1 0.0 collective-permute-start.11
  31.1 1.4 %collective-permute-start.12 = (f32[2,16,1024]{2,1,0:T(8,128)S(1)}, f32[2,16,1024]{2,1,0:T(8,128)S(1)}, u32[]{:S(2)}, u32[]{:S(2)}) collective-permute-start(f32[2,16,1024]{2,1,0:T(8,128)S(1)} %get-tuple-element.55), channel_id=1, source_target_pairs={{0,8},{4,20},{8,0},{12,28},{16,24},{20,4},{24,16},{28,12},{1,9},{5... | collective-permute-start | bytes 393224 | tf_op jit(solution)/shard_map/ppermute | solution.py:60
  32.6 1.5 %collective-permute-start.13 = (f32[2,16,1024]{2,1,0:T(8,128)S(1)}, f32[2,16,1024]{2,1,0:T(8,128)S(1)}, u32[]{:S(2)}, u32[]{:S(2)}) collective-permute-start(f32[2,16,1024]{2,1,0:T(8,128)S(1)} %get-tuple-element.56), channel_id=1, source_target_pairs={{0,16},{4,12},{8,24},{12,4},{16,0},{20,28},{24,8},{28,20},{1,17},{... | collective-permute-start | bytes 393224 | tf_op jit(solution)/shard_map/ppermute | solution.py:60
  34.1 0.4 collective-permute-start.14
  34.4 0.8 %collective-permute-done.10.refs_1_ = f32[2,16,1024]{2,1,0:T(8,128)S(1)} collective-permute-done((f32[2,16,1024]{2,1,0:T(8,128)S(1)}, f32[2,16,1024]{2,1,0:T(8,128)S(1)}, u32[]{:S(2)}, u32[]{:S(2)}) %collective-permute-start.10) | collective-permute-done | bytes 131104 | tf_op jit(solution)/shard_map/ppermute | solution.py:60
  35.2 0.6 %collective-permute-start.15 = (f32[2,16,1024]{2,1,0:T(8,128)S(1)}, f32[2,16,1024]{2,1,0:T(8,128)S(1)}, u32[]{:S(2)}, u32[]{:S(2)}) collective-permute-start(f32[2,16,1024]{2,1,0:T(8,128)S(1)} %get-tuple-element.58), channel_id=1, source_target_pairs={{0,20},{4,8},{8,28},{12,0},{16,4},{20,24},{24,12},{28,16},{1,21},{... | collective-permute-start | bytes 393224 | tf_op jit(solution)/shard_map/ppermute | solution.py:60
  35.8 2.2 %collective-permute-done.11.refs_2_ = f32[2,16,1024]{2,1,0:T(8,128)S(1)} collective-permute-done((f32[2,16,1024]{2,1,0:T(8,128)S(1)}, f32[2,16,1024]{2,1,0:T(8,128)S(1)}, u32[]{:S(2)}, u32[]{:S(2)}) %collective-permute-start.11) | collective-permute-done | bytes 131104 | tf_op jit(solution)/shard_map/ppermute | solution.py:60
  38.0 0.1 collective-permute-start.16
  38.1 4.2 %shard_map.74 = (f32[32,16,1024]{2,1,0:T(8,128)}, f32[32,16,1024]{2,1,0:T(8,128)}) custom-call(s32[32]{0:T(128)S(1)} %get-tuple-element.61.module_ref, f32[2,8,16,1024]{3,2,1,0:T(8,128)S(1)} %get-tuple-element.62.grad_ref, f32[32,16,1024]{2,1,0:T(8,128)S(1)} %bitcast.13, f32[32,16,1024]{2,1,0:T(8,128)S(1)} %bitcast.15), custom_call_target="tpu_custom_call" | custom-call | tf_op jit(solution)/shard_map/pallas_call | solution.py:219
  42.2 0.0 collective-permute-done.12.refs_3_
  42.2 0.0 collective-permute-done.13.refs_4_
  42.2 1.2 %collective-permute-done.14.refs_5_ = f32[2,16,1024]{2,1,0:T(8,128)S(1)} collective-permute-done((f32[2,16,1024]{2,1,0:T(8,128)S(1)}, f32[2,16,1024]{2,1,0:T(8,128)S(1)}, u32[]{:S(2)}, u32[]{:S(2)}) %collective-permute-start.14) | collective-permute-done | bytes 131104 | tf_op jit(solution)/shard_map/ppermute | solution.py:60
  43.4 0.0 collective-permute-done.15.refs_6_
  43.4 1.0 %shard_map.73 = f32[2,8,16,1024]{3,2,1,0:T(8,128)} custom-call(s32[1]{0:T(128)} %bitcast.here_ref.refs_0_, f32[2,16,1024]{2,1,0:T(8,128)S(1)} %collective-permute-done.10.refs_1_, f32[2,16,1024]{2,1,0:T(8,128)S(1)} %collective-permute-done.11.refs_2_, f32[2,16,1024]{2,1,0:T(8,128)S(1)} %collective-permute-done.12.refs_3_, ...), custom_call_target="tpu_custom_call" | custom-call | tf_op jit(solution)/shard_map/pallas_call | solution.py:226
  (5 shorter events, 0.0 us)
Async XLA Ops:
  0.6 23.5 %copy-start = (f32[32,1,16,1024]{3,2,1,0:T(8,128)S(1)}, f32[32,1,16,1024]{3,2,1,0:T(8,128)}, u32[]{:S(2)}) copy-start(f32[32,1,16,1024]{3,2,1,0:T(8,128)} %param.6) | copy-start | bytes 6291460
  0.6 1.4 %copy-start.3 = (f32[1,2,128,1024]{3,2,1,0:T(8,128)S(1)}, f32[1,2,128,1024]{3,2,1,0:T(8,128)}, u32[]{:S(2)}) copy-start(f32[1,2,128,1024]{3,2,1,0:T(8,128)} %param.4) | copy-start | bytes 3145732
  2.1 8.2 %collective-permute-start.2 = (f32[8,128]{1,0:T(8,128)S(1)}, f32[8,128]{1,0:T(8,128)S(1)}, u32[]{:S(2)}, u32[]{:S(2)}) collective-permute-start(f32[8,128]{1,0:T(8,128)S(1)} %shard_map.69.refs_2_), channel_id=1, source_target_pairs={{0,3},{1,0},{2,1},{3,2},{4,7},{5,4},{6,5},{7,6},{8,11},{9,8},{10,9... | collective-permute-start | bytes 12296 | tf_op jit(solution)/shard_map/ppermute | solution.py:184
  7.2 4.5 %collective-permute-start.1 = (f32[8,128]{1,0:T(8,128)S(1)}, f32[8,128]{1,0:T(8,128)S(1)}, u32[]{:S(2)}, u32[]{:S(2)}) collective-permute-start(f32[8,128]{1,0:T(8,128)S(1)} %shard_map.69.refs_2_), channel_id=1, source_target_pairs={{0,2},{1,3},{2,0},{3,1},{4,6},{5,7},{6,4},{7,5},{8,10},{9,11},{10,... | collective-permute-start | bytes 12296 | tf_op jit(solution)/shard_map/ppermute | solution.py:184
  7.2 5.4 %collective-permute-start = (f32[8,128]{1,0:T(8,128)S(1)}, f32[8,128]{1,0:T(8,128)S(1)}, u32[]{:S(2)}, u32[]{:S(2)}) collective-permute-start(f32[8,128]{1,0:T(8,128)S(1)} %shard_map.69.refs_2_), channel_id=1, source_target_pairs={{0,1},{1,2},{2,3},{3,0},{4,5},{5,6},{6,7},{7,4},{8,9},{9,10},{10,1... | collective-permute-start | bytes 12296 | tf_op jit(solution)/shard_map/ppermute | solution.py:184
  9.0 1.2 %copy-start.4 = (f32[1,2,128,1024]{3,2,1,0:T(8,128)S(1)}, f32[1,2,128,1024]{3,2,1,0:T(8,128)}, u32[]{:S(2)}) copy-start(f32[1,2,128,1024]{3,2,1,0:T(8,128)} %param.4) | copy-start | bytes 3145732
  13.4 6.4 %collective-permute-start.3 = (f32[2,16,1024]{2,1,0:T(8,128)S(1)}, f32[2,16,1024]{2,1,0:T(8,128)S(1)}, u32[]{:S(2)}, u32[]{:S(2)}) collective-permute-start(f32[2,16,1024]{2,1,0:T(8,128)S(1)} %get-tuple-element.45), channel_id=1, source_target_pairs={{0,24},{4,28},{8,16},{12,20},{16,8},{20,12},{24,0},{28,4},{1,25},{... | collective-permute-start | bytes 393224 | tf_op jit(solution)/shard_map/ppermute | solution.py:60
  15.9 6.8 %collective-permute-start.4 = (f32[2,16,1024]{2,1,0:T(8,128)S(1)}, f32[2,16,1024]{2,1,0:T(8,128)S(1)}, u32[]{:S(2)}, u32[]{:S(2)}) collective-permute-start(f32[2,16,1024]{2,1,0:T(8,128)S(1)} %get-tuple-element.46), channel_id=1, source_target_pairs={{0,28},{4,24},{8,20},{12,16},{16,12},{20,8},{24,4},{28,0},{1,29},{... | collective-permute-start | bytes 393224 | tf_op jit(solution)/shard_map/ppermute | solution.py:60
  15.9 10.5 %collective-permute-start.5 = (f32[2,16,1024]{2,1,0:T(8,128)S(1)}, f32[2,16,1024]{2,1,0:T(8,128)S(1)}, u32[]{:S(2)}, u32[]{:S(2)}) collective-permute-start(f32[2,16,1024]{2,1,0:T(8,128)S(1)} %get-tuple-element.47), channel_id=1, source_target_pairs={{0,8},{4,20},{8,0},{12,28},{16,24},{20,4},{24,16},{28,12},{1,9},{5... | collective-permute-start | bytes 393224 | tf_op jit(solution)/shard_map/ppermute | solution.py:60
  16.5 10.0 %collective-permute-start.6 = (f32[2,16,1024]{2,1,0:T(8,128)S(1)}, f32[2,16,1024]{2,1,0:T(8,128)S(1)}, u32[]{:S(2)}, u32[]{:S(2)}) collective-permute-start(f32[2,16,1024]{2,1,0:T(8,128)S(1)} %get-tuple-element.48), channel_id=1, source_target_pairs={{0,16},{4,12},{8,24},{12,4},{16,0},{20,28},{24,8},{28,20},{1,17},{... | collective-permute-start | bytes 393224 | tf_op jit(solution)/shard_map/ppermute | solution.py:60
  17.2 10.5 %collective-permute-start.7 = (f32[2,16,1024]{2,1,0:T(8,128)S(1)}, f32[2,16,1024]{2,1,0:T(8,128)S(1)}, u32[]{:S(2)}, u32[]{:S(2)}) collective-permute-start(f32[2,16,1024]{2,1,0:T(8,128)S(1)} %get-tuple-element.49), channel_id=1, source_target_pairs={{0,12},{4,16},{8,4},{12,24},{16,28},{20,0},{24,20},{28,8},{1,13},{... | collective-permute-start | bytes 393224 | tf_op jit(solution)/shard_map/ppermute | solution.py:60
  19.8 7.9 %collective-permute-start.8 = (f32[2,16,1024]{2,1,0:T(8,128)S(1)}, f32[2,16,1024]{2,1,0:T(8,128)S(1)}, u32[]{:S(2)}, u32[]{:S(2)}) collective-permute-start(f32[2,16,1024]{2,1,0:T(8,128)S(1)} %get-tuple-element.50), channel_id=1, source_target_pairs={{0,20},{4,8},{8,28},{12,0},{16,4},{20,24},{24,12},{28,16},{1,21},{... | collective-permute-start | bytes 393224 | tf_op jit(solution)/shard_map/ppermute | solution.py:60
  22.7 5.0 %collective-permute-start.9 = (f32[2,16,1024]{2,1,0:T(8,128)S(1)}, f32[2,16,1024]{2,1,0:T(8,128)S(1)}, u32[]{:S(2)}, u32[]{:S(2)}) collective-permute-start(f32[2,16,1024]{2,1,0:T(8,128)S(1)} %get-tuple-element.51), channel_id=1, source_target_pairs={{0,4},{4,0},{8,12},{12,8},{16,20},{20,16},{24,28},{28,24},{1,5},{5... | collective-permute-start | bytes 393224 | tf_op jit(solution)/shard_map/ppermute | solution.py:60
  24.1 1.6 %copy-start.1 = (f32[32,1,16,1024]{3,2,1,0:T(8,128)S(1)}, f32[32,1,16,1024]{3,2,1,0:T(8,128)}, u32[]{:S(2)}) copy-start(f32[32,1,16,1024]{3,2,1,0:T(8,128)} %param.7) | copy-start | bytes 6291460
  26.4 11.6 %copy-start.2 = (f32[32,1,16,1024]{3,2,1,0:T(8,128)S(1)}, f32[32,1,16,1024]{3,2,1,0:T(8,128)}, u32[]{:S(2)}) copy-start(f32[32,1,16,1024]{3,2,1,0:T(8,128)} %param.7) | copy-start | bytes 6291460
  28.6 6.6 %collective-permute-start.10 = (f32[2,16,1024]{2,1,0:T(8,128)S(1)}, f32[2,16,1024]{2,1,0:T(8,128)S(1)}, u32[]{:S(2)}, u32[]{:S(2)}) collective-permute-start(f32[2,16,1024]{2,1,0:T(8,128)S(1)} %get-tuple-element.53), channel_id=1, source_target_pairs={{0,24},{4,28},{8,16},{12,20},{16,8},{20,12},{24,0},{28,4},{1,25},{... | collective-permute-start | bytes 393224 | tf_op jit(solution)/shard_map/ppermute | solution.py:60
  31.1 6.9 %collective-permute-start.11 = (f32[2,16,1024]{2,1,0:T(8,128)S(1)}, f32[2,16,1024]{2,1,0:T(8,128)S(1)}, u32[]{:S(2)}, u32[]{:S(2)}) collective-permute-start(f32[2,16,1024]{2,1,0:T(8,128)S(1)} %get-tuple-element.54), channel_id=1, source_target_pairs={{0,28},{4,24},{8,20},{12,16},{16,12},{20,8},{24,4},{28,0},{1,29},{... | collective-permute-start | bytes 393224 | tf_op jit(solution)/shard_map/ppermute | solution.py:60
  31.1 11.1 %collective-permute-start.12 = (f32[2,16,1024]{2,1,0:T(8,128)S(1)}, f32[2,16,1024]{2,1,0:T(8,128)S(1)}, u32[]{:S(2)}, u32[]{:S(2)}) collective-permute-start(f32[2,16,1024]{2,1,0:T(8,128)S(1)} %get-tuple-element.55), channel_id=1, source_target_pairs={{0,8},{4,20},{8,0},{12,28},{16,24},{20,4},{24,16},{28,12},{1,9},{5... | collective-permute-start | bytes 393224 | tf_op jit(solution)/shard_map/ppermute | solution.py:60
  32.6 9.7 %collective-permute-start.13 = (f32[2,16,1024]{2,1,0:T(8,128)S(1)}, f32[2,16,1024]{2,1,0:T(8,128)S(1)}, u32[]{:S(2)}, u32[]{:S(2)}) collective-permute-start(f32[2,16,1024]{2,1,0:T(8,128)S(1)} %get-tuple-element.56), channel_id=1, source_target_pairs={{0,16},{4,12},{8,24},{12,4},{16,0},{20,28},{24,8},{28,20},{1,17},{... | collective-permute-start | bytes 393224 | tf_op jit(solution)/shard_map/ppermute | solution.py:60
  34.1 9.4 %collective-permute-start.14 = (f32[2,16,1024]{2,1,0:T(8,128)S(1)}, f32[2,16,1024]{2,1,0:T(8,128)S(1)}, u32[]{:S(2)}, u32[]{:S(2)}) collective-permute-start(f32[2,16,1024]{2,1,0:T(8,128)S(1)} %get-tuple-element.57), channel_id=1, source_target_pairs={{0,12},{4,16},{8,4},{12,24},{16,28},{20,0},{24,20},{28,8},{1,13},{... | collective-permute-start | bytes 393224 | tf_op jit(solution)/shard_map/ppermute | solution.py:60
  35.2 8.2 %collective-permute-start.15 = (f32[2,16,1024]{2,1,0:T(8,128)S(1)}, f32[2,16,1024]{2,1,0:T(8,128)S(1)}, u32[]{:S(2)}, u32[]{:S(2)}) collective-permute-start(f32[2,16,1024]{2,1,0:T(8,128)S(1)} %get-tuple-element.58), channel_id=1, source_target_pairs={{0,20},{4,8},{8,28},{12,0},{16,4},{20,24},{24,12},{28,16},{1,21},{... | collective-permute-start | bytes 393224 | tf_op jit(solution)/shard_map/ppermute | solution.py:60
  38.0 5.5 %collective-permute-start.16 = (f32[2,16,1024]{2,1,0:T(8,128)S(1)}, f32[2,16,1024]{2,1,0:T(8,128)S(1)}, u32[]{:S(2)}, u32[]{:S(2)}) collective-permute-start(f32[2,16,1024]{2,1,0:T(8,128)S(1)} %get-tuple-element.59), channel_id=1, source_target_pairs={{0,4},{4,0},{8,12},{12,8},{16,20},{20,16},{24,28},{28,24},{1,5},{5... | collective-permute-start | bytes 393224 | tf_op jit(solution)/shard_map/ppermute | solution.py:60

commit v2 on v1

--- a/solution.py
+++ b/solution.py
@@ -54,39 +54,44 @@
     return [6, 7, 2, 4, 3, 5, 1, 0] if size == 8 else [*range(1, size), 0]
 
 
-def exchange(arrays):
-    size = len(arrays)
-    return [
-        lax.ppermute(array, "path", [(i, target(i, k, size)) for i in range(size)]) if k else array
-        for k, array in zip(order_of(size), arrays)
-    ]
-
-
-def squares_kernel(delta_ref, out_ref):
-    total = jnp.zeros(out_ref.shape, jnp.float32)
-    for level in range(delta_ref.shape[0]):
-        block = delta_ref[level]
-        block = block * block
-        folded = block.reshape(block.shape[0] // 8, 8, block.shape[1]).sum(axis=0)
-        for lane in range(0, block.shape[1], 128):
-            total = total + folded[:, lane : lane + 128]
-    out_ref[...] = total
-
-
-def pack_kernel(here_ref, delta_ref, *outs):
+def early_of(size):
+    return 2 if size == 8 else 0
+
+
+def move(array, k, size):
+    if k == 0:
+        return array
+    return lax.ppermute(array, "path", [(i, target(i, k, size)) for i in range(size)])
+
+
+def pack_kernel(here_ref, delta_ref, square_ref, *outs):
+    total = jnp.zeros(square_ref.shape, jnp.float32)
     for k, out in zip(order_of(len(outs)), outs):
         place = target(here_ref[0], k, len(outs))
         for level in range(LEVELS):
-            out[level] = delta_ref[level, place]
-
-
-def scale_kernel(entries, shards, here_ref, ids_ref, *refs):
+            block = delta_ref[level, place]
+            out[level] = block
+            block = block * block
+            folded = block.reshape(block.shape[0] // 8, 8, block.shape[1]).sum(axis=0)
+            for lane in range(0, block.shape[1], 128):
+                total = total + folded[:, lane : lane + 128]
+    square_ref[...] = total
+
+
+def tiles_of(shape):
+    rows, width = shape[-2:]
+    return [(slice(row, row + 8), slice(lane, lane + 128)) for row in range(0, rows, 8) for lane in range(0, width, 128)]
+
+
+def scale_kernel(entries, shards, here_ref, ids_ref, plan_ref, decayed_ref, *refs):
+    del plan_ref, decayed_ref
     tiles, refs = refs[:shards], refs[shards:]
     tile = tiles[0][...]
     for other in tiles[1:]:
         tile = tile + other[...]
     total = jnp.broadcast_to(jnp.sum(tile, keepdims=True), (8, 128))
     rescale = 1.0 / jnp.sqrt(total / entries + 1e-06)
+    factor_ref, refs = refs[-1], refs[:-1]
     count = len(refs) // 2
     for level in range(LEVELS):
         own = ids_ref[here_ref[0], level]
@@ -94,12 +99,10 @@
         for path in range(ids_ref.shape[0]):
             sharers = sharers + jnp.where(ids_ref[path, level] == own, 1, 0)
         factor = rescale / jnp.full((8, 128), sharers, jnp.int32).astype(jnp.float32)
+        factor_ref[level] = factor
         for block, out in zip(refs[:count], refs[count:]):
-            _, rows, width = block.shape
-            for row in range(0, rows, 8):
-                for lane in range(0, width, 128):
-                    here = (level, slice(row, row + 8), slice(lane, lane + 128))
-                    out[here] = block[here] * factor
+            for tile in tiles_of(block.shape):
+                out[(level, *tile)] = block[(level, *tile)] * factor
 
 
 def plan_kernel(here_ref, ids_ref, chosen_ref, sender_ref, target_ref, module_ref):
@@ -118,30 +121,30 @@
             target_ref[level, j] = module_ref[module]
 
 
-def base_kernel(chosen_ref, params_ref, momentum_ref, out_ref):
-    for level in range(out_ref.shape[0]):
-        for j in range(out_ref.shape[1]):
-            module = chosen_ref[level, j]
-            out_ref[level, j] = params_ref[module] - moment_coef * momentum_ref[module]
-
-
-def outgoing_kernel(size, sender_ref, target_ref, base_ref, *refs):
-    received, outs, grad_ref = refs[:size], refs[size:-1], refs[-1]
+def outgoing_kernel(size, chosen_ref, sender_ref, target_ref, decayed_ref, *refs):
+    early = early_of(size)
+    factors = refs[2 * early : 3 * early]
+    received = refs[: 2 * early] + refs[3 * early : early + size]
+    outs, grad_ref = refs[early + size : -1], refs[-1]
     for level in range(LEVELS):
-        for i in range(size):
+        for i in range(early):
+            factor = factors[i][level]
+            for tile in tiles_of(received[i].shape):
+                grad_ref[(level, i, *tile)] = received[i][(level, *tile)] * factor
+        for i in range(early, size):
             grad_ref[level, i] = received[i][level]
         for i in range(1, size):
             leader = sender_ref[level, i]
 
             @pl.when(leader != i)
             def _():
-                grad_ref[level, leader] += received[i][level]
+                grad_ref[level, leader] += grad_ref[level, i]
 
         for j, out in enumerate(outs):
-            out[level] = base_ref[level, j] - grad_coef * grad_ref[level, target_ref[level, j]]
-
-
-def state_kernel(module_ref, grad_ref, params_ref, momentum_ref, new_params_ref, new_momentum_ref):
+            out[level] = decayed_ref[chosen_ref[level, j]] - grad_coef * grad_ref[level, target_ref[level, j]]
+
+
+def state_kernel(module_ref, grad_ref, decayed_ref, momentum_ref, new_params_ref, new_momentum_ref):
     count = new_params_ref.shape[0]
     first = pl.program_id(0) * count
     level = first // LEVEL_MODULES
@@ -150,15 +153,14 @@
         leader = module_ref[module]
         taken = jnp.where(leader < 0, 0.0, 1.0)
         grad = taken * grad_ref[level, jnp.maximum(leader, 0)]
-        new_moment = beta_coef * momentum_ref[module] + grad
-        new_momentum_ref[place] = new_moment
-        new_params_ref[place] = params_ref[module] - outer_rate * (grad + beta_coef * new_moment)
-
-
-def assemble_kernel(size, here_ref, *refs):
-    returned, out_ref, sems = refs[:size], refs[size], refs[size + 1]
+        new_momentum_ref[place] = beta_coef * momentum_ref[module] + grad
+        new_params_ref[place] = decayed_ref[module] - grad_coef * grad
+
+
+def assemble_kernel(size, rounds, here_ref, *refs):
+    returned, out_ref, sems = refs[: len(rounds)], refs[-2], refs[-1]
     copies = []
-    for j, k in enumerate(order_of(size)):
+    for j, k in enumerate(rounds):
         place = origin(here_ref[0], k, size)
         copies.append(pltpu.make_async_copy(returned[j], out_ref.at[:, place], sems.at[j]))
     for copy in copies:
@@ -179,21 +181,19 @@
     here = lax.axis_index("path").astype(jnp.int32).reshape(1)
     rows_shape = jax.ShapeDtypeStruct((LEVELS, own_rows, width), jnp.float32)
 
-    squares = call(squares_kernel, jax.ShapeDtypeStruct((8, 128), jnp.float32), [vmem], vmem)(own_slab)
+    order = order_of(path_count)
+    early = early_of(path_count)
+    squares, *raw = call(
+        pack_kernel,
+        [jax.ShapeDtypeStruct((8, 128), jnp.float32)] + [rows_shape] * path_count,
+        [smem, vmem],
+        [vmem] * (1 + path_count),
+    )(here, split_slab)
+    received = [move(raw[j], order[j], path_count) for j in range(early)]
     tiles = [squares] + [
         lax.ppermute(squares, "shard", [(i, (i + step) % shards) for i in range(shards)])
         for step in range(1, shards)
     ]
-    raw = call(
-        pack_kernel, [rows_shape] * path_count, [smem, vmem], [vmem] * path_count
-    )(here, split_slab)
-    packed = call(
-        lambda *refs: scale_kernel(entries, shards, *refs),
-        [rows_shape] * path_count,
-        [smem, smem] + [vmem] * (shards + path_count),
-        [vmem] * path_count,
-    )(here, assign, *tiles, *raw)
-    received = exchange(packed)
     by_round = jax.ShapeDtypeStruct((LEVELS, path_count), jnp.int32)
     chosen, sender, receiver, leaders = call(
         plan_kernel,
@@ -201,20 +201,23 @@
         [smem, smem],
         [smem] * 4,
     )(here, assign)
-    base = call(
-        base_kernel,
-        jax.ShapeDtypeStruct((LEVELS, path_count, own_rows, width), jnp.float32),
-        [smem, vmem, vmem],
-        vmem,
-    )(chosen, state_in, moment_in)
+    decayed = state_in - moment_coef * moment_in
+    *scaled, factor = call(
+        lambda *refs: scale_kernel(entries, shards, *refs),
+        [rows_shape] * (path_count - early) + [jax.ShapeDtypeStruct((LEVELS, 8, 128), jnp.float32)],
+        [smem, smem, smem, anywhere] + [vmem] * (shards + path_count - early),
+        [vmem] * (path_count - early + 1),
+    )(here, assign, chosen, decayed, *tiles, *raw[early:])
+    received += [move(scaled[j - early], order[j], path_count) for j in range(early, path_count)]
+    factors = [move(factor, order[j], path_count) for j in range(early)]
     *outgoing, grad = call(
         lambda *refs: outgoing_kernel(path_count, *refs),
-        [rows_shape] * path_count + [jax.ShapeDtypeStruct(base.shape, jnp.float32)],
-        [smem, smem, vmem] + [vmem] * path_count,
+        [rows_shape] * path_count + [jax.ShapeDtypeStruct((LEVELS, path_count, own_rows, width), jnp.float32)],
+        [smem, smem, smem, vmem] + [vmem] * (early + path_count),
         [vmem] * (path_count + 1),
-    )(sender, receiver, base, *received)
-    returned = exchange(outgoing)
-    block = LEVEL_MODULES // 4
+    )(chosen, sender, receiver, decayed, *received[: 2 * early], *factors, *received[2 * early :])
+    returned = [move(outgoing[j], order[j], path_count) for j in range(path_count)]
+    block = LEVEL_MODULES // 2
     state_block = pl.BlockSpec((block, own_rows, width), lambda i: (i, 0, 0))
     new_state, new_moment = call(
         state_kernel,
@@ -222,14 +225,20 @@
         [smem, vmem, vmem, vmem],
         [state_block, state_block],
         grid=(module_count // block,),
-    )(leaders, grad, state_in, moment_in)
-    path_params = call(
-        lambda *refs: assemble_kernel(path_count, *refs),
-        jax.ShapeDtypeStruct(split_slab.shape, jnp.float32),
-        [smem] + [anywhere] * path_count,
-        anywhere,
-        scratch_shapes=[pltpu.SemaphoreType.DMA((path_count,))],
-    )(here, *returned)
+    )(leaders, grad, decayed, moment_in)
+    path_params = None
+    last = path_count // 2
+    for part in ([*range(last), path_count - 1], [*range(last, path_count - 1)]):
+        rounds = [order[j] for j in part]
+        held = [] if path_params is None else [path_params]
+        path_params = call(
+            lambda *refs, rounds=rounds: assemble_kernel(path_count, rounds, *refs),
+            jax.ShapeDtypeStruct(split_slab.shape, jnp.float32),
+            [smem] + [anywhere] * (len(part) + len(held)),
+            anywhere,
+            scratch_shapes=[pltpu.SemaphoreType.DMA((len(part),))],
+            input_output_aliases={1 + len(part): 0} if held else {},
+        )(here, *[returned[j] for j in part], *held)
     return (path_params.reshape(path_delta.shape), new_state[:, None], new_moment[:, None])
 
 

time: 44.7 us -> 45.7 us (1.022)
  starting transfers between devices: 18.2 us -> 23.3 us
  local copies, waits for them, and re-layouts: 4.94 us -> 1.31 us
  other arithmetic: 0 us -> 2.67 us
  waiting for transfers between devices: 11.4 us -> 9.58 us
  Pallas kernels: 9.16 us -> 7.93 us
    ppermute x14 -> x16, starting transfers between devices: 12.1 us -> 17.2 us  [move(): lax.ppermute(array, 'path', [(i, target(i, k, size)) for i in range(size)])]
    unnamed x11 -> x7, local copies, waits for them, and re-layouts: 4.94 us -> 1.31 us
    sub x0 -> x1, other arithmetic: none -> 2.67 us  [local(): decayed = state_in - moment_coef * moment_in]
    ppermute x3, waiting for transfers between devices: 2.34 us -> 0.01 us  [local(): lax.ppermute(squares, 'shard', [(i, (i + step) % shards) for i in range(s...]
    pallas_call x1, Pallas kernels: 4.17 us -> 3.06 us  [local(): call(state_kernel, [jax.ShapeDtypeStruct(state_in.shape, jnp.float32)] *...]
    ppermute x14 -> x16, waiting for transfers between devices: 9.07 us -> 9.57 us  [move(): lax.ppermute(array, 'path', [(i, target(i, k, size)) for i in range(size)])]
    pallas_call x5 -> x4, Pallas kernels: 2.72 us -> 2.63 us  [the longest x2 1.65 us: local(): call(lambda *refs, rounds=rounds: assemble_kernel(path_count, rounds, *re...]
  transfers between devices with their start and end apart: 17 -> 19, of which waited for: 8 -> 8; matrix products, arithmetic and copies ran while one was open for 2% -> 6% of each run, Pallas kernels for 14% -> 13%
where the time goes in v2:
time: 45.7 us; the launch traced here: 45.5 us
  starting transfers between devices  23.3 us (51%)
  waiting for transfers between devices  9.58 us (21%)
  Pallas kernels  7.93 us (17%)
  other arithmetic  2.67 us (6%)
  local copies, waits for them, and re-layouts  1.31 us (3%)
  between operations  0.76 us (2%)
    ppermute x16, starting transfers between devices, move(): lax.ppermute(array, 'path', [(i, target(i, k, size)) for i in range(size)])  17.2 us
    ppermute x16, waiting for transfers between devices, move(): lax.ppermute(array, 'path', [(i, target(i, k, size)) for i in range(size)])  9.57 us
    ppermute x3, starting transfers between devices, local(): lax.ppermute(squares, 'shard', [(i, (i + step) % shards) for i in range(s...  6.11 us
    pallas_call x1, Pallas kernels, local(): call(state_kernel, [jax.ShapeDtypeStruct(state_in.shape, jnp.float32)] *...  3.06 us
    sub x1, other arithmetic, local(): decayed = state_in - moment_coef * moment_in  2.67 us
    pallas_call x2, Pallas kernels, local(): call(lambda *refs, rounds=rounds: assemble_kernel(path_count, rounds, *re...  1.65 us
    pallas_call x1, Pallas kernels, local(): call(plan_kernel, [by_round, by_round, by_round, jax.ShapeDtypeStruct((mo...  1.33 us
    unnamed x7, local copies, waits for them, and re-layouts  1.31 us
  transfers between devices with their start and end apart: 19, of which 8 were waited for; matrix products, arithmetic and copies ran while one was open for 6% of the time, Pallas kernels for 13%

profile of v2, /device:TPU:0, one launch (start us, length us, event | category | flops | bytes accessed | tf_op | source)
XLA Modules:
  0.0 45.5 jit_solution(7370424245252130563)
XLA Ops:
  0.6 1.2 %copy-done.1 = f32[1,2,128,1024]{3,2,1,0:T(8,128)S(1)} copy-done((f32[1,2,128,1024]{3,2,1,0:T(8,128)S(1)}, f32[1,2,128,1024]{3,2,1,0:T(8,128)}, u32[]{:S(2)}) %copy-start.1) | copy-done | bytes 1048600
  1.9 0.2 shard_map.68
  2.0 5.1 %collective-permute-start.4 = (f32[8,128]{1,0:T(8,128)S(1)}, f32[8,128]{1,0:T(8,128)S(1)}, u32[]{:S(2)}, u32[]{:S(2)}) collective-permute-start(f32[8,128]{1,0:T(8,128)S(1)} %get-tuple-element.39.refs_4_), channel_id=1, source_target_pairs={{0,3},{1,0},{2,1},{3,2},{4,7},{5,4},{6,5},{7,6},{8,11},{9,8},{10,9... | collective-permute-start | bytes 12296 | tf_op jit(solution)/shard_map/ppermute | solution.py:194
  7.1 0.0 collective-permute-start.3
  7.1 1.0 %collective-permute-start.2 = (f32[8,128]{1,0:T(8,128)S(1)}, f32[8,128]{1,0:T(8,128)S(1)}, u32[]{:S(2)}, u32[]{:S(2)}) collective-permute-start(f32[8,128]{1,0:T(8,128)S(1)} %get-tuple-element.39.refs_4_), channel_id=1, source_target_pairs={{0,1},{1,2},{2,3},{3,0},{4,5},{5,6},{6,7},{7,4},{8,9},{9,10},{10,1... | collective-permute-start | bytes 12296 | tf_op jit(solution)/shard_map/ppermute | solution.py:194
  8.1 2.4 %collective-permute-start = (f32[2,16,1024]{2,1,0:T(8,128)S(1)}, f32[2,16,1024]{2,1,0:T(8,128)S(1)}, u32[]{:S(2)}, u32[]{:S(2)}) collective-permute-start(f32[2,16,1024]{2,1,0:T(8,128)S(1)} %get-tuple-element.37), channel_id=1, source_target_pairs={{0,24},{4,28},{8,16},{12,20},{16,8},{20,12},{24,0},{28,4},{1,25},{... | collective-permute-start | bytes 393224 | tf_op jit(solution)/shard_map/ppermute | solution.py:64
  10.6 0.0 collective-permute-start.1
  10.6 2.7 %bitcast_subtract_fusion.refs_3_.decayed_ref = f32[32,16,1024]{2,1,0:T(8,128)S(1)} fusion(f32[32,1,16,1024]{3,2,1,0:T(8,128)} %param.6, f32[32,1,16,1024]{3,2,1,0:T(8,128)} %param.7), kind=kLoop, calls=%fused_computation | loop fusion | flops 1048576 | bytes 6291456 | tf_op jit(solution)/shard_map/sub | solution.py:204
  13.3 0.1 copy.8.ids_ref.refs_1_
  13.4 1.3 %shard_map.67 = (s32[2,8]{1,0:T(2,128)S(1)}, s32[2,8]{1,0:T(2,128)S(1)}, s32[2,8]{1,0:T(2,128)S(1)}, s32[32]{0:T(128)S(1)}) custom-call(s32[1]{0:T(128)} %bitcast.here_ref.refs_0_, s32[8,2]{1,0:T(8,128)S(1)} %copy.8.ids_ref.refs_1_), custom_call_target="tpu_custom_call" | custom-call | tf_op jit(solution)/shard_map/pallas_call | solution.py:198
  14.7 0.0 collective-permute-done.4.refs_7_
  14.7 0.0 collective-permute-done.3.refs_6_
  14.7 0.0 collective-permute-done.2.refs_5_
  14.7 0.8 %shard_map.69 = (f32[2,16,1024]{2,1,0:T(8,128)S(1)}, f32[2,16,1024]{2,1,0:T(8,128)S(1)}, f32[2,16,1024]{2,1,0:T(8,128)S(1)}, f32[2,16,1024]{2,1,0:T(8,128)S(1)},...) custom-call(s32[1]{0:T(128)} %bitcast.here_ref.refs_0_, ...), custom_call_target="tpu_custom_call" | custom-call | tf_op jit(solution)/shard_map/pallas_call | solution.py:205
  15.6 0.0 copy-start
  15.6 2.7 %collective-permute-start.8 = (f32[2,8,128]{2,1,0:T(8,128)S(1)}, f32[2,8,128]{2,1,0:T(8,128)S(1)}, u32[]{:S(2)}, u32[]{:S(2)}) collective-permute-start(f32[2,8,128]{2,1,0:T(8,128)S(1)} %get-tuple-element.48), channel_id=1, source_target_pairs={{0,28},{4,24},{8,20},{12,16},{16,12},{20,8},{24,4},{28,0},{1,29},{... | collective-permute-start | bytes 24584 | tf_op jit(solution)/shard_map/ppermute | solution.py:64
  18.3 0.5 %collective-permute-start.7 = (f32[2,8,128]{2,1,0:T(8,128)S(1)}, f32[2,8,128]{2,1,0:T(8,128)S(1)}, u32[]{:S(2)}, u32[]{:S(2)}) collective-permute-start(f32[2,8,128]{2,1,0:T(8,128)S(1)} %get-tuple-element.48), channel_id=1, source_target_pairs={{0,24},{4,28},{8,16},{12,20},{16,8},{20,12},{24,0},{28,4},{1,25},{... | collective-permute-start | bytes 24584 | tf_op jit(solution)/shard_map/ppermute | solution.py:64
  18.7 1.5 %collective-permute-start.5 = (f32[2,16,1024]{2,1,0:T(8,128)S(1)}, f32[2,16,1024]{2,1,0:T(8,128)S(1)}, u32[]{:S(2)}, u32[]{:S(2)}) collective-permute-start(f32[2,16,1024]{2,1,0:T(8,128)S(1)} %get-tuple-element.46), channel_id=1, source_target_pairs={{0,8},{4,20},{8,0},{12,28},{16,24},{20,4},{24,16},{28,12},{1,9},{5... | collective-permute-start | bytes 393224 | tf_op jit(solution)/shard_map/ppermute | solution.py:64
  20.2 0.0 collective-permute-done.8.refs_9_
  20.2 1.5 %collective-permute-start.6 = (f32[2,16,1024]{2,1,0:T(8,128)S(1)}, f32[2,16,1024]{2,1,0:T(8,128)S(1)}, u32[]{:S(2)}, u32[]{:S(2)}) collective-permute-start(f32[2,16,1024]{2,1,0:T(8,128)S(1)} %get-tuple-element.47), channel_id=1, source_target_pairs={{0,16},{4,12},{8,24},{12,4},{16,0},{20,28},{24,8},{28,20},{1,17},{... | collective-permute-start | bytes 393224 | tf_op jit(solution)/shard_map/ppermute | solution.py:64
  21.8 1.1 %collective-permute-done.7.refs_8_ = f32[2,8,128]{2,1,0:T(8,128)S(1)} collective-permute-done((f32[2,8,128]{2,1,0:T(8,128)S(1)}, f32[2,8,128]{2,1,0:T(8,128)S(1)}, u32[]{:S(2)}, u32[]{:S(2)}) %collective-permute-start.7) | collective-permute-done | bytes 8224 | tf_op jit(solution)/shard_map/ppermute | solution.py:64
  22.8 0.0 collective-permute-start.9
  22.8 0.0 collective-permute-done.refs_4_
  22.8 1.7 %collective-permute-start.10 = (f32[2,16,1024]{2,1,0:T(8,128)S(1)}, f32[2,16,1024]{2,1,0:T(8,128)S(1)}, u32[]{:S(2)}, u32[]{:S(2)}) collective-permute-start(f32[2,16,1024]{2,1,0:T(8,128)S(1)} %get-tuple-element.50), channel_id=1, source_target_pairs={{0,20},{4,8},{8,28},{12,0},{16,4},{20,24},{24,12},{28,16},{1,21},{... | collective-permute-start | bytes 393224 | tf_op jit(solution)/shard_map/ppermute | solution.py:64
  24.6 0.0 collective-permute-done.1.refs_5_
  24.6 0.0 collective-permute-start.11
  24.6 0.1 collective-permute-done.5.refs_6_
  24.7 0.5 %collective-permute-done.6.refs_7_ = f32[2,16,1024]{2,1,0:T(8,128)S(1)} collective-permute-done((f32[2,16,1024]{2,1,0:T(8,128)S(1)}, f32[2,16,1024]{2,1,0:T(8,128)S(1)}, u32[]{:S(2)}, u32[]{:S(2)}) %collective-permute-start.6) | collective-permute-done | bytes 131104 | tf_op jit(solution)/shard_map/ppermute | solution.py:64
  25.2 2.6 %collective-permute-done.9.refs_10_ = f32[2,16,1024]{2,1,0:T(8,128)S(1)} collective-permute-done((f32[2,16,1024]{2,1,0:T(8,128)S(1)}, f32[2,16,1024]{2,1,0:T(8,128)S(1)}, u32[]{:S(2)}, u32[]{:S(2)}) %collective-permute-start.9) | collective-permute-done | bytes 131104 | tf_op jit(solution)/shard_map/ppermute | solution.py:64
  27.8 0.1 collective-permute-done.10.refs_11_
  27.9 0.0 collective-permute-done.11.refs_12_
  27.9 0.9 %shard_map.70 = (f32[2,16,1024]{2,1,0:T(8,128)S(1)}, f32[2,16,1024]{2,1,0:T(8,128)S(1)}, f32[2,16,1024]{2,1,0:T(8,128)S(1)}, f32[2,16,1024]{2,1,0:T(8,128)S(1)},...) custom-call(s32[2,8]{1,0:T(2,128)S(1)} %get-tuple-element.34.refs_2_, ...), custom_call_target="tpu_custom_call" | custom-call | tf_op jit(solution)/shard_map/pallas_call | solution.py:213
  28.8 2.5 %collective-permute-start.15 = (f32[2,16,1024]{2,1,0:T(8,128)S(1)}, f32[2,16,1024]{2,1,0:T(8,128)S(1)}, u32[]{:S(2)}, u32[]{:S(2)}) collective-permute-start(f32[2,16,1024]{2,1,0:T(8,128)S(1)} %get-tuple-element.56), channel_id=1, source_target_pairs={{0,24},{4,28},{8,16},{12,20},{16,8},{20,12},{24,0},{28,4},{1,25},{... | collective-permute-start | bytes 393224 | tf_op jit(solution)/shard_map/ppermute | solution.py:64
  31.4 0.3 collective-permute-start.16
  31.7 1.4 %collective-permute-start.12 = (f32[2,16,1024]{2,1,0:T(8,128)S(1)}, f32[2,16,1024]{2,1,0:T(8,128)S(1)}, u32[]{:S(2)}, u32[]{:S(2)}) collective-permute-start(f32[2,16,1024]{2,1,0:T(8,128)S(1)} %get-tuple-element.53), channel_id=1, source_target_pairs={{0,12},{4,16},{8,4},{12,24},{16,28},{20,0},{24,20},{28,8},{1,13},{... | collective-permute-start | bytes 393224 | tf_op jit(solution)/shard_map/ppermute | solution.py:64
  33.0 0.5 %collective-permute-start.17 = (f32[2,16,1024]{2,1,0:T(8,128)S(1)}, f32[2,16,1024]{2,1,0:T(8,128)S(1)}, u32[]{:S(2)}, u32[]{:S(2)}) collective-permute-start(f32[2,16,1024]{2,1,0:T(8,128)S(1)} %get-tuple-element.58), channel_id=1, source_target_pairs={{0,8},{4,20},{8,0},{12,28},{16,24},{20,4},{24,16},{28,12},{1,9},{5... | collective-permute-start | bytes 393224 | tf_op jit(solution)/shard_map/ppermute | solution.py:64
  33.6 1.5 %collective-permute-start.18 = (f32[2,16,1024]{2,1,0:T(8,128)S(1)}, f32[2,16,1024]{2,1,0:T(8,128)S(1)}, u32[]{:S(2)}, u32[]{:S(2)}) collective-permute-start(f32[2,16,1024]{2,1,0:T(8,128)S(1)} %get-tuple-element.59), channel_id=1, source_target_pairs={{0,16},{4,12},{8,24},{12,4},{16,0},{20,28},{24,8},{28,20},{1,17},{... | collective-permute-start | bytes 393224 | tf_op jit(solution)/shard_map/ppermute | solution.py:64
  35.1 1.1 %collective-permute-done.15.refs_1_ = f32[2,16,1024]{2,1,0:T(8,128)S(1)} collective-permute-done((f32[2,16,1024]{2,1,0:T(8,128)S(1)}, f32[2,16,1024]{2,1,0:T(8,128)S(1)}, u32[]{:S(2)}, u32[]{:S(2)}) %collective-permute-start.15) | collective-permute-done | bytes 131104 | tf_op jit(solution)/shard_map/ppermute | solution.py:64
  36.2 0.0 collective-permute-start.13
  36.2 2.0 %collective-permute-done.16.refs_2_ = f32[2,16,1024]{2,1,0:T(8,128)S(1)} collective-permute-done((f32[2,16,1024]{2,1,0:T(8,128)S(1)}, f32[2,16,1024]{2,1,0:T(8,128)S(1)}, u32[]{:S(2)}, u32[]{:S(2)}) %collective-permute-start.16) | collective-permute-done | bytes 131104 | tf_op jit(solution)/shard_map/ppermute | solution.py:64
  38.2 0.5 %collective-permute-start.14 = (f32[2,16,1024]{2,1,0:T(8,128)S(1)}, f32[2,16,1024]{2,1,0:T(8,128)S(1)}, u32[]{:S(2)}, u32[]{:S(2)}) collective-permute-start(f32[2,16,1024]{2,1,0:T(8,128)S(1)} %get-tuple-element.55), channel_id=1, source_target_pairs={{0,4},{4,0},{8,12},{12,8},{16,20},{20,16},{24,28},{28,24},{1,5},{5... | collective-permute-start | bytes 393224 | tf_op jit(solution)/shard_map/ppermute | solution.py:64
  38.8 3.1 %shard_map.73 = (f32[32,16,1024]{2,1,0:T(8,128)}, f32[32,16,1024]{2,1,0:T(8,128)}) custom-call(s32[32]{0:T(128)S(1)} %get-tuple-element.61.module_ref, f32[2,8,16,1024]{3,2,1,0:T(8,128)S(1)} %get-tuple-element.62.grad_ref, f32[32,16,1024]{2,1,0:T(8,128)S(1)} %bitcast_subtract_fusion.refs_3_.decayed_ref, f32[32,16,1024]{2,1,0:T(8,128)S(1)} %bitcast.13), custom_call_target="tpu_custom_call" | custom-call | tf_op jit(solution)/shard_map/pallas_call | solution.py:222
  41.8 2.0 %collective-permute-done.17.refs_3_ = f32[2,16,1024]{2,1,0:T(8,128)S(1)} collective-permute-done((f32[2,16,1024]{2,1,0:T(8,128)S(1)}, f32[2,16,1024]{2,1,0:T(8,128)S(1)}, u32[]{:S(2)}, u32[]{:S(2)}) %collective-permute-start.17) | collective-permute-done | bytes 131104 | tf_op jit(solution)/shard_map/ppermute | solution.py:64
  43.8 0.0 collective-permute-done.18.refs_4_
  43.9 0.9 %shard_map.71.refs_4_ = f32[2,8,16,1024]{3,2,1,0:T(8,128)} custom-call(s32[1]{0:T(128)} %bitcast.here_ref.refs_0_, f32[2,16,1024]{2,1,0:T(8,128)S(1)} %collective-permute-done.15.refs_1_, f32[2,16,1024]{2,1,0:T(8,128)S(1)} %collective-permute-done.16.refs_2_, f32[2,16,1024]{2,1,0:T(8,128)S(1)} %collective-permute-done.17.refs_3_, ...), custom_call_target="tpu_custom_call" | custom-call | tf_op jit(solution)/shard_map/pallas_call | solution.py:234
  44.7 0.0 collective-permute-done.12.refs_1_
  44.8 0.0 collective-permute-done.14.refs_3_
  44.8 0.8 %shard_map.72 = f32[2,8,16,1024]{3,2,1,0:T(8,128)} custom-call(s32[1]{0:T(128)} %bitcast.here_ref.refs_0_, f32[2,16,1024]{2,1,0:T(8,128)S(1)} %collective-permute-done.12.refs_1_, f32[2,16,1024]{2,1,0:T(8,128)S(1)} %collective-permute-done.13.refs_2_, f32[2,16,1024]{2,1,0:T(8,128)S(1)} %collective-permute-done.14.refs_3_, ...), custom_call_target="tpu_custom_call", output_to_operand_aliasing={{}: (4, {})} | custom-call | tf_op jit(solution)/shard_map/pallas_call | solution.py:234
  (5 shorter events, 0.0 us)
Async XLA Ops:
  0.6 1.2 %copy-start.1 = (f32[1,2,128,1024]{3,2,1,0:T(8,128)S(1)}, f32[1,2,128,1024]{3,2,1,0:T(8,128)}, u32[]{:S(2)}) copy-start(f32[1,2,128,1024]{3,2,1,0:T(8,128)} %param.4) | copy-start | bytes 3145732
  2.0 12.7 %collective-permute-start.4 = (f32[8,128]{1,0:T(8,128)S(1)}, f32[8,128]{1,0:T(8,128)S(1)}, u32[]{:S(2)}, u32[]{:S(2)}) collective-permute-start(f32[8,128]{1,0:T(8,128)S(1)} %get-tuple-element.39.refs_4_), channel_id=1, source_target_pairs={{0,3},{1,0},{2,1},{3,2},{4,7},{5,4},{6,5},{7,6},{8,11},{9,8},{10,9... | collective-permute-start | bytes 12296 | tf_op jit(solution)/shard_map/ppermute | solution.py:194
  7.1 7.6 %collective-permute-start.3 = (f32[8,128]{1,0:T(8,128)S(1)}, f32[8,128]{1,0:T(8,128)S(1)}, u32[]{:S(2)}, u32[]{:S(2)}) collective-permute-start(f32[8,128]{1,0:T(8,128)S(1)} %get-tuple-element.39.refs_4_), channel_id=1, source_target_pairs={{0,2},{1,3},{2,0},{3,1},{4,6},{5,7},{6,4},{7,5},{8,10},{9,11},{10,... | collective-permute-start | bytes 12296 | tf_op jit(solution)/shard_map/ppermute | solution.py:194
  7.1 7.6 %collective-permute-start.2 = (f32[8,128]{1,0:T(8,128)S(1)}, f32[8,128]{1,0:T(8,128)S(1)}, u32[]{:S(2)}, u32[]{:S(2)}) collective-permute-start(f32[8,128]{1,0:T(8,128)S(1)} %get-tuple-element.39.refs_4_), channel_id=1, source_target_pairs={{0,1},{1,2},{2,3},{3,0},{4,5},{5,6},{6,7},{7,4},{8,9},{9,10},{10,1... | collective-permute-start | bytes 12296 | tf_op jit(solution)/shard_map/ppermute | solution.py:194
  8.1 14.7 %collective-permute-start = (f32[2,16,1024]{2,1,0:T(8,128)S(1)}, f32[2,16,1024]{2,1,0:T(8,128)S(1)}, u32[]{:S(2)}, u32[]{:S(2)}) collective-permute-start(f32[2,16,1024]{2,1,0:T(8,128)S(1)} %get-tuple-element.37), channel_id=1, source_target_pairs={{0,24},{4,28},{8,16},{12,20},{16,8},{20,12},{24,0},{28,4},{1,25},{... | collective-permute-start | bytes 393224 | tf_op jit(solution)/shard_map/ppermute | solution.py:64
  10.6 2.7 %copy-start.2 = (s32[8,2]{0,1:T(2,128)S(1)}, s32[8,2]{0,1:T(2,128)}, u32[]{:S(2)}) copy-start(s32[8,2]{0,1:T(2,128)} %param.5) | copy-start | bytes 196
  10.6 14.0 %collective-permute-start.1 = (f32[2,16,1024]{2,1,0:T(8,128)S(1)}, f32[2,16,1024]{2,1,0:T(8,128)S(1)}, u32[]{:S(2)}, u32[]{:S(2)}) collective-permute-start(f32[2,16,1024]{2,1,0:T(8,128)S(1)} %get-tuple-element.38), channel_id=1, source_target_pairs={{0,28},{4,24},{8,20},{12,16},{16,12},{20,8},{24,4},{28,0},{1,29},{... | collective-permute-start | bytes 393224 | tf_op jit(solution)/shard_map/ppermute | solution.py:64
  15.6 23.2 %copy-start = (f32[32,1,16,1024]{3,2,1,0:T(8,128)S(1)}, f32[32,1,16,1024]{3,2,1,0:T(8,128)}, u32[]{:S(2)}) copy-start(f32[32,1,16,1024]{3,2,1,0:T(8,128)} %param.7) | copy-start | bytes 6291460
  15.6 4.7 %collective-permute-start.8 = (f32[2,8,128]{2,1,0:T(8,128)S(1)}, f32[2,8,128]{2,1,0:T(8,128)S(1)}, u32[]{:S(2)}, u32[]{:S(2)}) collective-permute-start(f32[2,8,128]{2,1,0:T(8,128)S(1)} %get-tuple-element.48), channel_id=1, source_target_pairs={{0,28},{4,24},{8,20},{12,16},{16,12},{20,8},{24,4},{28,0},{1,29},{... | collective-permute-start | bytes 24584 | tf_op jit(solution)/shard_map/ppermute | solution.py:64
  18.3 4.5 %collective-permute-start.7 = (f32[2,8,128]{2,1,0:T(8,128)S(1)}, f32[2,8,128]{2,1,0:T(8,128)S(1)}, u32[]{:S(2)}, u32[]{:S(2)}) collective-permute-start(f32[2,8,128]{2,1,0:T(8,128)S(1)} %get-tuple-element.48), channel_id=1, source_target_pairs={{0,24},{4,28},{8,16},{12,20},{16,8},{20,12},{24,0},{28,4},{1,25},{... | collective-permute-start | bytes 24584 | tf_op jit(solution)/shard_map/ppermute | solution.py:64
  18.7 6.0 %collective-permute-start.5 = (f32[2,16,1024]{2,1,0:T(8,128)S(1)}, f32[2,16,1024]{2,1,0:T(8,128)S(1)}, u32[]{:S(2)}, u32[]{:S(2)}) collective-permute-start(f32[2,16,1024]{2,1,0:T(8,128)S(1)} %get-tuple-element.46), channel_id=1, source_target_pairs={{0,8},{4,20},{8,0},{12,28},{16,24},{20,4},{24,16},{28,12},{1,9},{5... | collective-permute-start | bytes 393224 | tf_op jit(solution)/shard_map/ppermute | solution.py:64
  20.2 5.0 %collective-permute-start.6 = (f32[2,16,1024]{2,1,0:T(8,128)S(1)}, f32[2,16,1024]{2,1,0:T(8,128)S(1)}, u32[]{:S(2)}, u32[]{:S(2)}) collective-permute-start(f32[2,16,1024]{2,1,0:T(8,128)S(1)} %get-tuple-element.47), channel_id=1, source_target_pairs={{0,16},{4,12},{8,24},{12,4},{16,0},{20,28},{24,8},{28,20},{1,17},{... | collective-permute-start | bytes 393224 | tf_op jit(solution)/shard_map/ppermute | solution.py:64
  22.8 5.0 %collective-permute-start.9 = (f32[2,16,1024]{2,1,0:T(8,128)S(1)}, f32[2,16,1024]{2,1,0:T(8,128)S(1)}, u32[]{:S(2)}, u32[]{:S(2)}) collective-permute-start(f32[2,16,1024]{2,1,0:T(8,128)S(1)} %get-tuple-element.49), channel_id=1, source_target_pairs={{0,12},{4,16},{8,4},{12,24},{16,28},{20,0},{24,20},{28,8},{1,13},{... | collective-permute-start | bytes 393224 | tf_op jit(solution)/shard_map/ppermute | solution.py:64
  22.8 5.1 %collective-permute-start.10 = (f32[2,16,1024]{2,1,0:T(8,128)S(1)}, f32[2,16,1024]{2,1,0:T(8,128)S(1)}, u32[]{:S(2)}, u32[]{:S(2)}) collective-permute-start(f32[2,16,1024]{2,1,0:T(8,128)S(1)} %get-tuple-element.50), channel_id=1, source_target_pairs={{0,20},{4,8},{8,28},{12,0},{16,4},{20,24},{24,12},{28,16},{1,21},{... | collective-permute-start | bytes 393224 | tf_op jit(solution)/shard_map/ppermute | solution.py:64
  24.6 3.4 %collective-permute-start.11 = (f32[2,16,1024]{2,1,0:T(8,128)S(1)}, f32[2,16,1024]{2,1,0:T(8,128)S(1)}, u32[]{:S(2)}, u32[]{:S(2)}) collective-permute-start(f32[2,16,1024]{2,1,0:T(8,128)S(1)} %get-tuple-element.51), channel_id=1, source_target_pairs={{0,4},{4,0},{8,12},{12,8},{16,20},{20,16},{24,28},{28,24},{1,5},{5... | collective-permute-start | bytes 393224 | tf_op jit(solution)/shard_map/ppermute | solution.py:64
  28.8 7.4 %collective-permute-start.15 = (f32[2,16,1024]{2,1,0:T(8,128)S(1)}, f32[2,16,1024]{2,1,0:T(8,128)S(1)}, u32[]{:S(2)}, u32[]{:S(2)}) collective-permute-start(f32[2,16,1024]{2,1,0:T(8,128)S(1)} %get-tuple-element.56), channel_id=1, source_target_pairs={{0,24},{4,28},{8,16},{12,20},{16,8},{20,12},{24,0},{28,4},{1,25},{... | collective-permute-start | bytes 393224 | tf_op jit(solution)/shard_map/ppermute | solution.py:64
  31.4 6.9 %collective-permute-start.16 = (f32[2,16,1024]{2,1,0:T(8,128)S(1)}, f32[2,16,1024]{2,1,0:T(8,128)S(1)}, u32[]{:S(2)}, u32[]{:S(2)}) collective-permute-start(f32[2,16,1024]{2,1,0:T(8,128)S(1)} %get-tuple-element.57), channel_id=1, source_target_pairs={{0,28},{4,24},{8,20},{12,16},{16,12},{20,8},{24,4},{28,0},{1,29},{... | collective-permute-start | bytes 393224 | tf_op jit(solution)/shard_map/ppermute | solution.py:64
  31.7 13.1 %collective-permute-start.12 = (f32[2,16,1024]{2,1,0:T(8,128)S(1)}, f32[2,16,1024]{2,1,0:T(8,128)S(1)}, u32[]{:S(2)}, u32[]{:S(2)}) collective-permute-start(f32[2,16,1024]{2,1,0:T(8,128)S(1)} %get-tuple-element.53), channel_id=1, source_target_pairs={{0,12},{4,16},{8,4},{12,24},{16,28},{20,0},{24,20},{28,8},{1,13},{... | collective-permute-start | bytes 393224 | tf_op jit(solution)/shard_map/ppermute | solution.py:64
  33.0 10.8 %collective-permute-start.17 = (f32[2,16,1024]{2,1,0:T(8,128)S(1)}, f32[2,16,1024]{2,1,0:T(8,128)S(1)}, u32[]{:S(2)}, u32[]{:S(2)}) collective-permute-start(f32[2,16,1024]{2,1,0:T(8,128)S(1)} %get-tuple-element.58), channel_id=1, source_target_pairs={{0,8},{4,20},{8,0},{12,28},{16,24},{20,4},{24,16},{28,12},{1,9},{5... | collective-permute-start | bytes 393224 | tf_op jit(solution)/shard_map/ppermute | solution.py:64
  33.6 10.3 %collective-permute-start.18 = (f32[2,16,1024]{2,1,0:T(8,128)S(1)}, f32[2,16,1024]{2,1,0:T(8,128)S(1)}, u32[]{:S(2)}, u32[]{:S(2)}) collective-permute-start(f32[2,16,1024]{2,1,0:T(8,128)S(1)} %get-tuple-element.59), channel_id=1, source_target_pairs={{0,16},{4,12},{8,24},{12,4},{16,0},{20,28},{24,8},{28,20},{1,17},{... | collective-permute-start | bytes 393224 | tf_op jit(solution)/shard_map/ppermute | solution.py:64
  36.2 8.5 %collective-permute-start.13 = (f32[2,16,1024]{2,1,0:T(8,128)S(1)}, f32[2,16,1024]{2,1,0:T(8,128)S(1)}, u32[]{:S(2)}, u32[]{:S(2)}) collective-permute-start(f32[2,16,1024]{2,1,0:T(8,128)S(1)} %get-tuple-element.54), channel_id=1, source_target_pairs={{0,20},{4,8},{8,28},{12,0},{16,4},{20,24},{24,12},{28,16},{1,21},{... | collective-permute-start | bytes 393224 | tf_op jit(solution)/shard_map/ppermute | solution.py:64
  38.2 6.5 %collective-permute-start.14 = (f32[2,16,1024]{2,1,0:T(8,128)S(1)}, f32[2,16,1024]{2,1,0:T(8,128)S(1)}, u32[]{:S(2)}, u32[]{:S(2)}) collective-permute-start(f32[2,16,1024]{2,1,0:T(8,128)S(1)} %get-tuple-element.55), channel_id=1, source_target_pairs={{0,4},{4,0},{8,12},{12,8},{16,20},{20,16},{24,28},{28,24},{1,5},{5... | collective-permute-start | bytes 393224 | tf_op jit(solution)/shard_map/ppermute | solution.py:64

commit v3 on v2

v3 whole, which is shorter than its diff:
```python
import jax
import jax.numpy as jnp
from jax import lax
from jax.experimental import pallas as pl
from jax.experimental.pallas import tpu as pltpu
from jax.sharding import PartitionSpec as P

LEVEL_MODULES = 16
LEVELS = 2
MOST_UNROLLED = 16

outer_rate = 0.7
beta_coef = 0.9
moment_coef = outer_rate * beta_coef * beta_coef
grad_coef = outer_rate * (1.0 + beta_coef)

VMEM_LIMIT = 16 * 1024 * 1024

vmem = pl.BlockSpec(memory_space=pltpu.VMEM)
smem = pl.BlockSpec(memory_space=pltpu.SMEM)
anywhere = pl.BlockSpec(memory_space=pl.ANY)


def call(kernel, out_shape, in_specs, out_specs, **more):
    return pl.pallas_call(
        kernel,
        out_shape=out_shape,
        in_specs=in_specs,
        out_specs=out_specs,
        compiler_params=pltpu.CompilerParams(vmem_limit_bytes=VMEM_LIMIT),
        **more,
    )


def mirrored(k, size):
    if size < 8:
        return k
    return (k & ~6) | ((k & 2) << 1) | ((k & 4) >> 1)


def target(here, k, size):
    if isinstance(here, int):
        return here ^ (mirrored(k, size) if here & 1 else k)
    return here ^ jnp.where(here & 1 == 1, mirrored(k, size), k)


def origin(here, k, size):
    if isinstance(here, int):
        return here ^ (mirrored(k, size) if (here ^ k) & 1 else k)
    return here ^ jnp.where((here ^ k) & 1 == 1, mirrored(k, size), k)


def order_of(size):
    return sorted(range(2, size, 2), key=lambda k: (-bin(k).count("1"), k)) + [0]


def move(array, k, size):
    if k == 0:
        return array
    return lax.ppermute(array, "path", [(i, target(i, k, size)) for i in range(size)])


def pack_kernel(size, here_ref, delta_ref, square_ref, *outs):
    total = jnp.zeros(square_ref.shape, jnp.float32)
    order = order_of(size)
    for level in range(LEVELS):
        for j, k in enumerate(order):
            block = delta_ref[level, target(here_ref[0], k, size) // 2]
            outs[level * len(order) + j][...] = block
            block = block * block
            folded = block.reshape(-1, 8, block.shape[-1]).sum(axis=0)
            for lane in range(0, block.shape[-1], 128):
                total = total + folded[:, lane : lane + 128]
    square_ref[...] = total


def scale_kernel(entries, shards, here_ref, ids_ref, plan_ref, *refs):
    del plan_ref
    tiles, refs = refs[:shards], refs[shards:]
    tile = tiles[0][...]
    for other in tiles[1:]:
        tile = tile + other[...]
    total = jnp.broadcast_to(jnp.sum(tile, keepdims=True), (8, 128))
    rescale = 1.0 / jnp.sqrt(total / entries + 1e-06)
    count = len(refs) // 2
    rounds = count // LEVELS
    for level in range(LEVELS):
        own = ids_ref[here_ref[0], level]
        sharers = jnp.int32(0)
        for path in range(ids_ref.shape[0]):
            sharers = sharers + jnp.where(ids_ref[path, level] == own, 1, 0)
        factor = rescale / jnp.full((8, 128), sharers, jnp.int32).astype(jnp.float32)
        for j in range(level * rounds, (level + 1) * rounds):
            block, out = refs[j], refs[count + j]
            halves, rows, width = block.shape
            for half in range(halves):
                for row in range(0, rows, 8):
                    for lane in range(0, width, 128):
                        here = (half, slice(row, row + 8), slice(lane, lane + 128))
                        out[here] = block[here] * factor


def plan_kernel(here_ref, ids_ref, chosen_ref, sibling_ref, sender_ref, receiver_ref, module_ref):
    size = ids_ref.shape[0]
    order = order_of(size)
    rounds = len(order)
    here = here_ref[0]
    for level in range(LEVELS):
        first = level * LEVEL_MODULES
        for module in range(LEVEL_MODULES):
            module_ref[first + module] = -1
        sources = [ids_ref[origin(core, k, size), level] + first for core in (here, here ^ 1) for k in order]
        for i in reversed(range(size)):
            module_ref[sources[i]] = i
        for i in range(size):
            sender_ref[level, i] = module_ref[sources[i]]
        for j, k in enumerate(order):
            module = ids_ref[target(here, k, size), level] + first
            chosen_ref[level, j] = module
            receiver_ref[level, j] = module_ref[module]
            sibling_ref[level, j] = ids_ref[target(here ^ 1, k, size), level] + first


def base_kernel(sibling_ref, decayed_ref, out_ref):
    for level in range(out_ref.shape[0]):
        for j in range(out_ref.shape[1]):
            out_ref[level, j] = decayed_ref[sibling_ref[level, j]]


def join_kernel(rounds, *refs):
    for j in range(rounds):
        refs[-1][j] = refs[j][...]


def outgoing_kernel(
    level, here_ref, chosen_ref, sender_ref, receiver_ref, decayed_ref, base_ref, mine_ref, theirs_ref, *refs
):
    outs, grad_ref = refs[:-1], refs[-1]
    rounds = len(outs)
    core = here_ref[0] & 1
    for j in range(rounds):
        grad_ref[j] = mine_ref[j]
        grad_ref[rounds + j] = theirs_ref[j]
    for i in range(1, 2 * rounds):
        leader = sender_ref[level, i]

        @pl.when(leader != i)
        def _():
            grad_ref[leader] += grad_ref[i]

    for j, out in enumerate(outs):
        leader = receiver_ref[level, j]
        out[core] = decayed_ref[chosen_ref[level, j]] - grad_coef * grad_ref[leader, core]
        out[1 - core] = base_ref[level, j] - grad_coef * grad_ref[leader, 1 - core]


def state_kernel(level, here_ref, module_ref, grad_ref, decayed_ref, momentum_ref, *outs):
    new_params_ref, new_momentum_ref = outs[-2:]
    core = here_ref[0] & 1
    count = new_params_ref.shape[0]
    first = level * LEVEL_MODULES + pl.program_id(0) * count
    for place in range(count):
        module = first + place
        leader = module_ref[module]
        taken = jnp.where(leader < 0, 0.0, 1.0)
        grad = taken * grad_ref[jnp.maximum(leader, 0), core]
        new_momentum_ref[place] = beta_coef * momentum_ref[module] + grad
        new_params_ref[place] = decayed_ref[module] - grad_coef * grad


def assemble_kernel(size, level, here_ref, *refs):
    order = order_of(size)
    out_ref, sems = refs[-2:]
    copies = []
    for j, k in enumerate(order):
        place = origin(here_ref[0], k, size) // 2
        copies.append(pltpu.make_async_copy(refs[j], out_ref.at[level, place], sems.at[j]))
    for copy in copies:
        copy.start()
    for copy in copies:
        copy.wait()


def local(path_delta, assign, params, momentum):
    own_slab = path_delta[0]
    size = assign.shape[0]
    module_count, _, own_rows, width = params.shape
    shards = lax.axis_size("shard")
    entries = float(own_slab.size * shards)
    state_in = params.reshape(module_count, own_rows, width)
    moment_in = momentum.reshape(module_count, own_rows, width)
    split_slab = own_slab.reshape(LEVELS, size // 2, 2, own_rows, width)
    here = lax.axis_index("path").astype(jnp.int32).reshape(1)
    order = order_of(size)
    rounds = len(order)
    chip_rows = jax.ShapeDtypeStruct((2, own_rows, width), jnp.float32)

    squares, *raw = call(
        lambda *refs: pack_kernel(size, *refs),
        [jax.ShapeDtypeStruct((8, 128), jnp.float32)] + [chip_rows] * (LEVELS * rounds),
        [smem, vmem],
        [vmem] * (1 + LEVELS * rounds),
    )(here, split_slab)
    tiles = [squares] + [
        lax.ppermute(squares, "shard", [(i, (i + step) % shards) for i in range(shards)])
        for step in range(1, shards)
    ]
    by_round = jax.ShapeDtypeStruct((LEVELS, rounds), jnp.int32)
    chosen, sibling, sender, receiver, leaders = call(
        plan_kernel,
        [
            by_round,
            by_round,
            jax.ShapeDtypeStruct((LEVELS, size), jnp.int32),
            by_round,
            jax.ShapeDtypeStruct((module_count,), jnp.int32),
        ],
        [smem, smem],
        [smem] * 5,
    )(here, assign)
    scaled = call(
        lambda *refs: scale_kernel(entries, shards, *refs),
        [chip_rows] * (LEVELS * rounds),
        [smem, smem, smem] + [vmem] * (shards + LEVELS * rounds),
        [vmem] * (LEVELS * rounds),
    )(here, assign, chosen, *tiles, *raw)
    decayed = state_in - moment_coef * moment_in
    base = call(
        base_kernel,
        jax.ShapeDtypeStruct((LEVELS, rounds, own_rows, width), jnp.float32),
        [smem, vmem],
        vmem,
    )(sibling, decayed)
    swap = [(i, i ^ 1) for i in range(size)]
    base = lax.ppermute(base, "path", swap)

    path_params, new_state, new_moment, before = None, None, None, []
    block = LEVEL_MODULES // 2
    for level in range(LEVELS):
        received = [move(scaled[level * rounds + j], k, size) for j, k in enumerate(order)]
        mine = call(
            lambda *refs: join_kernel(rounds, *refs),
            jax.ShapeDtypeStruct((rounds, 2, own_rows, width), jnp.float32),
            [vmem] * rounds + [anywhere] * len(before),
            vmem,
        )(*received, *before)
        theirs = lax.ppermute(mine, "path", swap)
        *outgoing, grad = call(
            lambda *refs, level=level: outgoing_kernel(level, *refs),
            [chip_rows] * rounds + [jax.ShapeDtypeStruct((size, 2, own_rows, width), jnp.float32)],
            [smem] * 4 + [vmem] * 4,
            [vmem] * (rounds + 1),
        )(here, chosen, sender, receiver, decayed, base, mine, theirs)
        before = [grad]
        returned = [move(outgoing[j], k, size) for j, k in enumerate(order)]
        held = [] if level == 0 else [path_params]
        path_params = call(
            lambda *refs, level=level: assemble_kernel(size, level, *refs),
            jax.ShapeDtypeStruct(split_slab.shape, jnp.float32),
            [smem] + [anywhere] * (rounds + len(held)),
            anywhere,
            scratch_shapes=[pltpu.SemaphoreType.DMA((rounds,))],
            input_output_aliases={1 + rounds: 0} if held else {},
        )(here, *returned, *held)
        held = [] if level == 0 else [new_state, new_moment]
        steps = LEVEL_MODULES // block
        state_block = pl.BlockSpec((block, own_rows, width), lambda i, level=level: (i + level * steps, 0, 0))
        new_state, new_moment = call(
            lambda *refs, level=level: state_kernel(level, *refs),
            [jax.ShapeDtypeStruct(state_in.shape, jnp.float32)] * 2,
            [smem, smem, vmem, vmem, vmem] + [anywhere] * len(held),
            [state_block, state_block],
            grid=(steps,),
            input_output_aliases={5: 0, 6: 1} if held else {},
        )(here, leaders, grad, decayed, moment_in, *held)
    return (path_params.reshape(path_delta.shape), new_state[:, None], new_moment[:, None])


def local_wide(path_delta, assign, params, momentum):
    own_slab = path_delta[0]
    path_count = assign.shape[0]
    module_count, _, own_rows, width = params.shape
    entries = float(own_slab.size * lax.axis_size("shard"))
    total_sq = lax.psum(jnp.sum(own_slab * own_slab), "shard")
    scaled = own_slab * (1.0 / jnp.sqrt(total_sq / entries + 1e-06))
    received = lax.all_to_all(
        scaled.reshape(LEVELS, path_count, own_rows, width), "path", split_axis=1, concat_axis=1, tiled=True
    )
    flat_ids = (assign + LEVEL_MODULES * jnp.arange(LEVELS, dtype=jnp.int32)[None, :]).T.reshape(-1)
    member = (jnp.arange(module_count, dtype=jnp.int32)[:, None] == flat_ids[None, :]).astype(jnp.float32)
    mean = member / jnp.maximum(jnp.sum(member, axis=1), 1.0)[:, None]
    grad = jnp.einsum(
        "mp,prd->mrd", mean, received.reshape(-1, own_rows, width), precision=lax.Precision.HIGHEST
    )
    new_moment = beta_coef * momentum[:, 0] + grad
    new_state = params[:, 0] - outer_rate * (grad + beta_coef * new_moment)
    outgoing = jnp.take(new_state, flat_ids, axis=0).reshape(LEVELS, path_count, own_rows, width)
    returned = lax.all_to_all(outgoing, "path", split_axis=1, concat_axis=1, tiled=True)
    return (returned.reshape(path_delta.shape), new_state[:, None], new_moment[:, None])


def solution(mesh):
    in_specs = (
        P("path", None, "shard", None),
        P(),
        P(None, "shard", "path", None),
        P(None, "shard", "path", None),
    )
    out_specs = (
        P("path", None, "shard", None),
        P(None, "shard", "path", None),
        P(None, "shard", "path", None),
    )
    chosen = local if 4 <= mesh.shape["path"] <= MOST_UNROLLED else local_wide
    return jax.shard_map(chosen, mesh=mesh, in_specs=in_specs, out_specs=out_specs, check_vma=False)
```

time: 45.7 us -> 47.9 us (1.048)
  starting transfers between devices: 23.3 us -> 20.2 us
  waiting for transfers between devices: 9.58 us -> 12.6 us
  Pallas kernels: 7.93 us -> 10.2 us
  local copies, waits for them, and re-layouts: 1.31 us -> 2.12 us
  other arithmetic: 2.67 us -> 2.03 us
    ppermute x16 -> x12, starting transfers between devices: 17.2 us -> 13.8 us  [move(): lax.ppermute(array, 'path', [(i, target(i, k, size)) for i in range(size)])]
    ppermute x3, waiting for transfers between devices: 0.01 us -> 2.3 us  [local(): lax.ppermute(squares, 'shard', [(i, (i + step) % shards) for i in range(s...]
    pallas_call x7 -> x12, Pallas kernels: 7.93 us -> 10.2 us  [the longest x2 3.97 us: local(): call(lambda *refs, level=level: state_kernel(level, *refs), [jax.ShapeDty...]
    unnamed x7 -> x5, local copies, waits for them, and re-layouts: 1.31 us -> 2.12 us
    ppermute x16 -> x12, waiting for transfers between devices: 9.57 us -> 10.2 us  [move(): lax.ppermute(array, 'path', [(i, target(i, k, size)) for i in range(size)])]
    sub x1, other arithmetic: 2.67 us -> 2.03 us  [local(): decayed = state_in - moment_coef * moment_in]
  transfers between devices with their start and end apart: 19 -> 18, of which waited for: 8 -> 12; matrix products, arithmetic and copies ran while one was open for 6% -> 6% of each run, Pallas kernels for 13% -> 18%
where the time goes in v3:
time: 47.9 us; the launch traced here: 47.8 us
  starting transfers between devices  20.2 us (42%)
  waiting for transfers between devices  12.6 us (26%)
  Pallas kernels  10.2 us (21%)
  local copies, waits for them, and re-layouts  2.12 us (4%)
  other arithmetic  2.03 us (4%)
  between operations  0.74 us (2%)
    ppermute x12, starting transfers between devices, move(): lax.ppermute(array, 'path', [(i, target(i, k, size)) for i in range(size)])  13.8 us
    ppermute x12, waiting for transfers between devices, move(): lax.ppermute(array, 'path', [(i, target(i, k, size)) for i in range(size)])  10.2 us
    ppermute x3, starting transfers between devices, local(): lax.ppermute(squares, 'shard', [(i, (i + step) % shards) for i in range(s...  6.11 us
    pallas_call x2, Pallas kernels, local(): call(lambda *refs, level=level: state_kernel(level, *refs), [jax.ShapeDty...  3.97 us
    ppermute x3, waiting for transfers between devices, local(): lax.ppermute(squares, 'shard', [(i, (i + step) % shards) for i in range(s...  2.3 us
    unnamed x5, local copies, waits for them, and re-layouts  2.12 us
    sub x1, other arithmetic, local(): decayed = state_in - moment_coef * moment_in  2.03 us
    pallas_call x2, Pallas kernels, local(): call(lambda *refs, level=level: outgoing_kernel(level, *refs), [chip_rows...  1.66 us
  transfers between devices with their start and end apart: 18, of which 12 were waited for; matrix products, arithmetic and copies ran while one was open for 6% of the time, Pallas kernels for 18%

profile of v3, /device:TPU:0, one launch (start us, length us, event | category | flops | bytes accessed | tf_op | source)
XLA Modules:
  0.0 47.8 jit_solution(2927334027755799879)
XLA Ops:
  0.7 1.4 %copy-done.1 = f32[1,2,128,1024]{3,2,1,0:T(8,128)S(1)} copy-done((f32[1,2,128,1024]{3,2,1,0:T(8,128)S(1)}, f32[1,2,128,1024]{3,2,1,0:T(8,128)}, u32[]{:S(2)}) %copy-start.1) | copy-done | bytes 1048600
  2.0 0.1 shard_map.69
  2.1 5.1 %collective-permute-start.3 = (f32[8,128]{1,0:T(8,128)S(1)}, f32[8,128]{1,0:T(8,128)S(1)}, u32[]{:S(2)}, u32[]{:S(2)}) collective-permute-start(f32[8,128]{1,0:T(8,128)S(1)} %get-tuple-element.43.refs_3_), channel_id=1, source_target_pairs={{0,3},{1,0},{2,1},{3,2},{4,7},{5,4},{6,5},{7,6},{8,11},{9,8},{10,9... | collective-permute-start | bytes 12296 | tf_op jit(solution)/shard_map/ppermute | solution.py:205
  7.2 0.0 collective-permute-start.2
  7.2 1.0 %collective-permute-start.1 = (f32[8,128]{1,0:T(8,128)S(1)}, f32[8,128]{1,0:T(8,128)S(1)}, u32[]{:S(2)}, u32[]{:S(2)}) collective-permute-start(f32[8,128]{1,0:T(8,128)S(1)} %get-tuple-element.43.refs_3_), channel_id=1, source_target_pairs={{0,1},{1,2},{2,3},{3,0},{4,5},{5,6},{6,7},{7,4},{8,9},{9,10},{10,1... | collective-permute-start | bytes 12296 | tf_op jit(solution)/shard_map/ppermute | solution.py:205
  8.2 0.8 %copy.10.ids_ref.refs_1_ = s32[8,2]{1,0:T(8,128)S(1)} copy(s32[8,2]{0,1:T(2,128)} %param.5) | data formatting | bytes 128 | tf_op args[1]
  9.0 1.3 %shard_map.67 = (s32[2,4]{1,0:T(2,128)S(1)}, s32[2,4]{1,0:T(2,128)S(1)}, s32[2,8]{1,0:T(2,128)S(1)}, s32[2,4]{1,0:T(2,128)S(1)}, s32[32]{0:T(128)S(1)}) custom-call(s32[1]{0:T(128)} %bitcast.here_ref.refs_0_, s32[8,2]{1,0:T(8,128)S(1)} %copy.10.ids_ref.refs_1_), custom_call_target="tpu_custom_call" | custom-call | tf_op jit(solution)/shard_map/pallas_call | solution.py:209
  10.3 0.0 collective-permute-done.3.refs_6_
  10.3 1.4 %collective-permute-done.2.refs_5_ = f32[8,128]{1,0:T(8,128)S(1)} collective-permute-done((f32[8,128]{1,0:T(8,128)S(1)}, f32[8,128]{1,0:T(8,128)S(1)}, u32[]{:S(2)}, u32[]{:S(2)}) %collective-permute-start.2) | collective-permute-done | bytes 4128 | tf_op jit(solution)/shard_map/ppermute | solution.py:205
  11.7 0.9 %collective-permute-done.1.refs_4_ = f32[8,128]{1,0:T(8,128)S(1)} collective-permute-done((f32[8,128]{1,0:T(8,128)S(1)}, f32[8,128]{1,0:T(8,128)S(1)}, u32[]{:S(2)}, u32[]{:S(2)}) %collective-permute-start.1) | collective-permute-done | bytes 4128 | tf_op jit(solution)/shard_map/ppermute | solution.py:205
  12.6 0.8 %shard_map.70 = (f32[2,16,1024]{2,1,0:T(8,128)S(1)}, f32[2,16,1024]{2,1,0:T(8,128)S(1)}, f32[2,16,1024]{2,1,0:T(8,128)S(1)}, f32[2,16,1024]{2,1,0:T(8,128)S(1)},...) custom-call(s32[1]{0:T(128)} %bitcast.here_ref.refs_0_, ...), custom_call_target="tpu_custom_call" | custom-call | tf_op jit(solution)/shard_map/pallas_call | solution.py:221
  13.5 2.5 %collective-permute-start.7 = (f32[2,16,1024]{2,1,0:T(8,128)S(1)}, f32[2,16,1024]{2,1,0:T(8,128)S(1)}, u32[]{:S(2)}, u32[]{:S(2)}) collective-permute-start(f32[2,16,1024]{2,1,0:T(8,128)S(1)} %get-tuple-element.56), channel_id=1, source_target_pairs={{0,24},{4,28},{8,16},{12,20},{16,8},{20,12},{24,0},{28,4},{1,25},{... | collective-permute-start | bytes 393224 | tf_op jit(solution)/shard_map/ppermute | solution.py:60
  16.0 0.5 %collective-permute-start.8 = (f32[2,16,1024]{2,1,0:T(8,128)S(1)}, f32[2,16,1024]{2,1,0:T(8,128)S(1)}, u32[]{:S(2)}, u32[]{:S(2)}) collective-permute-start(f32[2,16,1024]{2,1,0:T(8,128)S(1)} %get-tuple-element.57), channel_id=1, source_target_pairs={{0,8},{4,20},{8,0},{12,28},{16,24},{20,4},{24,16},{28,12},{1,9},{5... | collective-permute-start | bytes 393224 | tf_op jit(solution)/shard_map/ppermute | solution.py:60
  16.5 0.5 %collective-permute-start.9 = (f32[2,16,1024]{2,1,0:T(8,128)S(1)}, f32[2,16,1024]{2,1,0:T(8,128)S(1)}, u32[]{:S(2)}, u32[]{:S(2)}) collective-permute-start(f32[2,16,1024]{2,1,0:T(8,128)S(1)} %get-tuple-element.58), channel_id=1, source_target_pairs={{0,16},{4,12},{8,24},{12,4},{16,0},{20,28},{24,8},{28,20},{1,17},{... | collective-permute-start | bytes 393224 | tf_op jit(solution)/shard_map/ppermute | solution.py:60
  17.0 2.0 %bitcast_subtract_fusion.decayed_ref.refs_4_.refs_3_ = f32[32,16,1024]{2,1,0:T(8,128)S(1)} fusion(f32[32,1,16,1024]{3,2,1,0:T(8,128)} %param.6, f32[32,1,16,1024]{3,2,1,0:T(8,128)S(1)} %copy-done), kind=kLoop, calls=%fused_computation | loop fusion | flops 1048576 | bytes 6291456 | tf_op jit(solution)/shard_map/sub | solution.py:227
  19.0 0.6 %shard_map.68 = f32[2,4,16,1024]{3,2,1,0:T(8,128)S(1)} custom-call(s32[2,4]{1,0:T(2,128)S(1)} %get-tuple-element.42.sibling_ref, f32[32,16,1024]{2,1,0:T(8,128)S(1)} %bitcast_subtract_fusion.decayed_ref.refs_4_.refs_3_), custom_call_target="tpu_custom_call" | custom-call | tf_op jit(solution)/shard_map/pallas_call | solution.py:228
  19.6 0.1 collective-permute-start
  19.7 1.1 %collective-permute-done.7.refs_0_ = f32[2,16,1024]{2,1,0:T(8,128)S(1)} collective-permute-done((f32[2,16,1024]{2,1,0:T(8,128)S(1)}, f32[2,16,1024]{2,1,0:T(8,128)S(1)}, u32[]{:S(2)}, u32[]{:S(2)}) %collective-permute-start.7) | collective-permute-done | bytes 131104 | tf_op jit(solution)/shard_map/ppermute | solution.py:60
  20.8 0.3 collective-permute-done.8.refs_1_
  21.1 0.7 %collective-permute-done.9.refs_2_ = f32[2,16,1024]{2,1,0:T(8,128)S(1)} collective-permute-done((f32[2,16,1024]{2,1,0:T(8,128)S(1)}, f32[2,16,1024]{2,1,0:T(8,128)S(1)}, u32[]{:S(2)}, u32[]{:S(2)}) %collective-permute-start.9) | collective-permute-done | bytes 131104 | tf_op jit(solution)/shard_map/ppermute | solution.py:60
  21.9 0.1 collective-permute-start.10
  22.0 1.8 %collective-permute-start.4 = (f32[2,16,1024]{2,1,0:T(8,128)S(1)}, f32[2,16,1024]{2,1,0:T(8,128)S(1)}, u32[]{:S(2)}, u32[]{:S(2)}) collective-permute-start(f32[2,16,1024]{2,1,0:T(8,128)S(1)} %get-tuple-element.52), channel_id=1, source_target_pairs={{0,24},{4,28},{8,16},{12,20},{16,8},{20,12},{24,0},{28,4},{1,25},{... | collective-permute-start | bytes 393224 | tf_op jit(solution)/shard_map/ppermute | solution.py:60
  23.7 0.6 %collective-permute-start.5 = (f32[2,16,1024]{2,1,0:T(8,128)S(1)}, f32[2,16,1024]{2,1,0:T(8,128)S(1)}, u32[]{:S(2)}, u32[]{:S(2)}) collective-permute-start(f32[2,16,1024]{2,1,0:T(8,128)S(1)} %get-tuple-element.53), channel_id=1, source_target_pairs={{0,8},{4,20},{8,0},{12,28},{16,24},{20,4},{24,16},{28,12},{1,9},{5... | collective-permute-start | bytes 393224 | tf_op jit(solution)/shard_map/ppermute | solution.py:60
  24.3 1.2 %collective-permute-start.6 = (f32[2,16,1024]{2,1,0:T(8,128)S(1)}, f32[2,16,1024]{2,1,0:T(8,128)S(1)}, u32[]{:S(2)}, u32[]{:S(2)}) collective-permute-start(f32[2,16,1024]{2,1,0:T(8,128)S(1)} %get-tuple-element.54), channel_id=1, source_target_pairs={{0,16},{4,12},{8,24},{12,4},{16,0},{20,28},{24,8},{28,20},{1,17},{... | collective-permute-start | bytes 393224 | tf_op jit(solution)/shard_map/ppermute | solution.py:60
  25.5 0.0 collective-permute-done.refs_5_
  25.5 0.0 collective-permute-done.10.refs_7_
  25.5 0.8 %shard_map.72 = (f32[2,16,1024]{2,1,0:T(8,128)S(1)}, f32[2,16,1024]{2,1,0:T(8,128)S(1)}, f32[2,16,1024]{2,1,0:T(8,128)S(1)}, f32[2,16,1024]{2,1,0:T(8,128)S(1)}, f32[8,2,16,1024]{3,2,1,0:T(8,128)S(1)}) custom-call(s32[1]{0:T(128)} %bitcast.here_ref.refs_0_, s32[2,4]{1,0:T(2,128)S(1)} %get-tuple-element.39.refs_2_.refs_1_, ...), custom_call_target="tpu_custom_call" | custom-call | tf_op jit(solution)/shard_map/pallas_call | solution.py:248
  26.3 2.9 %collective-permute-done.4.refs_0_ = f32[2,16,1024]{2,1,0:T(8,128)S(1)} collective-permute-done((f32[2,16,1024]{2,1,0:T(8,128)S(1)}, f32[2,16,1024]{2,1,0:T(8,128)S(1)}, u32[]{:S(2)}, u32[]{:S(2)}) %collective-permute-start.4) | collective-permute-done | bytes 131104 | tf_op jit(solution)/shard_map/ppermute | solution.py:60
  29.3 1.7 %collective-permute-done.5.refs_1_ = f32[2,16,1024]{2,1,0:T(8,128)S(1)} collective-permute-done((f32[2,16,1024]{2,1,0:T(8,128)S(1)}, f32[2,16,1024]{2,1,0:T(8,128)S(1)}, u32[]{:S(2)}, u32[]{:S(2)}) %collective-permute-start.5) | collective-permute-done | bytes 131104 | tf_op jit(solution)/shard_map/ppermute | solution.py:60
  31.0 0.6 %collective-permute-done.6.refs_2_ = f32[2,16,1024]{2,1,0:T(8,128)S(1)} collective-permute-done((f32[2,16,1024]{2,1,0:T(8,128)S(1)}, f32[2,16,1024]{2,1,0:T(8,128)S(1)}, u32[]{:S(2)}, u32[]{:S(2)}) %collective-permute-start.6) | collective-permute-done | bytes 131104 | tf_op jit(solution)/shard_map/ppermute | solution.py:60
  31.6 0.1 collective-permute-start.11
  31.7 1.8 %collective-permute-start.15 = (f32[2,16,1024]{2,1,0:T(8,128)S(1)}, f32[2,16,1024]{2,1,0:T(8,128)S(1)}, u32[]{:S(2)}, u32[]{:S(2)}) collective-permute-start(f32[2,16,1024]{2,1,0:T(8,128)S(1)} %get-tuple-element.65), channel_id=1, source_target_pairs={{0,24},{4,28},{8,16},{12,20},{16,8},{20,12},{24,0},{28,4},{1,25},{... | collective-permute-start | bytes 393224 | tf_op jit(solution)/shard_map/ppermute | solution.py:60
  33.5 0.6 %collective-permute-start.16 = (f32[2,16,1024]{2,1,0:T(8,128)S(1)}, f32[2,16,1024]{2,1,0:T(8,128)S(1)}, u32[]{:S(2)}, u32[]{:S(2)}) collective-permute-start(f32[2,16,1024]{2,1,0:T(8,128)S(1)} %get-tuple-element.66), channel_id=1, source_target_pairs={{0,8},{4,20},{8,0},{12,28},{16,24},{20,4},{24,16},{28,12},{1,9},{5... | collective-permute-start | bytes 393224 | tf_op jit(solution)/shard_map/ppermute | solution.py:60
  34.0 1.2 %collective-permute-start.17 = (f32[2,16,1024]{2,1,0:T(8,128)S(1)}, f32[2,16,1024]{2,1,0:T(8,128)S(1)}, u32[]{:S(2)}, u32[]{:S(2)}) collective-permute-start(f32[2,16,1024]{2,1,0:T(8,128)S(1)} %get-tuple-element.67), channel_id=1, source_target_pairs={{0,16},{4,12},{8,24},{12,4},{16,0},{20,28},{24,8},{28,20},{1,17},{... | collective-permute-start | bytes 393224 | tf_op jit(solution)/shard_map/ppermute | solution.py:60
  35.2 0.0 collective-permute-done.11.refs_7_
  35.3 0.8 %shard_map.74 = (f32[2,16,1024]{2,1,0:T(8,128)S(1)}, f32[2,16,1024]{2,1,0:T(8,128)S(1)}, f32[2,16,1024]{2,1,0:T(8,128)S(1)}, f32[2,16,1024]{2,1,0:T(8,128)S(1)}, f32[8,2,16,1024]{3,2,1,0:T(8,128)S(1)}) custom-call(s32[1]{0:T(128)} %bitcast.here_ref.refs_0_, s32[2,4]{1,0:T(2,128)S(1)} %get-tuple-element.39.refs_2_.refs_1_, ...), custom_call_target="tpu_custom_call" | custom-call | tf_op jit(solution)/shard_map/pallas_call | solution.py:248
  36.1 1.8 %collective-permute-start.12 = (f32[2,16,1024]{2,1,0:T(8,128)S(1)}, f32[2,16,1024]{2,1,0:T(8,128)S(1)}, u32[]{:S(2)}, u32[]{:S(2)}) collective-permute-start(f32[2,16,1024]{2,1,0:T(8,128)S(1)} %get-tuple-element.61), channel_id=1, source_target_pairs={{0,24},{4,28},{8,16},{12,20},{16,8},{20,12},{24,0},{28,4},{1,25},{... | collective-permute-start | bytes 393224 | tf_op jit(solution)/shard_map/ppermute | solution.py:60
  37.8 0.6 %collective-permute-start.13 = (f32[2,16,1024]{2,1,0:T(8,128)S(1)}, f32[2,16,1024]{2,1,0:T(8,128)S(1)}, u32[]{:S(2)}, u32[]{:S(2)}) collective-permute-start(f32[2,16,1024]{2,1,0:T(8,128)S(1)} %get-tuple-element.62), channel_id=1, source_target_pairs={{0,8},{4,20},{8,0},{12,28},{16,24},{20,4},{24,16},{28,12},{1,9},{5... | collective-permute-start | bytes 393224 | tf_op jit(solution)/shard_map/ppermute | solution.py:60
  38.4 0.6 %collective-permute-done.15.refs_1_ = f32[2,16,1024]{2,1,0:T(8,128)S(1)} collective-permute-done((f32[2,16,1024]{2,1,0:T(8,128)S(1)}, f32[2,16,1024]{2,1,0:T(8,128)S(1)}, u32[]{:S(2)}, u32[]{:S(2)}) %collective-permute-start.15) | collective-permute-done | bytes 131104 | tf_op jit(solution)/shard_map/ppermute | solution.py:60
  39.0 0.8 %collective-permute-start.14 = (f32[2,16,1024]{2,1,0:T(8,128)S(1)}, f32[2,16,1024]{2,1,0:T(8,128)S(1)}, u32[]{:S(2)}, u32[]{:S(2)}) collective-permute-start(f32[2,16,1024]{2,1,0:T(8,128)S(1)} %get-tuple-element.63), channel_id=1, source_target_pairs={{0,16},{4,12},{8,24},{12,4},{16,0},{20,28},{24,8},{28,20},{1,17},{... | collective-permute-start | bytes 393224 | tf_op jit(solution)/shard_map/ppermute | solution.py:60
  39.8 2.0 %shard_map.77 = (f32[32,16,1024]{2,1,0:T(8,128)}, f32[32,16,1024]{2,1,0:T(8,128)}) custom-call(s32[1]{0:T(128)} %bitcast.here_ref.refs_0_, s32[32]{0:T(128)S(1)} %get-tuple-element.69.refs_1_, f32[8,2,16,1024]{3,2,1,0:T(8,128)S(1)} %get-tuple-element.60.refs_4_.refs_2_, f32[32,16,1024]{2,1,0:T(8,128)S(1)} %bitcast_subtract_fusion.decayed_ref.refs_4_.refs_3_, ...), custom_call_target="tpu_custom_call" | custom-call | tf_op jit(solution)/shard_map/pallas_call | solution.py:268
  41.8 0.0 collective-permute-done.16.refs_2_
  41.8 0.1 collective-permute-done.17.refs_3_
  41.9 0.8 %shard_map.75.refs_5_ = f32[2,4,2,16,1024]{4,3,2,1,0:T(8,128)} custom-call(s32[1]{0:T(128)} %bitcast.here_ref.refs_0_, f32[2,16,1024]{2,1,0:T(8,128)S(1)} %collective-permute-done.15.refs_1_, f32[2,16,1024]{2,1,0:T(8,128)S(1)} %collective-permute-done.16.refs_2_, f32[2,16,1024]{2,1,0:T(8,128)S(1)} %collective-permute-done.17.refs_3_, ...), custom_call_target="tpu_custom_call" | custom-call | tf_op jit(solution)/shard_map/pallas_call | solution.py:257
  42.7 2.0 %shard_map.78 = (f32[32,16,1024]{2,1,0:T(8,128)}, f32[32,16,1024]{2,1,0:T(8,128)}) custom-call(s32[1]{0:T(128)} %bitcast.here_ref.refs_0_, s32[32]{0:T(128)S(1)} %get-tuple-element.69.refs_1_, f32[8,2,16,1024]{3,2,1,0:T(8,128)S(1)} %get-tuple-element.70.refs_2_, ...), custom_call_target="tpu_custom_call", output_to_operand_aliasing={{0}: (5, {}), {1}: (6, {})} | custom-call | tf_op jit(solution)/shard_map/pallas_call | solution.py:268
  44.7 1.7 %collective-permute-done.13.refs_2_ = f32[2,16,1024]{2,1,0:T(8,128)S(1)} collective-permute-done((f32[2,16,1024]{2,1,0:T(8,128)S(1)}, f32[2,16,1024]{2,1,0:T(8,128)S(1)}, u32[]{:S(2)}, u32[]{:S(2)}) %collective-permute-start.13) | collective-permute-done | bytes 131104 | tf_op jit(solution)/shard_map/ppermute | solution.py:60
  46.4 0.6 %collective-permute-done.14.refs_3_ = f32[2,16,1024]{2,1,0:T(8,128)S(1)} collective-permute-done((f32[2,16,1024]{2,1,0:T(8,128)S(1)}, f32[2,16,1024]{2,1,0:T(8,128)S(1)}, u32[]{:S(2)}, u32[]{:S(2)}) %collective-permute-start.14) | collective-permute-done | bytes 131104 | tf_op jit(solution)/shard_map/ppermute | solution.py:60
  46.9 0.8 %shard_map.76 = f32[2,4,2,16,1024]{4,3,2,1,0:T(8,128)} custom-call(s32[1]{0:T(128)} %bitcast.here_ref.refs_0_, f32[2,16,1024]{2,1,0:T(8,128)S(1)} %collective-permute-done.12.refs_1_, f32[2,16,1024]{2,1,0:T(8,128)S(1)} %collective-permute-done.13.refs_2_, f32[2,16,1024]{2,1,0:T(8,128)S(1)} %collective-permute-done.14.refs_3_, ...), custom_call_target="tpu_custom_call", output_to_operand_aliasing={{}: (5, {})} | custom-call | tf_op jit(solution)/shard_map/pallas_call | solution.py:257
  (6 shorter events, 0.1 us)
Async XLA Ops:
  0.6 16.4 %copy-start = (f32[32,1,16,1024]{3,2,1,0:T(8,128)S(1)}, f32[32,1,16,1024]{3,2,1,0:T(8,128)}, u32[]{:S(2)}) copy-start(f32[32,1,16,1024]{3,2,1,0:T(8,128)} %param.7) | copy-start | bytes 6291460
  0.6 1.4 %copy-start.1 = (f32[1,2,128,1024]{3,2,1,0:T(8,128)S(1)}, f32[1,2,128,1024]{3,2,1,0:T(8,128)}, u32[]{:S(2)}) copy-start(f32[1,2,128,1024]{3,2,1,0:T(8,128)} %param.4) | copy-start | bytes 3145732
  2.1 8.2 %collective-permute-start.3 = (f32[8,128]{1,0:T(8,128)S(1)}, f32[8,128]{1,0:T(8,128)S(1)}, u32[]{:S(2)}, u32[]{:S(2)}) collective-permute-start(f32[8,128]{1,0:T(8,128)S(1)} %get-tuple-element.43.refs_3_), channel_id=1, source_target_pairs={{0,3},{1,0},{2,1},{3,2},{4,7},{5,4},{6,5},{7,6},{8,11},{9,8},{10,9... | collective-permute-start | bytes 12296 | tf_op jit(solution)/shard_map/ppermute | solution.py:205
  7.2 4.5 %collective-permute-start.2 = (f32[8,128]{1,0:T(8,128)S(1)}, f32[8,128]{1,0:T(8,128)S(1)}, u32[]{:S(2)}, u32[]{:S(2)}) collective-permute-start(f32[8,128]{1,0:T(8,128)S(1)} %get-tuple-element.43.refs_3_), channel_id=1, source_target_pairs={{0,2},{1,3},{2,0},{3,1},{4,6},{5,7},{6,4},{7,5},{8,10},{9,11},{10,... | collective-permute-start | bytes 12296 | tf_op jit(solution)/shard_map/ppermute | solution.py:205
  7.2 5.4 %collective-permute-start.1 = (f32[8,128]{1,0:T(8,128)S(1)}, f32[8,128]{1,0:T(8,128)S(1)}, u32[]{:S(2)}, u32[]{:S(2)}) collective-permute-start(f32[8,128]{1,0:T(8,128)S(1)} %get-tuple-element.43.refs_3_), channel_id=1, source_target_pairs={{0,1},{1,2},{2,3},{3,0},{4,5},{5,6},{6,7},{7,4},{8,9},{9,10},{10,1... | collective-permute-start | bytes 12296 | tf_op jit(solution)/shard_map/ppermute | solution.py:205
  13.5 7.3 %collective-permute-start.7 = (f32[2,16,1024]{2,1,0:T(8,128)S(1)}, f32[2,16,1024]{2,1,0:T(8,128)S(1)}, u32[]{:S(2)}, u32[]{:S(2)}) collective-permute-start(f32[2,16,1024]{2,1,0:T(8,128)S(1)} %get-tuple-element.56), channel_id=1, source_target_pairs={{0,24},{4,28},{8,16},{12,20},{16,8},{20,12},{24,0},{28,4},{1,25},{... | collective-permute-start | bytes 393224 | tf_op jit(solution)/shard_map/ppermute | solution.py:60
  16.0 5.2 %collective-permute-start.8 = (f32[2,16,1024]{2,1,0:T(8,128)S(1)}, f32[2,16,1024]{2,1,0:T(8,128)S(1)}, u32[]{:S(2)}, u32[]{:S(2)}) collective-permute-start(f32[2,16,1024]{2,1,0:T(8,128)S(1)} %get-tuple-element.57), channel_id=1, source_target_pairs={{0,8},{4,20},{8,0},{12,28},{16,24},{20,4},{24,16},{28,12},{1,9},{5... | collective-permute-start | bytes 393224 | tf_op jit(solution)/shard_map/ppermute | solution.py:60
  16.5 5.3 %collective-permute-start.9 = (f32[2,16,1024]{2,1,0:T(8,128)S(1)}, f32[2,16,1024]{2,1,0:T(8,128)S(1)}, u32[]{:S(2)}, u32[]{:S(2)}) collective-permute-start(f32[2,16,1024]{2,1,0:T(8,128)S(1)} %get-tuple-element.58), channel_id=1, source_target_pairs={{0,16},{4,12},{8,24},{12,4},{16,0},{20,28},{24,8},{28,20},{1,17},{... | collective-permute-start | bytes 393224 | tf_op jit(solution)/shard_map/ppermute | solution.py:60
  19.6 5.9 %collective-permute-start = (f32[2,4,16,1024]{3,2,1,0:T(8,128)S(1)}, f32[2,4,16,1024]{3,2,1,0:T(8,128)S(1)}, u32[]{:S(2)}, u32[]{:S(2)}) collective-permute-start(f32[2,4,16,1024]{3,2,1,0:T(8,128)S(1)} %shard_map.68), channel_id=1, source_target_pairs={{0,4},{4,0},{8,12},{12,8},{16,20},{20,16},{24,28},{28,24},{1,5},{5... | collective-permute-start | bytes 1572872 | tf_op jit(solution)/shard_map/ppermute | solution.py:235
  21.9 3.6 %collective-permute-start.10 = (f32[4,2,16,1024]{3,2,1,0:T(8,128)S(1)}, f32[4,2,16,1024]{3,2,1,0:T(8,128)S(1)}, u32[]{:S(2)}, u32[]{:S(2)}) collective-permute-start(f32[4,2,16,1024]{3,2,1,0:T(8,128)S(1)} %shard_map.71.refs_6_), channel_id=1, source_target_pairs={{0,4},{4,0},{8,12},{12,8},{16,20},{20,16},{24,28},{28,24},{1,5},{5... | collective-permute-start | bytes 1572872 | tf_op jit(solution)/shard_map/ppermute | solution.py:247
  22.0 7.3 %collective-permute-start.4 = (f32[2,16,1024]{2,1,0:T(8,128)S(1)}, f32[2,16,1024]{2,1,0:T(8,128)S(1)}, u32[]{:S(2)}, u32[]{:S(2)}) collective-permute-start(f32[2,16,1024]{2,1,0:T(8,128)S(1)} %get-tuple-element.52), channel_id=1, source_target_pairs={{0,24},{4,28},{8,16},{12,20},{16,8},{20,12},{24,0},{28,4},{1,25},{... | collective-permute-start | bytes 393224 | tf_op jit(solution)/shard_map/ppermute | solution.py:60
  23.7 7.2 %collective-permute-start.5 = (f32[2,16,1024]{2,1,0:T(8,128)S(1)}, f32[2,16,1024]{2,1,0:T(8,128)S(1)}, u32[]{:S(2)}, u32[]{:S(2)}) collective-permute-start(f32[2,16,1024]{2,1,0:T(8,128)S(1)} %get-tuple-element.53), channel_id=1, source_target_pairs={{0,8},{4,20},{8,0},{12,28},{16,24},{20,4},{24,16},{28,12},{1,9},{5... | collective-permute-start | bytes 393224 | tf_op jit(solution)/shard_map/ppermute | solution.py:60
  24.3 7.3 %collective-permute-start.6 = (f32[2,16,1024]{2,1,0:T(8,128)S(1)}, f32[2,16,1024]{2,1,0:T(8,128)S(1)}, u32[]{:S(2)}, u32[]{:S(2)}) collective-permute-start(f32[2,16,1024]{2,1,0:T(8,128)S(1)} %get-tuple-element.54), channel_id=1, source_target_pairs={{0,16},{4,12},{8,24},{12,4},{16,0},{20,28},{24,8},{28,20},{1,17},{... | collective-permute-start | bytes 393224 | tf_op jit(solution)/shard_map/ppermute | solution.py:60
  31.6 3.6 %collective-permute-start.11 = (f32[4,2,16,1024]{3,2,1,0:T(8,128)S(1)}, f32[4,2,16,1024]{3,2,1,0:T(8,128)S(1)}, u32[]{:S(2)}, u32[]{:S(2)}) collective-permute-start(f32[4,2,16,1024]{3,2,1,0:T(8,128)S(1)} %shard_map.73.refs_6_), channel_id=1, source_target_pairs={{0,4},{4,0},{8,12},{12,8},{16,20},{20,16},{24,28},{28,24},{1,5},{5... | collective-permute-start | bytes 1572872 | tf_op jit(solution)/shard_map/ppermute | solution.py:247
  31.7 7.3 %collective-permute-start.15 = (f32[2,16,1024]{2,1,0:T(8,128)S(1)}, f32[2,16,1024]{2,1,0:T(8,128)S(1)}, u32[]{:S(2)}, u32[]{:S(2)}) collective-permute-start(f32[2,16,1024]{2,1,0:T(8,128)S(1)} %get-tuple-element.65), channel_id=1, source_target_pairs={{0,24},{4,28},{8,16},{12,20},{16,8},{20,12},{24,0},{28,4},{1,25},{... | collective-permute-start | bytes 393224 | tf_op jit(solution)/shard_map/ppermute | solution.py:60
  33.5 8.3 %collective-permute-start.16 = (f32[2,16,1024]{2,1,0:T(8,128)S(1)}, f32[2,16,1024]{2,1,0:T(8,128)S(1)}, u32[]{:S(2)}, u32[]{:S(2)}) collective-permute-start(f32[2,16,1024]{2,1,0:T(8,128)S(1)} %get-tuple-element.66), channel_id=1, source_target_pairs={{0,8},{4,20},{8,0},{12,28},{16,24},{20,4},{24,16},{28,12},{1,9},{5... | collective-permute-start | bytes 393224 | tf_op jit(solution)/shard_map/ppermute | solution.py:60
  34.0 7.8 %collective-permute-start.17 = (f32[2,16,1024]{2,1,0:T(8,128)S(1)}, f32[2,16,1024]{2,1,0:T(8,128)S(1)}, u32[]{:S(2)}, u32[]{:S(2)}) collective-permute-start(f32[2,16,1024]{2,1,0:T(8,128)S(1)} %get-tuple-element.67), channel_id=1, source_target_pairs={{0,16},{4,12},{8,24},{12,4},{16,0},{20,28},{24,8},{28,20},{1,17},{... | collective-permute-start | bytes 393224 | tf_op jit(solution)/shard_map/ppermute | solution.py:60
  36.1 8.6 %collective-permute-start.12 = (f32[2,16,1024]{2,1,0:T(8,128)S(1)}, f32[2,16,1024]{2,1,0:T(8,128)S(1)}, u32[]{:S(2)}, u32[]{:S(2)}) collective-permute-start(f32[2,16,1024]{2,1,0:T(8,128)S(1)} %get-tuple-element.61), channel_id=1, source_target_pairs={{0,24},{4,28},{8,16},{12,20},{16,8},{20,12},{24,0},{28,4},{1,25},{... | collective-permute-start | bytes 393224 | tf_op jit(solution)/shard_map/ppermute | solution.py:60
  37.8 8.5 %collective-permute-start.13 = (f32[2,16,1024]{2,1,0:T(8,128)S(1)}, f32[2,16,1024]{2,1,0:T(8,128)S(1)}, u32[]{:S(2)}, u32[]{:S(2)}) collective-permute-start(f32[2,16,1024]{2,1,0:T(8,128)S(1)} %get-tuple-element.62), channel_id=1, source_target_pairs={{0,8},{4,20},{8,0},{12,28},{16,24},{20,4},{24,16},{28,12},{1,9},{5... | collective-permute-start | bytes 393224 | tf_op jit(solution)/shard_map/ppermute | solution.py:60
  39.0 7.9 %collective-permute-start.14 = (f32[2,16,1024]{2,1,0:T(8,128)S(1)}, f32[2,16,1024]{2,1,0:T(8,128)S(1)}, u32[]{:S(2)}, u32[]{:S(2)}) collective-permute-start(f32[2,16,1024]{2,1,0:T(8,128)S(1)} %get-tuple-element.63), channel_id=1, source_target_pairs={{0,16},{4,12},{8,24},{12,4},{16,0},{20,28},{24,8},{28,20},{1,17},{... | collective-permute-start | bytes 393224 | tf_op jit(solution)/shard_map/ppermute | solution.py:60

commit v4 on v3

v4 whole, which is shorter than its diff:
```python
import jax
import jax.numpy as jnp
from jax import lax
from jax.experimental import pallas as pl
from jax.experimental.pallas import tpu as pltpu
from jax.sharding import PartitionSpec as P

LEVEL_MODULES = 16
LEVELS = 2
MOST_UNROLLED = 16

outer_rate = 0.7
beta_coef = 0.9
moment_coef = outer_rate * beta_coef * beta_coef
grad_coef = outer_rate * (1.0 + beta_coef)

VMEM_LIMIT = 16 * 1024 * 1024

vmem = pl.BlockSpec(memory_space=pltpu.VMEM)
smem = pl.BlockSpec(memory_space=pltpu.SMEM)
anywhere = pl.BlockSpec(memory_space=pl.ANY)


def call(kernel, out_shape, in_specs, out_specs, **more):
    return pl.pallas_call(
        kernel,
        out_shape=out_shape,
        in_specs=in_specs,
        out_specs=out_specs,
        compiler_params=pltpu.CompilerParams(vmem_limit_bytes=VMEM_LIMIT),
        **more,
    )


def mirrored(k, size):
    if size < 8:
        return k
    return (k & ~6) | ((k & 2) << 1) | ((k & 4) >> 1)


def target(here, k, size):
    if isinstance(here, int):
        return here ^ (mirrored(k, size) if here & 1 else k)
    return here ^ jnp.where(here & 1 == 1, mirrored(k, size), k)


def origin(here, k, size):
    if isinstance(here, int):
        return here ^ (mirrored(k, size) if (here ^ k) & 1 else k)
    return here ^ jnp.where((here ^ k) & 1 == 1, mirrored(k, size), k)


def order_of(size):
    return sorted(range(2, size, 2), key=lambda k: (-bin(k).count("1"), k)) + [0]


def move(array, k, size):
    if k == 0:
        return array
    return lax.ppermute(array, "path", [(i, target(i, k, size)) for i in range(size)])


def pack_kernel(size, here_ref, delta_ref, square_ref, give_ref, *outs):
    total = jnp.zeros(square_ref.shape, jnp.float32)
    order = order_of(size)
    here = here_ref[0]
    core = here & 1
    for level in range(LEVELS):
        for j, k in enumerate(order):
            chip = target(here, k, size) // 2
            kept = delta_ref[level, chip, core]
            given = delta_ref[level, chip, 1 - core]
            outs[level * len(order) + j][...] = kept
            give_ref[level, chip] = given
            block = kept * kept + given * given
            folded = block.reshape(-1, 8, block.shape[-1]).sum(axis=0)
            for lane in range(0, block.shape[-1], 128):
                total = total + folded[:, lane : lane + 128]
    square_ref[...] = total


def pair_kernel(here_ref, own_ref, other_ref, out_ref):
    core = here_ref[0] & 1
    out_ref[core] = own_ref[...]
    out_ref[1 - core] = other_ref[...]


def add_kernel(a_ref, b_ref, out_ref):
    out_ref[...] = a_ref[...] + b_ref[...]


def scale_kernel(entries, here_ref, ids_ref, plan_ref, squares_ref, other_ref, gift_ref, *refs):
    del plan_ref
    here = here_ref[0]
    count = len(refs) // 2
    rounds = count // LEVELS
    order = order_of(2 * rounds)
    for source in range(2):
        tile = squares_ref[source] + other_ref[source]
        total = jnp.broadcast_to(jnp.sum(tile, keepdims=True), (8, 128))
        rescale = 1.0 / jnp.sqrt(total / entries + 1e-06)
        path = (here // 2) * 2 + source
        for level in range(LEVELS):
            own = ids_ref[path, level]
            sharers = jnp.int32(0)
            for other in range(ids_ref.shape[0]):
                sharers = sharers + jnp.where(ids_ref[other, level] == own, 1, 0)
            factor = rescale / jnp.full((8, 128), sharers, jnp.int32).astype(jnp.float32)

            def scale(own_rows, level=level, source=source, factor=factor):
                for j, k in enumerate(order):
                    out = refs[count + level * rounds + j]
                    chip = target(here, k, 2 * rounds) // 2
                    _, rows, width = out.shape
                    for row in range(0, rows, 8):
                        for lane in range(0, width, 128):
                            at = (slice(row, row + 8), slice(lane, lane + 128))
                            if own_rows:
                                block = refs[level * rounds + j][at]
                            else:
                                block = gift_ref[(level, chip, *at)]
                            out[(source, *at)] = block * factor

            pl.when(here & 1 == source)(lambda scale=scale: scale(True))
            pl.when(here & 1 != source)(lambda scale=scale: scale(False))


def plan_kernel(here_ref, ids_ref, chosen_ref, sender_ref, receiver_ref, module_ref):
    size = ids_ref.shape[0]
    order = order_of(size)
    here = here_ref[0]
    for level in range(LEVELS):
        first = level * LEVEL_MODULES
        for module in range(LEVEL_MODULES):
            module_ref[first + module] = -1
        sources = [ids_ref[(origin(here, k, size) // 2) * 2 + half, level] + first for k in order for half in range(2)]
        for i in reversed(range(size)):
            module_ref[sources[i]] = i
        for i in range(size):
            sender_ref[level, i] = module_ref[sources[i]]
        for j, k in enumerate(order):
            for half in range(2):
                module = ids_ref[(target(here, k, size) // 2) * 2 + half, level] + first
                chosen_ref[level, 2 * j + half] = module
                receiver_ref[level, 2 * j + half] = module_ref[module]


def outgoing_kernel(level, rounds, chosen_ref, sender_ref, receiver_ref, decayed_ref, *refs):
    received, outs, grad_ref = refs[:rounds], refs[rounds:-1], refs[-1]
    for i in range(2 * rounds):
        grad_ref[i] = received[i // 2][i % 2]
    for i in range(1, 2 * rounds):
        leader = sender_ref[level, i]

        @pl.when(leader != i)
        def _():
            grad_ref[leader] += grad_ref[i]

    for i in range(2 * rounds):
        decayed = decayed_ref[chosen_ref[level, i]]
        outs[i // 2][i % 2] = decayed - grad_coef * grad_ref[receiver_ref[level, i]]


def state_kernel(level, module_ref, grad_ref, decayed_ref, momentum_ref, *outs):
    new_params_ref, new_momentum_ref = outs[-2:]
    count = new_params_ref.shape[0]
    first = level * LEVEL_MODULES + pl.program_id(0) * count
    for place in range(count):
        module = first + place
        leader = module_ref[module]
        taken = jnp.where(leader < 0, 0.0, 1.0)
        grad = taken * grad_ref[jnp.maximum(leader, 0)]
        new_momentum_ref[place] = beta_coef * momentum_ref[module] + grad
        new_params_ref[place] = decayed_ref[module] - grad_coef * grad


def give_back_kernel(size, here_ref, *refs):
    here = here_ref[0]
    for j, k in enumerate(order_of(size)):
        refs[-1][origin(here, k, size) // 2] = refs[j][1 - (here & 1)]


def assemble_kernel(size, level, here_ref, *refs):
    order = order_of(size)
    here = here_ref[0]
    core = here & 1
    out_ref, sems = refs[-2:]
    copies = []
    for j, k in enumerate(order):
        chip = origin(here, k, size) // 2
        copies.append(pltpu.make_async_copy(refs[j].at[core], out_ref.at[level, chip, core], sems.at[0, j]))
        copies.append(pltpu.make_async_copy(refs[len(order)].at[j], out_ref.at[level, j, 1 - core], sems.at[1, j]))
    for copy in copies:
        copy.start()
    for copy in copies:
        copy.wait()


def local(path_delta, assign, params, momentum):
    own_slab = path_delta[0]
    size = assign.shape[0]
    module_count, _, own_rows, width = params.shape
    shards = lax.axis_size("shard")
    entries = float(own_slab.size * shards)
    state_in = params.reshape(module_count, own_rows, width)
    moment_in = momentum.reshape(module_count, own_rows, width)
    split_slab = own_slab.reshape(LEVELS, size // 2, 2, own_rows, width)
    here = lax.axis_index("path").astype(jnp.int32).reshape(1)
    order = order_of(size)
    rounds = len(order)
    swap = [(i, i ^ 1) for i in range(size)]
    rows = jax.ShapeDtypeStruct((own_rows, width), jnp.float32)
    both = jax.ShapeDtypeStruct((2, own_rows, width), jnp.float32)
    by_chip = jax.ShapeDtypeStruct((rounds, own_rows, width), jnp.float32)
    by_path = jax.ShapeDtypeStruct((size, own_rows, width), jnp.float32)
    tile = jax.ShapeDtypeStruct((8, 128), jnp.float32)
    tiles = jax.ShapeDtypeStruct((2, 8, 128), jnp.float32)
    places = jax.ShapeDtypeStruct((LEVELS, size), jnp.int32)

    squares, give, *kept = call(
        lambda *refs: pack_kernel(size, *refs),
        [tile, jax.ShapeDtypeStruct((LEVELS, *by_chip.shape), jnp.float32)] + [rows] * (LEVELS * rounds),
        [smem, vmem],
        [vmem] * (2 + LEVELS * rounds),
    )(here, split_slab)
    other = lax.ppermute(squares, "path", swap)
    gift = lax.ppermute(give, "path", swap)
    squares = call(pair_kernel, tiles, [smem, vmem, vmem], vmem)(here, squares, other)
    other = jnp.zeros_like(squares)
    step = 1
    while step < shards:
        if step > 1:
            squares = call(add_kernel, tiles, [vmem, vmem], vmem)(squares, other)
        other = lax.ppermute(squares, "shard", [(i, i ^ step) for i in range(shards)])
        step *= 2
    chosen, sender, receiver, leaders = call(
        plan_kernel,
        [places, places, places, jax.ShapeDtypeStruct((module_count,), jnp.int32)],
        [smem, smem],
        [smem] * 4,
    )(here, assign)
    scaled = call(
        lambda *refs: scale_kernel(entries, *refs),
        [both] * (LEVELS * rounds),
        [smem, smem, smem] + [vmem] * (3 + LEVELS * rounds),
        [vmem] * (LEVELS * rounds),
    )(here, assign, chosen, squares, other, gift, *kept)
    decayed = state_in - moment_coef * moment_in

    path_params, new_state, new_moment = None, None, None
    block = LEVEL_MODULES // 2
    steps = LEVEL_MODULES // block
    for level in range(LEVELS):
        received = [move(scaled[level * rounds + j], k, size) for j, k in enumerate(order)]
        *outgoing, grad = call(
            lambda *refs, level=level: outgoing_kernel(level, rounds, *refs),
            [both] * rounds + [by_path],
            [smem] * 3 + [vmem] * (1 + rounds),
            [vmem] * (rounds + 1),
        )(chosen, sender, receiver, decayed, *received)
        returned = [move(outgoing[j], k, size) for j, k in enumerate(order)]
        held = [] if level == 0 else [new_state, new_moment]
        state_block = pl.BlockSpec((block, own_rows, width), lambda i, level=level: (i + level * steps, 0, 0))
        new_state, new_moment = call(
            lambda *refs, level=level: state_kernel(level, *refs),
            [jax.ShapeDtypeStruct(state_in.shape, jnp.float32)] * 2,
            [smem, vmem, vmem, vmem] + [anywhere] * len(held),
            [state_block, state_block],
            grid=(steps,),
            input_output_aliases={4: 0, 5: 1} if held else {},
        )(leaders, grad, decayed, moment_in, *held)
        before = [new_state] if level == LEVELS - 1 else []
        back = call(
            lambda *refs: give_back_kernel(size, *refs),
            by_chip,
            [smem] + [vmem] * rounds + [anywhere] * len(before),
            vmem,
        )(here, *returned, *before)
        back = lax.ppermute(back, "path", swap)
        held = [] if level == 0 else [path_params]
        path_params = call(
            lambda *refs, level=level: assemble_kernel(size, level, *refs),
            jax.ShapeDtypeStruct(split_slab.shape, jnp.float32),
            [smem] + [anywhere] * (rounds + 1 + len(held)),
            anywhere,
            scratch_shapes=[pltpu.SemaphoreType.DMA((2, rounds))],
            input_output_aliases={2 + rounds: 0} if held else {},
        )(here, *returned, back, *held)
    return (path_params.reshape(path_delta.shape), new_state[:, None], new_moment[:, None])


def local_wide(path_delta, assign, params, momentum):
    own_slab = path_delta[0]
    path_count = assign.shape[0]
    module_count, _, own_rows, width = params.shape
    entries = float(own_slab.size * lax.axis_size("shard"))
    total_sq = lax.psum(jnp.sum(own_slab * own_slab), "shard")
    scaled = own_slab * (1.0 / jnp.sqrt(total_sq / entries + 1e-06))
    received = lax.all_to_all(
        scaled.reshape(LEVELS, path_count, own_rows, width), "path", split_axis=1, concat_axis=1, tiled=True
    )
    flat_ids = (assign + LEVEL_MODULES * jnp.arange(LEVELS, dtype=jnp.int32)[None, :]).T.reshape(-1)
    member = (jnp.arange(module_count, dtype=jnp.int32)[:, None] == flat_ids[None, :]).astype(jnp.float32)
    mean = member / jnp.maximum(jnp.sum(member, axis=1), 1.0)[:, None]
    grad = jnp.einsum(
        "mp,prd->mrd", mean, received.reshape(-1, own_rows, width), precision=lax.Precision.HIGHEST
    )
    new_moment = beta_coef * momentum[:, 0] + grad
    new_state = params[:, 0] - outer_rate * (grad + beta_coef * new_moment)
    outgoing = jnp.take(new_state, flat_ids, axis=0).reshape(LEVELS, path_count, own_rows, width)
    returned = lax.all_to_all(outgoing, "path", split_axis=1, concat_axis=1, tiled=True)
    return (returned.reshape(path_delta.shape), new_state[:, None], new_moment[:, None])


def solution(mesh):
    in_specs = (
        P("path", None, "shard", None),
        P(),
        P(None, "shard", "path", None),
        P(None, "shard", "path", None),
    )
    out_specs = (
        P("path", None, "shard", None),
        P(None, "shard", "path", None),
        P(None, "shard", "path", None),
    )
    chosen = local if 4 <= mesh.shape["path"] <= MOST_UNROLLED else local_wide
    return jax.shard_map(chosen, mesh=mesh, in_specs=in_specs, out_specs=out_specs, check_vma=False)
```

time: 47.9 us -> 46 us (0.960)
  waiting for transfers between devices: 12.6 us -> 6.56 us
  starting transfers between devices: 20.2 us -> 22.2 us
  local copies, waits for them, and re-layouts: 2.12 us -> 3.71 us
    ppermute x12, waiting for transfers between devices: 10.2 us -> 3.23 us  [move(): lax.ppermute(array, 'path', [(i, target(i, k, size)) for i in range(size)])]
    unnamed x5 -> x7, local copies, waits for them, and re-layouts: 2.12 us -> 3.71 us
    ppermute x12, starting transfers between devices: 13.8 us -> 15.3 us  [move(): lax.ppermute(array, 'path', [(i, target(i, k, size)) for i in range(size)])]
    ppermute x6, waiting for transfers between devices: 2.31 us -> 3.33 us  [the longest x2 1.62 us: local(): lax.ppermute(squares, 'shard', [(i, i ^ step) for i in range(shards)])]
    ppermute x6, starting transfers between devices: 6.34 us -> 6.84 us  [the longest x2 5.72 us: local(): lax.ppermute(squares, 'shard', [(i, i ^ step) for i in range(shards)])]
    pallas_call x8 -> x9, Pallas kernels: 4.56 us -> 4.9 us  [the longest x2 1.54 us: local(): call(lambda *refs, level=level: outgoing_kernel(level, rounds, *refs), [b...]
  transfers between devices with their start and end apart: 18 -> 18, of which waited for: 12 -> 5; matrix products, arithmetic and copies ran while one was open for 6% -> 6% of each run, Pallas kernels for 18% -> 17%
where the time goes in v4:
time: 46 us; the launch traced here: 45.8 us
  starting transfers between devices  22.2 us (48%)
  Pallas kernels  10.6 us (23%)
  waiting for transfers between devices  6.56 us (14%)
  local copies, waits for them, and re-layouts  3.71 us (8%)
  other arithmetic  2.03 us (4%)
  between operations  0.77 us (2%)
    ppermute x12, starting transfers between devices, move(): lax.ppermute(array, 'path', [(i, target(i, k, size)) for i in range(size)])  15.3 us
    ppermute x2, starting transfers between devices, local(): lax.ppermute(squares, 'shard', [(i, i ^ step) for i in range(shards)])  5.72 us
    pallas_call x2, Pallas kernels, local(): call(lambda *refs, level=level: state_kernel(level, *refs), [jax.ShapeDty...  3.99 us
    unnamed x7, local copies, waits for them, and re-layouts  3.71 us
    ppermute x12, waiting for transfers between devices, move(): lax.ppermute(array, 'path', [(i, target(i, k, size)) for i in range(size)])  3.23 us
    sub x1, other arithmetic, local(): decayed = state_in - moment_coef * moment_in  2.03 us
    pallas_call x2, Pallas kernels, local(): call(lambda *refs, level=level: assemble_kernel(size, level, *refs), jax....  1.69 us
    ppermute x2, waiting for transfers between devices, local(): lax.ppermute(squares, 'shard', [(i, i ^ step) for i in range(shards)])  1.62 us
  transfers between devices with their start and end apart: 18, of which 5 were waited for; matrix products, arithmetic and copies ran while one was open for 6% of the time, Pallas kernels for 17%

profile of v4, /device:TPU:0, one launch (start us, length us, event | category | flops | bytes accessed | tf_op | source)
XLA Modules:
  0.0 45.8 jit_solution(17075107620728100053)
XLA Ops:
  0.7 1.4 %copy-done.2 = f32[1,2,128,1024]{3,2,1,0:T(8,128)S(1)} copy-done((f32[1,2,128,1024]{3,2,1,0:T(8,128)S(1)}, f32[1,2,128,1024]{3,2,1,0:T(8,128)}, u32[]{:S(2)}) %copy-start.2) | copy-done | bytes 1048600
  2.0 0.9 %shard_map.68 = (f32[8,128]{1,0:T(8,128)S(1)}, f32[2,4,16,1024]{3,2,1,0:T(8,128)}, f32[16,1024]{1,0:T(8,128)S(1)}, f32[16,1024]{1,0:T(8,128)S(1)}, f32[16,1024]{...) custom-call(s32[1]{0:T(128)} %bitcast.here_ref.refs_0_, ...), custom_call_target="tpu_custom_call" | custom-call | tf_op jit(solution)/shard_map/pallas_call | solution.py:220
  2.9 0.5 collective-permute-start.3
  3.4 0.1 collective-permute-start
  3.4 1.4 %collective-permute-done.other_ref = f32[8,128]{1,0:T(8,128)S(1)} collective-permute-done((f32[8,128]{1,0:T(8,128)S(1)}, f32[8,128]{1,0:T(8,128)S(1)}, u32[]{:S(2)}, u32[]{:S(2)}) %collective-permute-start) | collective-permute-done | bytes 4128 | tf_op jit(solution)/shard_map/ppermute | solution.py:226
  4.8 2.7 %collective-permute-start.1 = (f32[2,8,128]{2,1,0:T(8,128)S(1)}, f32[2,8,128]{2,1,0:T(8,128)S(1)}, u32[]{:S(2)}, u32[]{:S(2)}) collective-permute-start(f32[2,8,128]{2,1,0:T(8,128)S(1)} %shard_map.69.a_ref), channel_id=1, source_target_pairs={{0,1},{1,0},{2,3},{3,2},{4,5},{5,4},{6,7},{7,6},{8,9},{9,8},{10,11... | collective-permute-start | bytes 24584 | tf_op jit(solution)/shard_map/ppermute | solution.py:234
  7.5 1.6 %collective-permute-done.1.b_ref = f32[2,8,128]{2,1,0:T(8,128)S(1)} collective-permute-done((f32[2,8,128]{2,1,0:T(8,128)S(1)}, f32[2,8,128]{2,1,0:T(8,128)S(1)}, u32[]{:S(2)}, u32[]{:S(2)}) %collective-permute-start.1) | collective-permute-done | bytes 8224 | tf_op jit(solution)/shard_map/ppermute | solution.py:234
  9.1 3.0 %collective-permute-start.2 = (f32[2,8,128]{2,1,0:T(8,128)S(1)}, f32[2,8,128]{2,1,0:T(8,128)S(1)}, u32[]{:S(2)}, u32[]{:S(2)}) collective-permute-start(f32[2,8,128]{2,1,0:T(8,128)S(1)} %shard_map.70.refs_3_), channel_id=1, source_target_pairs={{0,2},{1,3},{2,0},{3,1},{4,6},{5,7},{6,4},{7,5},{8,10},{9,11},{10,... | collective-permute-start | bytes 24584 | tf_op jit(solution)/shard_map/ppermute | solution.py:234
  12.2 0.8 %copy.10.ids_ref.refs_1_ = s32[8,2]{1,0:T(8,128)S(1)} copy(s32[8,2]{0,1:T(2,128)} %param.5) | data formatting | bytes 128 | tf_op args[1]
  12.9 1.3 %shard_map.67 = (s32[2,8]{1,0:T(2,128)S(1)}, s32[2,8]{1,0:T(2,128)S(1)}, s32[2,8]{1,0:T(2,128)S(1)}, s32[32]{0:T(128)S(1)}) custom-call(s32[1]{0:T(128)} %bitcast.here_ref.refs_0_, s32[8,2]{1,0:T(8,128)S(1)} %copy.10.ids_ref.refs_1_), custom_call_target="tpu_custom_call" | custom-call | tf_op jit(solution)/shard_map/pallas_call | solution.py:236
  14.3 0.0 collective-permute-done.2.refs_4_
  14.3 0.0 collective-permute-done.3.refs_5_
  14.3 1.0 %shard_map.71 = (f32[2,16,1024]{2,1,0:T(8,128)S(1)}, f32[2,16,1024]{2,1,0:T(8,128)S(1)}, f32[2,16,1024]{2,1,0:T(8,128)S(1)}, f32[2,16,1024]{2,1,0:T(8,128)S(1)},...) custom-call(s32[1]{0:T(128)} %bitcast.here_ref.refs_0_, ...), custom_call_target="tpu_custom_call" | custom-call | tf_op jit(solution)/shard_map/pallas_call | solution.py:242
  15.4 2.5 %collective-permute-start.10 = (f32[2,16,1024]{2,1,0:T(8,128)S(1)}, f32[2,16,1024]{2,1,0:T(8,128)S(1)}, u32[]{:S(2)}, u32[]{:S(2)}) collective-permute-start(f32[2,16,1024]{2,1,0:T(8,128)S(1)} %get-tuple-element.62), channel_id=1, source_target_pairs={{0,24},{4,28},{8,16},{12,20},{16,8},{20,12},{24,0},{28,4},{1,25},{... | collective-permute-start | bytes 393224 | tf_op jit(solution)/shard_map/ppermute | solution.py:60
  17.9 0.5 %collective-permute-start.11 = (f32[2,16,1024]{2,1,0:T(8,128)S(1)}, f32[2,16,1024]{2,1,0:T(8,128)S(1)}, u32[]{:S(2)}, u32[]{:S(2)}) collective-permute-start(f32[2,16,1024]{2,1,0:T(8,128)S(1)} %get-tuple-element.63), channel_id=1, source_target_pairs={{0,8},{4,20},{8,0},{12,28},{16,24},{20,4},{24,16},{28,12},{1,9},{5... | collective-permute-start | bytes 393224 | tf_op jit(solution)/shard_map/ppermute | solution.py:60
  18.4 0.5 %collective-permute-start.12 = (f32[2,16,1024]{2,1,0:T(8,128)S(1)}, f32[2,16,1024]{2,1,0:T(8,128)S(1)}, u32[]{:S(2)}, u32[]{:S(2)}) collective-permute-start(f32[2,16,1024]{2,1,0:T(8,128)S(1)} %get-tuple-element.64), channel_id=1, source_target_pairs={{0,16},{4,12},{8,24},{12,4},{16,0},{20,28},{24,8},{28,20},{1,17},{... | collective-permute-start | bytes 393224 | tf_op jit(solution)/shard_map/ppermute | solution.py:60
  18.9 2.0 %bitcast_subtract_fusion.refs_3_.refs_2_ = f32[32,16,1024]{2,1,0:T(8,128)S(1)} fusion(f32[32,1,16,1024]{3,2,1,0:T(8,128)} %param.6, f32[32,1,16,1024]{3,2,1,0:T(8,128)S(1)} %copy-done), kind=kLoop, calls=%fused_computation | loop fusion | flops 1048576 | bytes 6291456 | tf_op jit(solution)/shard_map/sub | solution.py:248
  20.9 2.5 %collective-permute-start.4 = (f32[2,16,1024]{2,1,0:T(8,128)S(1)}, f32[2,16,1024]{2,1,0:T(8,128)S(1)}, u32[]{:S(2)}, u32[]{:S(2)}) collective-permute-start(f32[2,16,1024]{2,1,0:T(8,128)S(1)} %get-tuple-element.52), channel_id=1, source_target_pairs={{0,24},{4,28},{8,16},{12,20},{16,8},{20,12},{24,0},{28,4},{1,25},{... | collective-permute-start | bytes 393224 | tf_op jit(solution)/shard_map/ppermute | solution.py:60
  23.5 0.5 %collective-permute-start.5 = (f32[2,16,1024]{2,1,0:T(8,128)S(1)}, f32[2,16,1024]{2,1,0:T(8,128)S(1)}, u32[]{:S(2)}, u32[]{:S(2)}) collective-permute-start(f32[2,16,1024]{2,1,0:T(8,128)S(1)} %get-tuple-element.53), channel_id=1, source_target_pairs={{0,8},{4,20},{8,0},{12,28},{16,24},{20,4},{24,16},{28,12},{1,9},{5... | collective-permute-start | bytes 393224 | tf_op jit(solution)/shard_map/ppermute | solution.py:60
  24.0 0.0 collective-permute-done.10.refs_4_
  24.0 0.5 %collective-permute-start.6 = (f32[2,16,1024]{2,1,0:T(8,128)S(1)}, f32[2,16,1024]{2,1,0:T(8,128)S(1)}, u32[]{:S(2)}, u32[]{:S(2)}) collective-permute-start(f32[2,16,1024]{2,1,0:T(8,128)S(1)} %get-tuple-element.54), channel_id=1, source_target_pairs={{0,16},{4,12},{8,24},{12,4},{16,0},{20,28},{24,8},{28,20},{1,17},{... | collective-permute-start | bytes 393224 | tf_op jit(solution)/shard_map/ppermute | solution.py:60
  24.5 0.0 collective-permute-done.11.refs_5_
  24.5 0.0 collective-permute-done.12.refs_6_
  24.5 0.8 %shard_map.73 = (f32[2,16,1024]{2,1,0:T(8,128)S(1)}, f32[2,16,1024]{2,1,0:T(8,128)S(1)}, f32[2,16,1024]{2,1,0:T(8,128)S(1)}, f32[2,16,1024]{2,1,0:T(8,128)S(1)}, f32[8,16,1024]{2,1,0:T(8,128)S(1)}) custom-call(s32[2,8]{1,0:T(2,128)S(1)} %get-tuple-element.39.refs_2_.refs_0_, s32[2,8]{1,0:T(2,128)S(1)} %get-tuple-element.40.refs_1_, ...), custom_call_target="tpu_custom_call" | custom-call | tf_op jit(solution)/shard_map/pallas_call | solution.py:255
  25.3 3.9 %collective-permute-start.14 = (f32[2,16,1024]{2,1,0:T(8,128)S(1)}, f32[2,16,1024]{2,1,0:T(8,128)S(1)}, u32[]{:S(2)}, u32[]{:S(2)}) collective-permute-start(f32[2,16,1024]{2,1,0:T(8,128)S(1)} %get-tuple-element.70), channel_id=1, source_target_pairs={{0,24},{4,28},{8,16},{12,20},{16,8},{20,12},{24,0},{28,4},{1,25},{... | collective-permute-start | bytes 393224 | tf_op jit(solution)/shard_map/ppermute | solution.py:60
  29.2 0.1 collective-permute-start.15
  29.3 0.0 collective-permute-done.4.refs_4_
  29.3 0.6 %collective-permute-start.16 = (f32[2,16,1024]{2,1,0:T(8,128)S(1)}, f32[2,16,1024]{2,1,0:T(8,128)S(1)}, u32[]{:S(2)}, u32[]{:S(2)}) collective-permute-start(f32[2,16,1024]{2,1,0:T(8,128)S(1)} %get-tuple-element.72), channel_id=1, source_target_pairs={{0,16},{4,12},{8,24},{12,4},{16,0},{20,28},{24,8},{28,20},{1,17},{... | collective-permute-start | bytes 393224 | tf_op jit(solution)/shard_map/ppermute | solution.py:60
  30.0 1.3 %collective-permute-done.5.refs_5_ = f32[2,16,1024]{2,1,0:T(8,128)S(1)} collective-permute-done((f32[2,16,1024]{2,1,0:T(8,128)S(1)}, f32[2,16,1024]{2,1,0:T(8,128)S(1)}, u32[]{:S(2)}, u32[]{:S(2)}) %collective-permute-start.5) | collective-permute-done | bytes 131104 | tf_op jit(solution)/shard_map/ppermute | solution.py:60
  31.3 1.9 %collective-permute-done.6.refs_6_ = f32[2,16,1024]{2,1,0:T(8,128)S(1)} collective-permute-done((f32[2,16,1024]{2,1,0:T(8,128)S(1)}, f32[2,16,1024]{2,1,0:T(8,128)S(1)}, u32[]{:S(2)}, u32[]{:S(2)}) %collective-permute-start.6) | collective-permute-done | bytes 131104 | tf_op jit(solution)/shard_map/ppermute | solution.py:60
  33.2 0.8 %shard_map.72 = (f32[2,16,1024]{2,1,0:T(8,128)S(1)}, f32[2,16,1024]{2,1,0:T(8,128)S(1)}, f32[2,16,1024]{2,1,0:T(8,128)S(1)}, f32[2,16,1024]{2,1,0:T(8,128)S(1)}, f32[8,16,1024]{2,1,0:T(8,128)S(1)}) custom-call(s32[2,8]{1,0:T(2,128)S(1)} %get-tuple-element.39.refs_2_.refs_0_, s32[2,8]{1,0:T(2,128)S(1)} %get-tuple-element.40.refs_1_, ...), custom_call_target="tpu_custom_call" | custom-call | tf_op jit(solution)/shard_map/pallas_call | solution.py:255
  33.9 1.4 %collective-permute-start.7 = (f32[2,16,1024]{2,1,0:T(8,128)S(1)}, f32[2,16,1024]{2,1,0:T(8,128)S(1)}, u32[]{:S(2)}, u32[]{:S(2)}) collective-permute-start(f32[2,16,1024]{2,1,0:T(8,128)S(1)} %get-tuple-element.56), channel_id=1, source_target_pairs={{0,24},{4,28},{8,16},{12,20},{16,8},{20,12},{24,0},{28,4},{1,25},{... | collective-permute-start | bytes 393224 | tf_op jit(solution)/shard_map/ppermute | solution.py:60
  35.4 0.7 %collective-permute-start.8 = (f32[2,16,1024]{2,1,0:T(8,128)S(1)}, f32[2,16,1024]{2,1,0:T(8,128)S(1)}, u32[]{:S(2)}, u32[]{:S(2)}) collective-permute-start(f32[2,16,1024]{2,1,0:T(8,128)S(1)} %get-tuple-element.57), channel_id=1, source_target_pairs={{0,8},{4,20},{8,0},{12,28},{16,24},{20,4},{24,16},{28,12},{1,9},{5... | collective-permute-start | bytes 393224 | tf_op jit(solution)/shard_map/ppermute | solution.py:60
  36.0 0.0 collective-permute-done.14.refs_1_
  36.1 1.4 %collective-permute-start.9 = (f32[2,16,1024]{2,1,0:T(8,128)S(1)}, f32[2,16,1024]{2,1,0:T(8,128)S(1)}, u32[]{:S(2)}, u32[]{:S(2)}) collective-permute-start(f32[2,16,1024]{2,1,0:T(8,128)S(1)} %get-tuple-element.58), channel_id=1, source_target_pairs={{0,16},{4,12},{8,24},{12,4},{16,0},{20,28},{24,8},{28,20},{1,17},{... | collective-permute-start | bytes 393224 | tf_op jit(solution)/shard_map/ppermute | solution.py:60
  37.5 2.0 %shard_map.74 = (f32[32,16,1024]{2,1,0:T(8,128)}, f32[32,16,1024]{2,1,0:T(8,128)}) custom-call(s32[32]{0:T(128)S(1)} %get-tuple-element.60.refs_0_, f32[8,16,1024]{2,1,0:T(8,128)S(1)} %get-tuple-element.66.refs_1_, f32[32,16,1024]{2,1,0:T(8,128)S(1)} %bitcast_subtract_fusion.refs_3_.refs_2_, f32[32,16,1024]{2,1,0:T(8,128)S(1)} %bitcast.13), custom_call_target="tpu_custom_call" | custom-call | tf_op jit(solution)/shard_map/pallas_call | solution.py:264
  39.5 2.0 %shard_map.75 = (f32[32,16,1024]{2,1,0:T(8,128)}, f32[32,16,1024]{2,1,0:T(8,128)}) custom-call(s32[32]{0:T(128)S(1)} %get-tuple-element.60.refs_0_, f32[8,16,1024]{2,1,0:T(8,128)S(1)} %get-tuple-element.61.refs_1_, f32[32,16,1024]{2,1,0:T(8,128)S(1)} %bitcast_subtract_fusion.refs_3_.refs_2_, ...), custom_call_target="tpu_custom_call", output_to_operand_aliasing={{0}: (4, {}), {1}: (5, {})} | custom-call | tf_op jit(solution)/shard_map/pallas_call | solution.py:264
  41.5 0.0 collective-permute-done.15.refs_2_
  41.5 0.0 collective-permute-done.16.refs_3_
  41.5 0.1 collective-permute-start.17
  41.6 0.0 collective-permute-done.7.refs_1_
  41.6 0.0 collective-permute-done.9.refs_3_
  41.6 0.0 copy-start.1
  41.7 1.6 %copy-done.1 = f32[32,16,1024]{2,1,0:T(8,128)S(1)} copy-done((f32[32,16,1024]{2,1,0:T(8,128)S(1)}, f32[32,16,1024]{2,1,0:T(8,128)}, u32[]{:S(2)}) %copy-start.1) | copy-done | bytes 2097176
  43.3 0.5 %collective-permute-start.13 = (f32[4,16,1024]{2,1,0:T(8,128)S(1)}, f32[4,16,1024]{2,1,0:T(8,128)S(1)}, u32[]{:S(2)}, u32[]{:S(2)}) collective-permute-start(f32[4,16,1024]{2,1,0:T(8,128)S(1)} %shard_map.76), channel_id=1, source_target_pairs={{0,4},{4,0},{8,12},{12,8},{16,20},{20,16},{24,28},{28,24},{1,5},{5... | collective-permute-start | bytes 786440 | tf_op jit(solution)/shard_map/ppermute | solution.py:279
  43.8 0.8 %shard_map.78.refs_6_ = f32[2,4,2,16,1024]{4,3,2,1,0:T(8,128)} custom-call(s32[1]{0:T(128)} %bitcast.here_ref.refs_0_, f32[2,16,1024]{2,1,0:T(8,128)S(1)} %collective-permute-done.14.refs_1_, f32[2,16,1024]{2,1,0:T(8,128)S(1)} %collective-permute-done.15.refs_2_, f32[2,16,1024]{2,1,0:T(8,128)S(1)} %collective-permute-done.16.refs_3_, ...), custom_call_target="tpu_custom_call" | custom-call | tf_op jit(solution)/shard_map/pallas_call | solution.py:281
  44.7 0.3 collective-permute-done.13.refs_5_
  45.0 0.8 %shard_map.79 = f32[2,4,2,16,1024]{4,3,2,1,0:T(8,128)} custom-call(s32[1]{0:T(128)} %bitcast.here_ref.refs_0_, f32[2,16,1024]{2,1,0:T(8,128)S(1)} %collective-permute-done.7.refs_1_, f32[2,16,1024]{2,1,0:T(8,128)S(1)} %collective-permute-done.8.refs_2_, f32[2,16,1024]{2,1,0:T(8,128)S(1)} %collective-permute-done.9.refs_3_, ...), custom_call_target="tpu_custom_call", output_to_operand_aliasing={{}: (6, {})} | custom-call | tf_op jit(solution)/shard_map/pallas_call | solution.py:281
  (9 shorter events, 0.1 us)
Async XLA Ops:
  0.6 18.3 %copy-start = (f32[32,1,16,1024]{3,2,1,0:T(8,128)S(1)}, f32[32,1,16,1024]{3,2,1,0:T(8,128)}, u32[]{:S(2)}) copy-start(f32[32,1,16,1024]{3,2,1,0:T(8,128)} %param.7) | copy-start | bytes 6291460
  0.6 1.4 %copy-start.2 = (f32[1,2,128,1024]{3,2,1,0:T(8,128)S(1)}, f32[1,2,128,1024]{3,2,1,0:T(8,128)}, u32[]{:S(2)}) copy-start(f32[1,2,128,1024]{3,2,1,0:T(8,128)} %param.4) | copy-start | bytes 3145732
  2.9 11.4 %collective-permute-start.3 = (f32[2,4,16,1024]{3,2,1,0:T(8,128)}, f32[2,4,16,1024]{3,2,1,0:T(8,128)S(1)}, u32[]{:S(2)}, u32[]{:S(2)}) collective-permute-start(f32[2,4,16,1024]{3,2,1,0:T(8,128)} %get-tuple-element.43), channel_id=1, source_target_pairs={{0,4},{4,0},{8,12},{12,8},{16,20},{20,16},{24,28},{28,24},{1,5},{5... | collective-permute-start | bytes 1572872 | tf_op jit(solution)/shard_map/ppermute | solution.py:227
  3.4 1.5 %collective-permute-start = (f32[8,128]{1,0:T(8,128)S(1)}, f32[8,128]{1,0:T(8,128)S(1)}, u32[]{:S(2)}, u32[]{:S(2)}) collective-permute-start(f32[8,128]{1,0:T(8,128)S(1)} %get-tuple-element.42.own_ref), channel_id=1, source_target_pairs={{0,4},{4,0},{8,12},{12,8},{16,20},{20,16},{24,28},{28,24},{1,5},{5... | collective-permute-start | bytes 12296 | tf_op jit(solution)/shard_map/ppermute | solution.py:226
  4.8 4.3 %collective-permute-start.1 = (f32[2,8,128]{2,1,0:T(8,128)S(1)}, f32[2,8,128]{2,1,0:T(8,128)S(1)}, u32[]{:S(2)}, u32[]{:S(2)}) collective-permute-start(f32[2,8,128]{2,1,0:T(8,128)S(1)} %shard_map.69.a_ref), channel_id=1, source_target_pairs={{0,1},{1,0},{2,3},{3,2},{4,5},{5,4},{6,7},{7,6},{8,9},{9,8},{10,11... | collective-permute-start | bytes 24584 | tf_op jit(solution)/shard_map/ppermute | solution.py:234
  9.1 5.2 %collective-permute-start.2 = (f32[2,8,128]{2,1,0:T(8,128)S(1)}, f32[2,8,128]{2,1,0:T(8,128)S(1)}, u32[]{:S(2)}, u32[]{:S(2)}) collective-permute-start(f32[2,8,128]{2,1,0:T(8,128)S(1)} %shard_map.70.refs_3_), channel_id=1, source_target_pairs={{0,2},{1,3},{2,0},{3,1},{4,6},{5,7},{6,4},{7,5},{8,10},{9,11},{10,... | collective-permute-start | bytes 24584 | tf_op jit(solution)/shard_map/ppermute | solution.py:234
  15.4 8.6 %collective-permute-start.10 = (f32[2,16,1024]{2,1,0:T(8,128)S(1)}, f32[2,16,1024]{2,1,0:T(8,128)S(1)}, u32[]{:S(2)}, u32[]{:S(2)}) collective-permute-start(f32[2,16,1024]{2,1,0:T(8,128)S(1)} %get-tuple-element.62), channel_id=1, source_target_pairs={{0,24},{4,28},{8,16},{12,20},{16,8},{20,12},{24,0},{28,4},{1,25},{... | collective-permute-start | bytes 393224 | tf_op jit(solution)/shard_map/ppermute | solution.py:60
  17.9 6.6 %collective-permute-start.11 = (f32[2,16,1024]{2,1,0:T(8,128)S(1)}, f32[2,16,1024]{2,1,0:T(8,128)S(1)}, u32[]{:S(2)}, u32[]{:S(2)}) collective-permute-start(f32[2,16,1024]{2,1,0:T(8,128)S(1)} %get-tuple-element.63), channel_id=1, source_target_pairs={{0,8},{4,20},{8,0},{12,28},{16,24},{20,4},{24,16},{28,12},{1,9},{5... | collective-permute-start | bytes 393224 | tf_op jit(solution)/shard_map/ppermute | solution.py:60
  18.4 6.1 %collective-permute-start.12 = (f32[2,16,1024]{2,1,0:T(8,128)S(1)}, f32[2,16,1024]{2,1,0:T(8,128)S(1)}, u32[]{:S(2)}, u32[]{:S(2)}) collective-permute-start(f32[2,16,1024]{2,1,0:T(8,128)S(1)} %get-tuple-element.64), channel_id=1, source_target_pairs={{0,16},{4,12},{8,24},{12,4},{16,0},{20,28},{24,8},{28,20},{1,17},{... | collective-permute-start | bytes 393224 | tf_op jit(solution)/shard_map/ppermute | solution.py:60
  20.9 8.4 %collective-permute-start.4 = (f32[2,16,1024]{2,1,0:T(8,128)S(1)}, f32[2,16,1024]{2,1,0:T(8,128)S(1)}, u32[]{:S(2)}, u32[]{:S(2)}) collective-permute-start(f32[2,16,1024]{2,1,0:T(8,128)S(1)} %get-tuple-element.52), channel_id=1, source_target_pairs={{0,24},{4,28},{8,16},{12,20},{16,8},{20,12},{24,0},{28,4},{1,25},{... | collective-permute-start | bytes 393224 | tf_op jit(solution)/shard_map/ppermute | solution.py:60
  23.5 7.8 %collective-permute-start.5 = (f32[2,16,1024]{2,1,0:T(8,128)S(1)}, f32[2,16,1024]{2,1,0:T(8,128)S(1)}, u32[]{:S(2)}, u32[]{:S(2)}) collective-permute-start(f32[2,16,1024]{2,1,0:T(8,128)S(1)} %get-tuple-element.53), channel_id=1, source_target_pairs={{0,8},{4,20},{8,0},{12,28},{16,24},{20,4},{24,16},{28,12},{1,9},{5... | collective-permute-start | bytes 393224 | tf_op jit(solution)/shard_map/ppermute | solution.py:60
  24.0 9.2 %collective-permute-start.6 = (f32[2,16,1024]{2,1,0:T(8,128)S(1)}, f32[2,16,1024]{2,1,0:T(8,128)S(1)}, u32[]{:S(2)}, u32[]{:S(2)}) collective-permute-start(f32[2,16,1024]{2,1,0:T(8,128)S(1)} %get-tuple-element.54), channel_id=1, source_target_pairs={{0,16},{4,12},{8,24},{12,4},{16,0},{20,28},{24,8},{28,20},{1,17},{... | collective-permute-start | bytes 393224 | tf_op jit(solution)/shard_map/ppermute | solution.py:60
  25.3 10.8 %collective-permute-start.14 = (f32[2,16,1024]{2,1,0:T(8,128)S(1)}, f32[2,16,1024]{2,1,0:T(8,128)S(1)}, u32[]{:S(2)}, u32[]{:S(2)}) collective-permute-start(f32[2,16,1024]{2,1,0:T(8,128)S(1)} %get-tuple-element.70), channel_id=1, source_target_pairs={{0,24},{4,28},{8,16},{12,20},{16,8},{20,12},{24,0},{28,4},{1,25},{... | collective-permute-start | bytes 393224 | tf_op jit(solution)/shard_map/ppermute | solution.py:60
  29.2 12.3 %collective-permute-start.15 = (f32[2,16,1024]{2,1,0:T(8,128)S(1)}, f32[2,16,1024]{2,1,0:T(8,128)S(1)}, u32[]{:S(2)}, u32[]{:S(2)}) collective-permute-start(f32[2,16,1024]{2,1,0:T(8,128)S(1)} %get-tuple-element.71), channel_id=1, source_target_pairs={{0,8},{4,20},{8,0},{12,28},{16,24},{20,4},{24,16},{28,12},{1,9},{5... | collective-permute-start | bytes 393224 | tf_op jit(solution)/shard_map/ppermute | solution.py:60
  29.3 12.2 %collective-permute-start.16 = (f32[2,16,1024]{2,1,0:T(8,128)S(1)}, f32[2,16,1024]{2,1,0:T(8,128)S(1)}, u32[]{:S(2)}, u32[]{:S(2)}) collective-permute-start(f32[2,16,1024]{2,1,0:T(8,128)S(1)} %get-tuple-element.72), channel_id=1, source_target_pairs={{0,16},{4,12},{8,24},{12,4},{16,0},{20,28},{24,8},{28,20},{1,17},{... | collective-permute-start | bytes 393224 | tf_op jit(solution)/shard_map/ppermute | solution.py:60
  33.9 7.7 %collective-permute-start.7 = (f32[2,16,1024]{2,1,0:T(8,128)S(1)}, f32[2,16,1024]{2,1,0:T(8,128)S(1)}, u32[]{:S(2)}, u32[]{:S(2)}) collective-permute-start(f32[2,16,1024]{2,1,0:T(8,128)S(1)} %get-tuple-element.56), channel_id=1, source_target_pairs={{0,24},{4,28},{8,16},{12,20},{16,8},{20,12},{24,0},{28,4},{1,25},{... | collective-permute-start | bytes 393224 | tf_op jit(solution)/shard_map/ppermute | solution.py:60
  35.4 6.3 %collective-permute-start.8 = (f32[2,16,1024]{2,1,0:T(8,128)S(1)}, f32[2,16,1024]{2,1,0:T(8,128)S(1)}, u32[]{:S(2)}, u32[]{:S(2)}) collective-permute-start(f32[2,16,1024]{2,1,0:T(8,128)S(1)} %get-tuple-element.57), channel_id=1, source_target_pairs={{0,8},{4,20},{8,0},{12,28},{16,24},{20,4},{24,16},{28,12},{1,9},{5... | collective-permute-start | bytes 393224 | tf_op jit(solution)/shard_map/ppermute | solution.py:60
  36.1 5.6 %collective-permute-start.9 = (f32[2,16,1024]{2,1,0:T(8,128)S(1)}, f32[2,16,1024]{2,1,0:T(8,128)S(1)}, u32[]{:S(2)}, u32[]{:S(2)}) collective-permute-start(f32[2,16,1024]{2,1,0:T(8,128)S(1)} %get-tuple-element.58), channel_id=1, source_target_pairs={{0,16},{4,12},{8,24},{12,4},{16,0},{20,28},{24,8},{28,20},{1,17},{... | collective-permute-start | bytes 393224 | tf_op jit(solution)/shard_map/ppermute | solution.py:60
  41.5 2.3 %collective-permute-start.17 = (f32[4,16,1024]{2,1,0:T(8,128)S(1)}, f32[4,16,1024]{2,1,0:T(8,128)S(1)}, u32[]{:S(2)}, u32[]{:S(2)}) collective-permute-start(f32[4,16,1024]{2,1,0:T(8,128)S(1)} %shard_map.77), channel_id=1, source_target_pairs={{0,4},{4,0},{8,12},{12,8},{16,20},{20,16},{24,28},{28,24},{1,5},{5... | collective-permute-start | bytes 786440 | tf_op jit(solution)/shard_map/ppermute | solution.py:279
  41.6 1.6 %copy-start.1 = (f32[32,16,1024]{2,1,0:T(8,128)S(1)}, f32[32,16,1024]{2,1,0:T(8,128)}, u32[]{:S(2)}) copy-start(f32[32,16,1024]{2,1,0:T(8,128)} %get-tuple-element.69.refs_5_) | copy-start | bytes 6291460
  43.3 1.7 %collective-permute-start.13 = (f32[4,16,1024]{2,1,0:T(8,128)S(1)}, f32[4,16,1024]{2,1,0:T(8,128)S(1)}, u32[]{:S(2)}, u32[]{:S(2)}) collective-permute-start(f32[4,16,1024]{2,1,0:T(8,128)S(1)} %shard_map.76), channel_id=1, source_target_pairs={{0,4},{4,0},{8,12},{12,8},{16,20},{20,16},{24,28},{28,24},{1,5},{5... | collective-permute-start | bytes 786440 | tf_op jit(solution)/shard_map/ppermute | solution.py:279

commit v5 on v4

--- a/solution.py
+++ b/solution.py
@@ -60,69 +60,75 @@
     return lax.ppermute(array, "path", [(i, target(i, k, size)) for i in range(size)])
 
 
-def pack_kernel(size, here_ref, delta_ref, square_ref, give_ref, *outs):
-    total = jnp.zeros(square_ref.shape, jnp.float32)
+def tiles_of(rows, width):
+    return [(slice(row, row + 8), slice(lane, lane + 128)) for row in range(0, rows, 8) for lane in range(0, width, 128)]
+
+
+def pack_kernel(here_ref, delta_ref, keep_ref, give_ref):
+    levels, chips, halves, rows, width = delta_ref.shape
+    spots = tiles_of(rows, width)
+
+    def pack(core):
+        totals = [jnp.zeros((8, 128), jnp.float32) for _ in range(4)]
+        for level in range(levels):
+            for chip in range(chips):
+                for t, spot in enumerate(spots):
+                    place = (level * chips + chip) * len(spots) + t
+                    kept = delta_ref[(level, chip, core, *spot)]
+                    given = delta_ref[(level, chip, 1 - core, *spot)]
+                    keep_ref[place] = kept
+                    give_ref[place] = given
+                    totals[t % 4] = totals[t % 4] + (kept * kept + given * given)
+        total = (totals[0] + totals[1]) + (totals[2] + totals[3])
+        keep_ref[levels * chips * len(spots)] = total
+        give_ref[levels * chips * len(spots)] = total
+
+    for core in range(halves):
+        pl.when(here_ref[0] & 1 == core)(lambda core=core: pack(core))
+
+
+def merge_kernel(size, here_ref, keep_ref, gift_ref, *outs):
     order = order_of(size)
+    chips = len(order)
     here = here_ref[0]
     core = here & 1
+    last = keep_ref.shape[0] - 1
+    count = last // (LEVELS * chips)
     for level in range(LEVELS):
         for j, k in enumerate(order):
-            chip = target(here, k, size) // 2
-            kept = delta_ref[level, chip, core]
-            given = delta_ref[level, chip, 1 - core]
-            outs[level * len(order) + j][...] = kept
-            give_ref[level, chip] = given
-            block = kept * kept + given * given
-            folded = block.reshape(-1, 8, block.shape[-1]).sum(axis=0)
-            for lane in range(0, block.shape[-1], 128):
-                total = total + folded[:, lane : lane + 128]
-    square_ref[...] = total
-
-
-def pair_kernel(here_ref, own_ref, other_ref, out_ref):
-    core = here_ref[0] & 1
-    out_ref[core] = own_ref[...]
-    out_ref[1 - core] = other_ref[...]
+            out = outs[level * chips + j]
+            first = (level * chips + target(here, k, size) // 2) * count
+            out[pl.ds(core * count, count)] = keep_ref[pl.ds(first, count)]
+            out[pl.ds((1 - core) * count, count)] = gift_ref[pl.ds(first, count)]
+            if level == 0:
+                out[2 * count + core] = keep_ref[last]
+                out[2 * count + 1 - core] = gift_ref[last]
+
+
+def collect_kernel(size, here_ref, *refs):
+    for j, k in enumerate(order_of(size)):
+        block = refs[j]
+        chip = origin(here_ref[0], k, size) // 2
+        for source in range(2):
+            refs[-1][2 * chip + source] = block[block.shape[0] - 2 + source]
 
 
 def add_kernel(a_ref, b_ref, out_ref):
     out_ref[...] = a_ref[...] + b_ref[...]
 
 
-def scale_kernel(entries, here_ref, ids_ref, plan_ref, squares_ref, other_ref, gift_ref, *refs):
-    del plan_ref
-    here = here_ref[0]
-    count = len(refs) // 2
-    rounds = count // LEVELS
-    order = order_of(2 * rounds)
-    for source in range(2):
-        tile = squares_ref[source] + other_ref[source]
+def factor_kernel(entries, here_ref, ids_ref, squares_ref, other_ref, out_ref):
+    size = ids_ref.shape[0]
+    sources = [(origin(here_ref[0], k, size) // 2) * 2 + half for k in order_of(size) for half in range(2)]
+    for i, path in enumerate(sources):
+        tile = squares_ref[path] + other_ref[path]
         total = jnp.broadcast_to(jnp.sum(tile, keepdims=True), (8, 128))
         rescale = 1.0 / jnp.sqrt(total / entries + 1e-06)
-        path = (here // 2) * 2 + source
         for level in range(LEVELS):
-            own = ids_ref[path, level]
             sharers = jnp.int32(0)
-            for other in range(ids_ref.shape[0]):
-                sharers = sharers + jnp.where(ids_ref[other, level] == own, 1, 0)
-            factor = rescale / jnp.full((8, 128), sharers, jnp.int32).astype(jnp.float32)
-
-            def scale(own_rows, level=level, source=source, factor=factor):
-                for j, k in enumerate(order):
-                    out = refs[count + level * rounds + j]
-                    chip = target(here, k, 2 * rounds) // 2
-                    _, rows, width = out.shape
-                    for row in range(0, rows, 8):
-                        for lane in range(0, width, 128):
-                            at = (slice(row, row + 8), slice(lane, lane + 128))
-                            if own_rows:
-                                block = refs[level * rounds + j][at]
-                            else:
-                                block = gift_ref[(level, chip, *at)]
-                            out[(source, *at)] = block * factor
-
-            pl.when(here & 1 == source)(lambda scale=scale: scale(True))
-            pl.when(here & 1 != source)(lambda scale=scale: scale(False))
+            for other in range(size):
+                sharers = sharers + jnp.where(ids_ref[other, level] == ids_ref[path, level], 1, 0)
+            out_ref[level, i] = rescale / jnp.full((8, 128), sharers, jnp.int32).astype(jnp.float32)
 
 
 def plan_kernel(here_ref, ids_ref, chosen_ref, sender_ref, receiver_ref, module_ref):
@@ -145,10 +151,14 @@
                 receiver_ref[level, 2 * j + half] = module_ref[module]
 
 
-def outgoing_kernel(level, rounds, chosen_ref, sender_ref, receiver_ref, decayed_ref, *refs):
-    received, outs, grad_ref = refs[:rounds], refs[rounds:-1], refs[-1]
+def outgoing_kernel(level, rounds, chosen_ref, sender_ref, receiver_ref, factor_ref, decayed_ref, *refs):
+    received, outs, (grad_ref, token_ref) = refs[:rounds], refs[rounds:-2], refs[-2:]
+    token_ref[0] = 0
+    spots = tiles_of(*grad_ref.shape[1:])
     for i in range(2 * rounds):
-        grad_ref[i] = received[i // 2][i % 2]
+        factor = factor_ref[level, i]
+        for t, spot in enumerate(spots):
+            grad_ref[(i, *spot)] = received[i // 2][(i % 2) * len(spots) + t] * factor
     for i in range(1, 2 * rounds):
         leader = sender_ref[level, i]
 
@@ -161,8 +171,9 @@
         outs[i // 2][i % 2] = decayed - grad_coef * grad_ref[receiver_ref[level, i]]
 
 
-def state_kernel(level, module_ref, grad_ref, decayed_ref, momentum_ref, *outs):
-    new_params_ref, new_momentum_ref = outs[-2:]
+def state_kernel(level, module_ref, grad_ref, decayed_ref, momentum_ref, *refs):
+    new_params_ref, new_momentum_ref, token_ref = refs[-3:]
+    token_ref[0] = 0
     count = new_params_ref.shape[0]
     first = level * LEVEL_MODULES + pl.program_id(0) * count
     for place in range(count):
@@ -209,83 +220,100 @@
     order = order_of(size)
     rounds = len(order)
     swap = [(i, i ^ 1) for i in range(size)]
-    rows = jax.ShapeDtypeStruct((own_rows, width), jnp.float32)
-    both = jax.ShapeDtypeStruct((2, own_rows, width), jnp.float32)
-    by_chip = jax.ShapeDtypeStruct((rounds, own_rows, width), jnp.float32)
-    by_path = jax.ShapeDtypeStruct((size, own_rows, width), jnp.float32)
-    tile = jax.ShapeDtypeStruct((8, 128), jnp.float32)
-    tiles = jax.ShapeDtypeStruct((2, 8, 128), jnp.float32)
+    count = own_rows * width // 1024
+    shape = lambda *dims: jax.ShapeDtypeStruct(dims, jnp.float32)
     places = jax.ShapeDtypeStruct((LEVELS, size), jnp.int32)
-
-    squares, give, *kept = call(
-        lambda *refs: pack_kernel(size, *refs),
-        [tile, jax.ShapeDtypeStruct((LEVELS, *by_chip.shape), jnp.float32)] + [rows] * (LEVELS * rounds),
-        [smem, vmem],
-        [vmem] * (2 + LEVELS * rounds),
+    token = jax.ShapeDtypeStruct((1,), jnp.int32)
+
+    keep, give = call(
+        pack_kernel, [shape(LEVELS * rounds * count + 1, 8, 128)] * 2, [smem, vmem], [vmem] * 2
     )(here, split_slab)
-    other = lax.ppermute(squares, "path", swap)
     gift = lax.ppermute(give, "path", swap)
-    squares = call(pair_kernel, tiles, [smem, vmem, vmem], vmem)(here, squares, other)
-    other = jnp.zeros_like(squares)
-    step = 1
-    while step < shards:
-        if step > 1:
-            squares = call(add_kernel, tiles, [vmem, vmem], vmem)(squares, other)
-        other = lax.ppermute(squares, "shard", [(i, i ^ step) for i in range(shards)])
-        step *= 2
+    messages = call(
+        lambda *refs: merge_kernel(size, *refs),
+        [shape(2 * count + 2 * (level == 0), 8, 128) for level in range(LEVELS) for _ in order],
+        [smem, vmem, vmem],
+        [vmem] * (LEVELS * rounds),
+    )(here, keep, gift)
+    received = [
+        [move(messages[level * rounds + j], k, size) for j, k in enumerate(order)] for level in range(LEVELS)
+    ]
     chosen, sender, receiver, leaders = call(
         plan_kernel,
         [places, places, places, jax.ShapeDtypeStruct((module_count,), jnp.int32)],
         [smem, smem],
         [smem] * 4,
     )(here, assign)
-    scaled = call(
-        lambda *refs: scale_kernel(entries, *refs),
-        [both] * (LEVELS * rounds),
-        [smem, smem, smem] + [vmem] * (3 + LEVELS * rounds),
-        [vmem] * (LEVELS * rounds),
-    )(here, assign, chosen, squares, other, gift, *kept)
     decayed = state_in - moment_coef * moment_in
 
-    path_params, new_state, new_moment = None, None, None
+    squares = call(
+        lambda *refs: collect_kernel(size, *refs),
+        shape(size, 8, 128),
+        [smem] + [vmem] * rounds + [smem, anywhere],
+        vmem,
+    )(here, *received[0], chosen, decayed)
+    other = jnp.zeros_like(squares)
+    step = 1
+    while step < shards:
+        if step > 1:
+            squares = call(add_kernel, shape(size, 8, 128), [vmem, vmem], vmem)(squares, other)
+        other = lax.ppermute(squares, "shard", [(i, i ^ step) for i in range(shards)])
+        step *= 2
+    factors = call(
+        lambda *refs: factor_kernel(entries, *refs),
+        shape(LEVELS, size, 8, 128),
+        [smem, smem, vmem, vmem],
+        vmem,
+    )(here, assign, squares, other)
+
+    returned, grads, updated = [], [], []
+    for level in range(LEVELS):
+        *outgoing, grad, done = call(
+            lambda *refs, level=level: outgoing_kernel(level, rounds, *refs),
+            [shape(2, own_rows, width)] * rounds + [shape(size, own_rows, width), token],
+            [smem] * 3 + [vmem] * (2 + rounds),
+            [vmem] * (rounds + 1) + [smem],
+        )(chosen, sender, receiver, factors, decayed, *received[level])
+        returned.append([move(outgoing[j], k, size) for j, k in enumerate(order)])
+        grads.append(grad)
+        updated.append(done)
+
+    new_state, new_moment, tokens = None, None, []
     block = LEVEL_MODULES // 2
     steps = LEVEL_MODULES // block
     for level in range(LEVELS):
-        received = [move(scaled[level * rounds + j], k, size) for j, k in enumerate(order)]
-        *outgoing, grad = call(
-            lambda *refs, level=level: outgoing_kernel(level, rounds, *refs),
-            [both] * rounds + [by_path],
-            [smem] * 3 + [vmem] * (1 + rounds),
-            [vmem] * (rounds + 1),
-        )(chosen, sender, receiver, decayed, *received)
-        returned = [move(outgoing[j], k, size) for j, k in enumerate(order)]
         held = [] if level == 0 else [new_state, new_moment]
         state_block = pl.BlockSpec((block, own_rows, width), lambda i, level=level: (i + level * steps, 0, 0))
-        new_state, new_moment = call(
+        new_state, new_moment, done = call(
             lambda *refs, level=level: state_kernel(level, *refs),
-            [jax.ShapeDtypeStruct(state_in.shape, jnp.float32)] * 2,
+            [shape(*state_in.shape)] * 2 + [token],
             [smem, vmem, vmem, vmem] + [anywhere] * len(held),
-            [state_block, state_block],
+            [state_block, state_block, smem],
             grid=(steps,),
             input_output_aliases={4: 0, 5: 1} if held else {},
-        )(leaders, grad, decayed, moment_in, *held)
-        before = [new_state] if level == LEVELS - 1 else []
+        )(leaders, grads[level], decayed, moment_in, *held)
+        tokens.append(done)
+
+    path_params = None
+    before = updated[1:] + tokens
+    for level in range(LEVELS):
         back = call(
             lambda *refs: give_back_kernel(size, *refs),
-            by_chip,
-            [smem] + [vmem] * rounds + [anywhere] * len(before),
+            shape(rounds, own_rows, width),
+            [smem] + [vmem] * rounds + [smem] * len(before),
             vmem,
-        )(here, *returned, *before)
+        )(here, *returned[level], *before)
         back = lax.ppermute(back, "path", swap)
         held = [] if level == 0 else [path_params]
         path_params = call(
             lambda *refs, level=level: assemble_kernel(size, level, *refs),
-            jax.ShapeDtypeStruct(split_slab.shape, jnp.float32),
+            shape(*split_slab.shape),
             [smem] + [anywhere] * (rounds + 1 + len(held)),
             anywhere,
             scratch_shapes=[pltpu.SemaphoreType.DMA((2, rounds))],
             input_output_aliases={2 + rounds: 0} if held else {},
-        )(here, *returned, back, *held)
+        )(here, *returned[level], back, *held)
+        before = tokens
     return (path_params.reshape(path_delta.shape), new_state[:, None], new_moment[:, None])
 
 

time: 46 us -> 49.2 us (1.070); the launches traced: 45.8 us -> 48.4 us
  Pallas kernels: 10.6 us -> 14.3 us
  waiting for transfers between devices: 6.56 us -> 8.74 us
  starting transfers between devices: 22.2 us -> 20.3 us
  local copies, waits for them, and re-layouts: 3.71 us -> 2.12 us
    pallas_call x12 -> x13, Pallas kernels: 9.24 us -> 13 us  [the longest x2 3.96 us: local(): call(lambda *refs, level=level: state_kernel(level, *refs), [shape(*state...]
    unnamed x7 -> x13, local copies, waits for them, and re-layouts: 3.71 us -> 2.12 us
    ppermute x1, waiting for transfers between devices: 0.01 us -> 1.54 us  [local(): gift = lax.ppermute(give, 'path', swap)]
    ppermute x2, starting transfers between devices: 5.72 us -> 4.23 us  [local(): lax.ppermute(squares, 'shard', [(i, i ^ step) for i in range(shards)])]
    ppermute x1 -> x0, waiting for transfers between devices: 1.4 us -> none  [local(): other = lax.ppermute(squares, 'path', swap)]
    ppermute x12, waiting for transfers between devices: 3.23 us -> 4.55 us  [move(): lax.ppermute(array, 'path', [(i, target(i, k, size)) for i in range(size)])]
    ppermute x2, waiting for transfers between devices: 1.62 us -> 2.34 us  [local(): lax.ppermute(squares, 'shard', [(i, i ^ step) for i in range(shards)])]
  transfers between devices with their start and end apart: 18 -> 17, of which waited for: 5 -> 6; matrix products, arithmetic and copies ran while one was open for 6% -> 4% of each run, Pallas kernels for 17% -> 26%
where the time goes in v5:
time: 49.2 us; the launch traced here: 48.4 us
  starting transfers between devices  20.3 us (41%)
  Pallas kernels  14.3 us (29%)
  waiting for transfers between devices  8.74 us (18%)
  local copies, waits for them, and re-layouts  2.12 us (4%)
  other arithmetic  2.03 us (4%)
  between operations  0.81 us (2%)
    ppermute x12, starting transfers between devices, move(): lax.ppermute(array, 'path', [(i, target(i, k, size)) for i in range(size)])  15 us
    ppermute x12, waiting for transfers between devices, move(): lax.ppermute(array, 'path', [(i, target(i, k, size)) for i in range(size)])  4.55 us
    ppermute x2, starting transfers between devices, local(): lax.ppermute(squares, 'shard', [(i, i ^ step) for i in range(shards)])  4.23 us
    pallas_call x2, Pallas kernels, local(): call(lambda *refs, level=level: state_kernel(level, *refs), [shape(*state...  3.96 us
    pallas_call x2, Pallas kernels, local(): call(lambda *refs: give_back_kernel(size, *refs), shape(rounds, own_rows,...  3.31 us
    pallas_call x2, Pallas kernels, local(): call(lambda *refs, level=level: outgoing_kernel(level, rounds, *refs), [s...  2.47 us
    ppermute x2, waiting for transfers between devices, local(): lax.ppermute(squares, 'shard', [(i, i ^ step) for i in range(shards)])  2.34 us
    unnamed x13, local copies, waits for them, and re-layouts  2.12 us
  transfers between devices with their start and end apart: 17, of which 6 were waited for; matrix products, arithmetic and copies ran while one was open for 4% of the time, Pallas kernels for 26%

profile of v5, /device:TPU:0, one launch (start us, length us, event | category | flops | bytes accessed | tf_op | source)
XLA Modules:
  0.0 48.4 jit_solution(563515985419242393)
XLA Ops:
  0.6 0.0 copy-start
  0.7 1.4 %copy-done.2 = f32[1,2,128,1024]{3,2,1,0:T(8,128)S(1)} copy-done((f32[1,2,128,1024]{3,2,1,0:T(8,128)S(1)}, f32[1,2,128,1024]{3,2,1,0:T(8,128)}, u32[]{:S(2)}) %copy-start.2) | copy-done | bytes 1048600
  2.0 0.1 shard_map.68
  2.1 0.5 %collective-permute-start = (f32[129,8,128]{2,1,0:T(8,128)S(1)}, f32[129,8,128]{2,1,0:T(8,128)S(1)}, u32[]{:S(2)}, u32[]{:S(2)}) collective-permute-start(f32[129,8,128]{2,1,0:T(8,128)S(1)} %get-tuple-element.38), channel_id=1, source_target_pairs={{0,4},{4,0},{8,12},{12,8},{16,20},{20,16},{24,28},{28,24},{1,5},{5... | collective-permute-start | bytes 1585160 | tf_op jit(solution)/shard_map/ppermute | solution.py:231
  2.6 1.5 %collective-permute-done.refs_2_ = f32[129,8,128]{2,1,0:T(8,128)S(1)} collective-permute-done((f32[129,8,128]{2,1,0:T(8,128)S(1)}, f32[129,8,128]{2,1,0:T(8,128)S(1)}, u32[]{:S(2)}, u32[]{:S(2)}) %collective-permute-start) | collective-permute-done | bytes 528416 | tf_op jit(solution)/shard_map/ppermute | solution.py:231
  4.2 0.1 shard_map.69
  4.3 0.0 copy-start.3
  4.3 0.6 %copy-done.3 = f32[32,8,128]{2,1,0:T(8,128)} copy-done((f32[32,8,128]{2,1,0:T(8,128)}, f32[32,8,128]{2,1,0:T(8,128)S(1)}, u32[]{:S(2)}) %copy-start.3) | copy-done | bytes 131096
  4.9 3.8 %collective-permute-start.1 = (f32[34,8,128]{2,1,0:T(8,128)S(1)}, f32[34,8,128]{2,1,0:T(8,128)S(1)}, u32[]{:S(2)}, u32[]{:S(2)}) collective-permute-start(f32[34,8,128]{2,1,0:T(8,128)S(1)} %get-tuple-element.39), channel_id=1, source_target_pairs={{0,24},{4,28},{8,16},{12,20},{16,8},{20,12},{24,0},{28,4},{1,25},{... | collective-permute-start | bytes 417800 | tf_op jit(solution)/shard_map/ppermute | solution.py:60
  8.8 0.5 %collective-permute-start.2 = (f32[34,8,128]{2,1,0:T(8,128)S(1)}, f32[34,8,128]{2,1,0:T(8,128)S(1)}, u32[]{:S(2)}, u32[]{:S(2)}) collective-permute-start(f32[34,8,128]{2,1,0:T(8,128)S(1)} %get-tuple-element.40), channel_id=1, source_target_pairs={{0,8},{4,20},{8,0},{12,28},{16,24},{20,4},{24,16},{28,12},{1,9},{5... | collective-permute-start | bytes 417800 | tf_op jit(solution)/shard_map/ppermute | solution.py:60
  9.3 0.0 collective-permute-start.3
  9.3 2.0 %bitcast_subtract_fusion.refs_6_.refs_4_.refs_2_ = f32[32,16,1024]{2,1,0:T(8,128)S(1)} fusion(f32[32,1,16,1024]{3,2,1,0:T(8,128)} %param.6, f32[32,1,16,1024]{3,2,1,0:T(8,128)S(1)} %copy-done), kind=kLoop, calls=%fused_computation | loop fusion | flops 1048576 | bytes 6291456 | tf_op jit(solution)/shard_map/sub | solution.py:247
  11.4 0.1 copy.10.ids_ref.refs_1_
  11.4 1.3 %shard_map.67 = (s32[2,8]{1,0:T(2,128)S(1)}, s32[2,8]{1,0:T(2,128)S(1)}, s32[2,8]{1,0:T(2,128)S(1)}, s32[32]{0:T(128)S(1)}) custom-call(s32[1]{0:T(128)} %bitcast.here_ref.refs_0_, s32[8,2]{1,0:T(8,128)S(1)} %copy.10.ids_ref.refs_1_), custom_call_target="tpu_custom_call" | custom-call | tf_op jit(solution)/shard_map/pallas_call | solution.py:241
  12.8 0.2 collective-permute-done.1.refs_1_.refs_5_
  13.0 3.0 %collective-permute-done.2.refs_2_.refs_6_ = f32[34,8,128]{2,1,0:T(8,128)S(1)} collective-permute-done((f32[34,8,128]{2,1,0:T(8,128)S(1)}, f32[34,8,128]{2,1,0:T(8,128)S(1)}, u32[]{:S(2)}, u32[]{:S(2)}) %collective-permute-start.2) | collective-permute-done | bytes 139296 | tf_op jit(solution)/shard_map/ppermute | solution.py:60
  16.0 0.0 collective-permute-done.3.refs_3_.refs_7_
  16.0 0.6 %shard_map.70.a_ref = f32[8,8,128]{2,1,0:T(8,128)S(1)} custom-call(s32[1]{0:T(128)} %bitcast.here_ref.refs_0_, f32[34,8,128]{2,1,0:T(8,128)S(1)} %collective-permute-done.1.refs_1_.refs_5_, f32[34,8,128]{2,1,0:T(8,128)S(1)} %collective-permute-done.2.refs_2_.refs_6_, f32[34,8,128]{2,1,0:T(8,128)S(1)} %collective-permute-done.3.refs_3_.refs_7_, ...), custom_call_target="tpu_custom_call" | custom-call | tf_op jit(solution)/shard_map/pallas_call | solution.py:249
  16.6 1.6 %collective-permute-start.4 = (f32[8,8,128]{2,1,0:T(8,128)S(1)}, f32[8,8,128]{2,1,0:T(8,128)S(1)}, u32[]{:S(2)}, u32[]{:S(2)}) collective-permute-start(f32[8,8,128]{2,1,0:T(8,128)S(1)} %shard_map.70.a_ref), channel_id=1, source_target_pairs={{0,1},{1,0},{2,3},{3,2},{4,5},{5,4},{6,7},{7,6},{8,9},{9,8},{10,11... | collective-permute-start | bytes 98312 | tf_op jit(solution)/shard_map/ppermute | solution.py:260
  18.2 2.3 %collective-permute-done.4.b_ref = f32[8,8,128]{2,1,0:T(8,128)S(1)} collective-permute-done((f32[8,8,128]{2,1,0:T(8,128)S(1)}, f32[8,8,128]{2,1,0:T(8,128)S(1)}, u32[]{:S(2)}, u32[]{:S(2)}) %collective-permute-start.4) | collective-permute-done | bytes 32800 | tf_op jit(solution)/shard_map/ppermute | solution.py:260
  20.6 2.6 %collective-permute-start.5 = (f32[8,8,128]{2,1,0:T(8,128)S(1)}, f32[8,8,128]{2,1,0:T(8,128)S(1)}, u32[]{:S(2)}, u32[]{:S(2)}) collective-permute-start(f32[8,8,128]{2,1,0:T(8,128)S(1)} %shard_map.71.refs_2_), channel_id=1, source_target_pairs={{0,2},{1,3},{2,0},{3,1},{4,6},{5,7},{6,4},{7,5},{8,10},{9,11},{10,... | collective-permute-start | bytes 98312 | tf_op jit(solution)/shard_map/ppermute | solution.py:260
  23.2 1.6 %collective-permute-start.6 = (f32[32,8,128]{2,1,0:T(8,128)S(1)}, f32[32,8,128]{2,1,0:T(8,128)S(1)}, u32[]{:S(2)}, u32[]{:S(2)}) collective-permute-start(f32[32,8,128]{2,1,0:T(8,128)S(1)} %copy-done.4), channel_id=1, source_target_pairs={{0,24},{4,28},{8,16},{12,20},{16,8},{20,12},{24,0},{28,4},{1,25},{... | collective-permute-start | bytes 393224 | tf_op jit(solution)/shard_map/ppermute | solution.py:60
  24.8 1.2 %collective-permute-start.7 = (f32[32,8,128]{2,1,0:T(8,128)S(1)}, f32[32,8,128]{2,1,0:T(8,128)S(1)}, u32[]{:S(2)}, u32[]{:S(2)}) collective-permute-start(f32[32,8,128]{2,1,0:T(8,128)S(1)} %get-tuple-element.44), channel_id=1, source_target_pairs={{0,8},{4,20},{8,0},{12,28},{16,24},{20,4},{24,16},{28,12},{1,9},{5... | collective-permute-start | bytes 393224 | tf_op jit(solution)/shard_map/ppermute | solution.py:60
  26.0 0.6 %collective-permute-start.8 = (f32[32,8,128]{2,1,0:T(8,128)S(1)}, f32[32,8,128]{2,1,0:T(8,128)S(1)}, u32[]{:S(2)}, u32[]{:S(2)}) collective-permute-start(f32[32,8,128]{2,1,0:T(8,128)S(1)} %get-tuple-element.45), channel_id=1, source_target_pairs={{0,16},{4,12},{8,24},{12,4},{16,0},{20,28},{24,8},{28,20},{1,17},{... | collective-permute-start | bytes 393224 | tf_op jit(solution)/shard_map/ppermute | solution.py:60
  26.7 0.8 %shard_map.72.refs_3_ = f32[2,8,8,128]{3,2,1,0:T(8,128)S(1)} custom-call(s32[1]{0:T(128)} %bitcast.here_ref.refs_0_, s32[8,2]{1,0:T(8,128)S(1)} %copy.10.ids_ref.refs_1_, f32[8,8,128]{2,1,0:T(8,128)S(1)} %shard_map.71.refs_2_, f32[8,8,128]{2,1,0:T(8,128)S(1)} %collective-permute-done.5.refs_3_), custom_call_target="tpu_custom_call" | custom-call | tf_op jit(solution)/shard_map/pallas_call | solution.py:262
  27.5 0.0 copy-start.1
  27.5 1.2 %shard_map.74 = (f32[2,16,1024]{2,1,0:T(8,128)S(1)}, f32[2,16,1024]{2,1,0:T(8,128)S(1)}, f32[2,16,1024]{2,1,0:T(8,128)S(1)}, f32[2,16,1024]{2,1,0:T(8,128)S(1)}, f32[8,16,1024]{2,1,0:T(8,128)S(1)}, /*index=5*/s32[1]{0:T(128)}) custom-call(s32[2,8]{1,0:T(2,128)S(1)} %get-tuple-element.34.refs_5_.refs_0_, s32[2,8]{1,0:T(2,128)S(1)} %get-tuple-element.35.refs_1_, ...), custom_call_target="tpu_custom_call" | custom-call | tf_op jit(solution)/shard_map/pallas_call | solution.py:271
  28.7 1.7 %collective-permute-start.13 = (f32[2,16,1024]{2,1,0:T(8,128)S(1)}, f32[2,16,1024]{2,1,0:T(8,128)S(1)}, u32[]{:S(2)}, u32[]{:S(2)}) collective-permute-start(f32[2,16,1024]{2,1,0:T(8,128)S(1)} %get-tuple-element.58), channel_id=1, source_target_pairs={{0,24},{4,28},{8,16},{12,20},{16,8},{20,12},{24,0},{28,4},{1,25},{... | collective-permute-start | bytes 393224 | tf_op jit(solution)/shard_map/ppermute | solution.py:60
  30.4 1.2 %collective-permute-start.14 = (f32[2,16,1024]{2,1,0:T(8,128)S(1)}, f32[2,16,1024]{2,1,0:T(8,128)S(1)}, u32[]{:S(2)}, u32[]{:S(2)}) collective-permute-start(f32[2,16,1024]{2,1,0:T(8,128)S(1)} %get-tuple-element.59), channel_id=1, source_target_pairs={{0,8},{4,20},{8,0},{12,28},{16,24},{20,4},{24,16},{28,12},{1,9},{5... | collective-permute-start | bytes 393224 | tf_op jit(solution)/shard_map/ppermute | solution.py:60
  31.7 0.0 collective-permute-done.6.refs_5_
  31.7 0.6 %collective-permute-start.15 = (f32[2,16,1024]{2,1,0:T(8,128)S(1)}, f32[2,16,1024]{2,1,0:T(8,128)S(1)}, u32[]{:S(2)}, u32[]{:S(2)}) collective-permute-start(f32[2,16,1024]{2,1,0:T(8,128)S(1)} %get-tuple-element.60), channel_id=1, source_target_pairs={{0,16},{4,12},{8,24},{12,4},{16,0},{20,28},{24,8},{28,20},{1,17},{... | collective-permute-start | bytes 393224 | tf_op jit(solution)/shard_map/ppermute | solution.py:60
  32.3 0.0 collective-permute-done.7.refs_6_
  32.3 1.3 %collective-permute-done.8.refs_7_ = f32[32,8,128]{2,1,0:T(8,128)S(1)} collective-permute-done((f32[32,8,128]{2,1,0:T(8,128)S(1)}, f32[32,8,128]{2,1,0:T(8,128)S(1)}, u32[]{:S(2)}, u32[]{:S(2)}) %collective-permute-start.8) | collective-permute-done | bytes 131104 | tf_op jit(solution)/shard_map/ppermute | solution.py:60
  33.6 1.2 %shard_map.73 = (f32[2,16,1024]{2,1,0:T(8,128)S(1)}, f32[2,16,1024]{2,1,0:T(8,128)S(1)}, f32[2,16,1024]{2,1,0:T(8,128)S(1)}, f32[2,16,1024]{2,1,0:T(8,128)S(1)}, f32[8,16,1024]{2,1,0:T(8,128)S(1)}, /*index=5*/s32[1]{0:T(128)}) custom-call(s32[2,8]{1,0:T(2,128)S(1)} %get-tuple-element.34.refs_5_.refs_0_, s32[2,8]{1,0:T(2,128)S(1)} %get-tuple-element.35.refs_1_, ...), custom_call_target="tpu_custom_call" | custom-call | tf_op jit(solution)/shard_map/pallas_call | solution.py:271
  34.9 1.6 %collective-permute-start.9 = (f32[2,16,1024]{2,1,0:T(8,128)S(1)}, f32[2,16,1024]{2,1,0:T(8,128)S(1)}, u32[]{:S(2)}, u32[]{:S(2)}) collective-permute-start(f32[2,16,1024]{2,1,0:T(8,128)S(1)} %get-tuple-element.47), channel_id=1, source_target_pairs={{0,24},{4,28},{8,16},{12,20},{16,8},{20,12},{24,0},{28,4},{1,25},{... | collective-permute-start | bytes 393224 | tf_op jit(solution)/shard_map/ppermute | solution.py:60
  36.4 1.0 %collective-permute-start.10 = (f32[2,16,1024]{2,1,0:T(8,128)S(1)}, f32[2,16,1024]{2,1,0:T(8,128)S(1)}, u32[]{:S(2)}, u32[]{:S(2)}) collective-permute-start(f32[2,16,1024]{2,1,0:T(8,128)S(1)} %get-tuple-element.48), channel_id=1, source_target_pairs={{0,8},{4,20},{8,0},{12,28},{16,24},{20,4},{24,16},{28,12},{1,9},{5... | collective-permute-start | bytes 393224 | tf_op jit(solution)/shard_map/ppermute | solution.py:60
  37.5 0.0 collective-permute-done.13.refs_1_
  37.5 1.0 %collective-permute-start.11 = (f32[2,16,1024]{2,1,0:T(8,128)S(1)}, f32[2,16,1024]{2,1,0:T(8,128)S(1)}, u32[]{:S(2)}, u32[]{:S(2)}) collective-permute-start(f32[2,16,1024]{2,1,0:T(8,128)S(1)} %get-tuple-element.49), channel_id=1, source_target_pairs={{0,16},{4,12},{8,24},{12,4},{16,0},{20,28},{24,8},{28,20},{1,17},{... | collective-permute-start | bytes 393224 | tf_op jit(solution)/shard_map/ppermute | solution.py:60
  38.4 2.0 %shard_map.75 = (f32[32,16,1024]{2,1,0:T(8,128)}, f32[32,16,1024]{2,1,0:T(8,128)}, s32[1]{0:T(128)}) custom-call(s32[32]{0:T(128)S(1)} %get-tuple-element.51.refs_0_, f32[8,16,1024]{2,1,0:T(8,128)S(1)} %get-tuple-element.52.refs_1_, f32[32,16,1024]{2,1,0:T(8,128)S(1)} %bitcast_subtract_fusion.refs_6_.refs_4_.refs_2_, f32[32,16,1024]{2,1,0:T(8,128)S(1)} %bitcast.13), custom_call_target="tpu_custom_call" | custom-call | tf_op jit(solution)/shard_map/pallas_call | solution.py:287
  40.4 2.0 %shard_map.76 = (f32[32,16,1024]{2,1,0:T(8,128)}, f32[32,16,1024]{2,1,0:T(8,128)}, s32[1]{0:T(128)}) custom-call(s32[32]{0:T(128)S(1)} %get-tuple-element.51.refs_0_, f32[8,16,1024]{2,1,0:T(8,128)S(1)} %get-tuple-element.54.refs_1_, f32[32,16,1024]{2,1,0:T(8,128)S(1)} %bitcast_subtract_fusion.refs_6_.refs_4_.refs_2_, ...), custom_call_target="tpu_custom_call", output_to_operand_aliasing={{0}: (4, {}), {1}: (5, {})} | custom-call | tf_op jit(solution)/shard_map/pallas_call | solution.py:287
  42.4 0.0 collective-permute-done.14.refs_2_
  42.4 2.0 %shard_map.78 = f32[4,16,1024]{2,1,0:T(8,128)S(1)} custom-call(s32[1]{0:T(128)} %bitcast.here_ref.refs_0_, f32[2,16,1024]{2,1,0:T(8,128)S(1)} %collective-permute-done.13.refs_1_, f32[2,16,1024]{2,1,0:T(8,128)S(1)} %collective-permute-done.14.refs_2_, f32[2,16,1024]{2,1,0:T(8,128)S(1)} %collective-permute-done.15.refs_3_, ...), custom_call_target="tpu_custom_call" | custom-call | tf_op jit(solution)/shard_map/pallas_call | solution.py:300
  44.4 0.1 collective-permute-start.16
  44.5 1.3 %shard_map.77 = f32[4,16,1024]{2,1,0:T(8,128)S(1)} custom-call(s32[1]{0:T(128)} %bitcast.here_ref.refs_0_, f32[2,16,1024]{2,1,0:T(8,128)S(1)} %collective-permute-done.9.refs_1_, f32[2,16,1024]{2,1,0:T(8,128)S(1)} %collective-permute-done.10.refs_2_, f32[2,16,1024]{2,1,0:T(8,128)S(1)} %collective-permute-done.11.refs_3_, ...), custom_call_target="tpu_custom_call" | custom-call | tf_op jit(solution)/shard_map/pallas_call | solution.py:300
  45.8 0.5 %collective-permute-start.12 = (f32[4,16,1024]{2,1,0:T(8,128)S(1)}, f32[4,16,1024]{2,1,0:T(8,128)S(1)}, u32[]{:S(2)}, u32[]{:S(2)}) collective-permute-start(f32[4,16,1024]{2,1,0:T(8,128)S(1)} %shard_map.77), channel_id=1, source_target_pairs={{0,4},{4,0},{8,12},{12,8},{16,20},{20,16},{24,28},{28,24},{1,5},{5... | collective-permute-start | bytes 786440 | tf_op jit(solution)/shard_map/ppermute | solution.py:306
  46.4 0.8 %shard_map.79.refs_6_ = f32[2,4,2,16,1024]{4,3,2,1,0:T(8,128)} custom-call(s32[1]{0:T(128)} %bitcast.here_ref.refs_0_, f32[2,16,1024]{2,1,0:T(8,128)S(1)} %collective-permute-done.13.refs_1_, f32[2,16,1024]{2,1,0:T(8,128)S(1)} %collective-permute-done.14.refs_2_, f32[2,16,1024]{2,1,0:T(8,128)S(1)} %collective-permute-done.15.refs_3_, ...), custom_call_target="tpu_custom_call" | custom-call | tf_op jit(solution)/shard_map/pallas_call | solution.py:308
  47.2 0.3 collective-permute-done.12.refs_5_
  47.5 0.8 %shard_map.80 = f32[2,4,2,16,1024]{4,3,2,1,0:T(8,128)} custom-call(s32[1]{0:T(128)} %bitcast.here_ref.refs_0_, f32[2,16,1024]{2,1,0:T(8,128)S(1)} %collective-permute-done.9.refs_1_, f32[2,16,1024]{2,1,0:T(8,128)S(1)} %collective-permute-done.10.refs_2_, f32[2,16,1024]{2,1,0:T(8,128)S(1)} %collective-permute-done.11.refs_3_, ...), custom_call_target="tpu_custom_call", output_to_operand_aliasing={{}: (6, {})} | custom-call | tf_op jit(solution)/shard_map/pallas_call | solution.py:308
  (14 shorter events, 0.0 us)
Async XLA Ops:
  0.6 8.7 %copy-start = (f32[32,1,16,1024]{3,2,1,0:T(8,128)S(1)}, f32[32,1,16,1024]{3,2,1,0:T(8,128)}, u32[]{:S(2)}) copy-start(f32[32,1,16,1024]{3,2,1,0:T(8,128)} %param.7) | copy-start | bytes 6291460
  0.6 1.4 %copy-start.2 = (f32[1,2,128,1024]{3,2,1,0:T(8,128)S(1)}, f32[1,2,128,1024]{3,2,1,0:T(8,128)}, u32[]{:S(2)}) copy-start(f32[1,2,128,1024]{3,2,1,0:T(8,128)} %param.4) | copy-start | bytes 3145732
  2.1 2.1 %collective-permute-start = (f32[129,8,128]{2,1,0:T(8,128)S(1)}, f32[129,8,128]{2,1,0:T(8,128)S(1)}, u32[]{:S(2)}, u32[]{:S(2)}) collective-permute-start(f32[129,8,128]{2,1,0:T(8,128)S(1)} %get-tuple-element.38), channel_id=1, source_target_pairs={{0,4},{4,0},{8,12},{12,8},{16,20},{20,16},{24,28},{28,24},{1,5},{5... | collective-permute-start | bytes 1585160 | tf_op jit(solution)/shard_map/ppermute | solution.py:231
  4.3 0.7 %copy-start.3 = (f32[32,8,128]{2,1,0:T(8,128)}, f32[32,8,128]{2,1,0:T(8,128)S(1)}, u32[]{:S(2)}) copy-start(f32[32,8,128]{2,1,0:T(8,128)S(1)} %get-tuple-element.43) | copy-start | bytes 393220
  4.9 8.1 %collective-permute-start.1 = (f32[34,8,128]{2,1,0:T(8,128)S(1)}, f32[34,8,128]{2,1,0:T(8,128)S(1)}, u32[]{:S(2)}, u32[]{:S(2)}) collective-permute-start(f32[34,8,128]{2,1,0:T(8,128)S(1)} %get-tuple-element.39), channel_id=1, source_target_pairs={{0,24},{4,28},{8,16},{12,20},{16,8},{20,12},{24,0},{28,4},{1,25},{... | collective-permute-start | bytes 417800 | tf_op jit(solution)/shard_map/ppermute | solution.py:60
  8.8 7.3 %collective-permute-start.2 = (f32[34,8,128]{2,1,0:T(8,128)S(1)}, f32[34,8,128]{2,1,0:T(8,128)S(1)}, u32[]{:S(2)}, u32[]{:S(2)}) collective-permute-start(f32[34,8,128]{2,1,0:T(8,128)S(1)} %get-tuple-element.40), channel_id=1, source_target_pairs={{0,8},{4,20},{8,0},{12,28},{16,24},{20,4},{24,16},{28,12},{1,9},{5... | collective-permute-start | bytes 417800 | tf_op jit(solution)/shard_map/ppermute | solution.py:60
  9.3 2.1 %copy-start.5 = (s32[8,2]{0,1:T(2,128)S(1)}, s32[8,2]{0,1:T(2,128)}, u32[]{:S(2)}) copy-start(s32[8,2]{0,1:T(2,128)} %param.5) | copy-start | bytes 196
  9.3 6.7 %collective-permute-start.3 = (f32[34,8,128]{2,1,0:T(8,128)S(1)}, f32[34,8,128]{2,1,0:T(8,128)S(1)}, u32[]{:S(2)}, u32[]{:S(2)}) collective-permute-start(f32[34,8,128]{2,1,0:T(8,128)S(1)} %get-tuple-element.41), channel_id=1, source_target_pairs={{0,16},{4,12},{8,24},{12,4},{16,0},{20,28},{24,8},{28,20},{1,17},{... | collective-permute-start | bytes 417800 | tf_op jit(solution)/shard_map/ppermute | solution.py:60
  11.4 11.7 %copy-start.4 = (f32[32,8,128]{2,1,0:T(8,128)S(1)}, f32[32,8,128]{2,1,0:T(8,128)}, u32[]{:S(2)}) copy-start(f32[32,8,128]{2,1,0:T(8,128)} %copy-done.3) | copy-start | bytes 393220
  16.6 4.0 %collective-permute-start.4 = (f32[8,8,128]{2,1,0:T(8,128)S(1)}, f32[8,8,128]{2,1,0:T(8,128)S(1)}, u32[]{:S(2)}, u32[]{:S(2)}) collective-permute-start(f32[8,8,128]{2,1,0:T(8,128)S(1)} %shard_map.70.a_ref), channel_id=1, source_target_pairs={{0,1},{1,0},{2,3},{3,2},{4,5},{5,4},{6,7},{7,6},{8,9},{9,8},{10,11... | collective-permute-start | bytes 98312 | tf_op jit(solution)/shard_map/ppermute | solution.py:260
  20.6 6.1 %collective-permute-start.5 = (f32[8,8,128]{2,1,0:T(8,128)S(1)}, f32[8,8,128]{2,1,0:T(8,128)S(1)}, u32[]{:S(2)}, u32[]{:S(2)}) collective-permute-start(f32[8,8,128]{2,1,0:T(8,128)S(1)} %shard_map.71.refs_2_), channel_id=1, source_target_pairs={{0,2},{1,3},{2,0},{3,1},{4,6},{5,7},{6,4},{7,5},{8,10},{9,11},{10,... | collective-permute-start | bytes 98312 | tf_op jit(solution)/shard_map/ppermute | solution.py:260
  23.2 8.5 %collective-permute-start.6 = (f32[32,8,128]{2,1,0:T(8,128)S(1)}, f32[32,8,128]{2,1,0:T(8,128)S(1)}, u32[]{:S(2)}, u32[]{:S(2)}) collective-permute-start(f32[32,8,128]{2,1,0:T(8,128)S(1)} %copy-done.4), channel_id=1, source_target_pairs={{0,24},{4,28},{8,16},{12,20},{16,8},{20,12},{24,0},{28,4},{1,25},{... | collective-permute-start | bytes 393224 | tf_op jit(solution)/shard_map/ppermute | solution.py:60
  24.8 7.5 %collective-permute-start.7 = (f32[32,8,128]{2,1,0:T(8,128)S(1)}, f32[32,8,128]{2,1,0:T(8,128)S(1)}, u32[]{:S(2)}, u32[]{:S(2)}) collective-permute-start(f32[32,8,128]{2,1,0:T(8,128)S(1)} %get-tuple-element.44), channel_id=1, source_target_pairs={{0,8},{4,20},{8,0},{12,28},{16,24},{20,4},{24,16},{28,12},{1,9},{5... | collective-permute-start | bytes 393224 | tf_op jit(solution)/shard_map/ppermute | solution.py:60
  26.0 7.6 %collective-permute-start.8 = (f32[32,8,128]{2,1,0:T(8,128)S(1)}, f32[32,8,128]{2,1,0:T(8,128)S(1)}, u32[]{:S(2)}, u32[]{:S(2)}) collective-permute-start(f32[32,8,128]{2,1,0:T(8,128)S(1)} %get-tuple-element.45), channel_id=1, source_target_pairs={{0,16},{4,12},{8,24},{12,4},{16,0},{20,28},{24,8},{28,20},{1,17},{... | collective-permute-start | bytes 393224 | tf_op jit(solution)/shard_map/ppermute | solution.py:60
  27.5 10.9 %copy-start.1 = (f32[32,1,16,1024]{3,2,1,0:T(8,128)S(1)}, f32[32,1,16,1024]{3,2,1,0:T(8,128)}, u32[]{:S(2)}) copy-start(f32[32,1,16,1024]{3,2,1,0:T(8,128)} %param.7) | copy-start | bytes 6291460
  28.7 8.7 %collective-permute-start.13 = (f32[2,16,1024]{2,1,0:T(8,128)S(1)}, f32[2,16,1024]{2,1,0:T(8,128)S(1)}, u32[]{:S(2)}, u32[]{:S(2)}) collective-permute-start(f32[2,16,1024]{2,1,0:T(8,128)S(1)} %get-tuple-element.58), channel_id=1, source_target_pairs={{0,24},{4,28},{8,16},{12,20},{16,8},{20,12},{24,0},{28,4},{1,25},{... | collective-permute-start | bytes 393224 | tf_op jit(solution)/shard_map/ppermute | solution.py:60
  30.4 11.9 %collective-permute-start.14 = (f32[2,16,1024]{2,1,0:T(8,128)S(1)}, f32[2,16,1024]{2,1,0:T(8,128)S(1)}, u32[]{:S(2)}, u32[]{:S(2)}) collective-permute-start(f32[2,16,1024]{2,1,0:T(8,128)S(1)} %get-tuple-element.59), channel_id=1, source_target_pairs={{0,8},{4,20},{8,0},{12,28},{16,24},{20,4},{24,16},{28,12},{1,9},{5... | collective-permute-start | bytes 393224 | tf_op jit(solution)/shard_map/ppermute | solution.py:60
  31.7 10.7 %collective-permute-start.15 = (f32[2,16,1024]{2,1,0:T(8,128)S(1)}, f32[2,16,1024]{2,1,0:T(8,128)S(1)}, u32[]{:S(2)}, u32[]{:S(2)}) collective-permute-start(f32[2,16,1024]{2,1,0:T(8,128)S(1)} %get-tuple-element.60), channel_id=1, source_target_pairs={{0,16},{4,12},{8,24},{12,4},{16,0},{20,28},{24,8},{28,20},{1,17},{... | collective-permute-start | bytes 393224 | tf_op jit(solution)/shard_map/ppermute | solution.py:60
  34.9 9.6 %collective-permute-start.9 = (f32[2,16,1024]{2,1,0:T(8,128)S(1)}, f32[2,16,1024]{2,1,0:T(8,128)S(1)}, u32[]{:S(2)}, u32[]{:S(2)}) collective-permute-start(f32[2,16,1024]{2,1,0:T(8,128)S(1)} %get-tuple-element.47), channel_id=1, source_target_pairs={{0,24},{4,28},{8,16},{12,20},{16,8},{20,12},{24,0},{28,4},{1,25},{... | collective-permute-start | bytes 393224 | tf_op jit(solution)/shard_map/ppermute | solution.py:60
  36.4 8.0 %collective-permute-start.10 = (f32[2,16,1024]{2,1,0:T(8,128)S(1)}, f32[2,16,1024]{2,1,0:T(8,128)S(1)}, u32[]{:S(2)}, u32[]{:S(2)}) collective-permute-start(f32[2,16,1024]{2,1,0:T(8,128)S(1)} %get-tuple-element.48), channel_id=1, source_target_pairs={{0,8},{4,20},{8,0},{12,28},{16,24},{20,4},{24,16},{28,12},{1,9},{5... | collective-permute-start | bytes 393224 | tf_op jit(solution)/shard_map/ppermute | solution.py:60
  37.5 7.0 %collective-permute-start.11 = (f32[2,16,1024]{2,1,0:T(8,128)S(1)}, f32[2,16,1024]{2,1,0:T(8,128)S(1)}, u32[]{:S(2)}, u32[]{:S(2)}) collective-permute-start(f32[2,16,1024]{2,1,0:T(8,128)S(1)} %get-tuple-element.49), channel_id=1, source_target_pairs={{0,16},{4,12},{8,24},{12,4},{16,0},{20,28},{24,8},{28,20},{1,17},{... | collective-permute-start | bytes 393224 | tf_op jit(solution)/shard_map/ppermute | solution.py:60
  44.4 2.0 %collective-permute-start.16 = (f32[4,16,1024]{2,1,0:T(8,128)S(1)}, f32[4,16,1024]{2,1,0:T(8,128)S(1)}, u32[]{:S(2)}, u32[]{:S(2)}) collective-permute-start(f32[4,16,1024]{2,1,0:T(8,128)S(1)} %shard_map.78), channel_id=1, source_target_pairs={{0,4},{4,0},{8,12},{12,8},{16,20},{20,16},{24,28},{28,24},{1,5},{5... | collective-permute-start | bytes 786440 | tf_op jit(solution)/shard_map/ppermute | solution.py:306
  45.8 1.7 %collective-permute-start.12 = (f32[4,16,1024]{2,1,0:T(8,128)S(1)}, f32[4,16,1024]{2,1,0:T(8,128)S(1)}, u32[]{:S(2)}, u32[]{:S(2)}) collective-permute-start(f32[4,16,1024]{2,1,0:T(8,128)S(1)} %shard_map.77), channel_id=1, source_target_pairs={{0,4},{4,0},{8,12},{12,8},{16,20},{20,16},{24,28},{28,24},{1,5},{5... | collective-permute-start | bytes 786440 | tf_op jit(solution)/shard_map/ppermute | solution.py:306
